TPU v7x, 32 devices: a whole 2x2x4 slice. The times are simulated.
32 devices in a mesh: dp: 8 (over z, y), mp: 4 (over x, core).
Axes of the slice: x: 2, y: 2, z: 4, core: 2. Of those that a mesh axis runs over, the one named last changes fastest.
Arguments:
- tokens: bfloat16 [4096, 2560], P(('dp', 'mp')), may hold values from -6 to 6
- upstream: bfloat16 [4096, 2560], P(('dp', 'mp')), may hold values from -6 to 6
- offsets: int32 [4096], P('dp'), may hold values from 0 to 799, as said below
- query_weight: float32 [2560, 2560], P('dp', 'mp'), may hold values from -0.125 to 0.125
- keyval_weight: float32 [2, 2560, 640], P(None, 'dp', 'mp'), may hold values from -0.125 to 0.125
- output_weight: float32 [2560, 2560], P('dp', 'mp'), may hold values from -0.625 to 0.625
- gateup_weight: float32 [2, 2560, 7168], P(None, 'dp', 'mp'), may hold values from -0.125 to 0.125
- down_weight: float32 [2560, 7168], P('dp', 'mp'), may hold values from -0.0625 to 0.0625
- norm_gains: float32 [2, 2560], P(None, 'dp')
- first_query: float32 [2560, 2560], P('dp', 'mp'), may hold values from -0.6 to 0.6
- first_keyval: float32 [2, 2560, 640], P(None, 'dp', 'mp'), may hold values from -0.6 to 0.6
- first_output: float32 [2560, 2560], P('dp', 'mp'), may hold values from -0.6 to 0.6
- first_gateup: float32 [2, 2560, 7168], P(None, 'dp', 'mp'), may hold values from -0.6 to 0.6
- first_down: float32 [2560, 7168], P('dp', 'mp'), may hold values from -0.6 to 0.6
- first_gains: float32 [2, 2560], P(None, 'dp'), may hold values from -0.6 to 0.6
- second_query: float32 [2560, 2560], P('dp', 'mp'), may hold values from 0.02 to 0.2
- second_keyval: float32 [2, 2560, 640], P(None, 'dp', 'mp'), may hold values from 0.02 to 0.2
- second_output: float32 [2560, 2560], P('dp', 'mp'), may hold values from 0.02 to 0.2
- second_gateup: float32 [2, 2560, 7168], P(None, 'dp', 'mp'), may hold values from 0.02 to 0.2
- second_down: float32 [2560, 7168], P('dp', 'mp'), may hold values from 0.02 to 0.2
- second_gains: float32 [2, 2560], P(None, 'dp'), may hold values from 0.02 to 0.2
Outputs:
- block_out: bfloat16 [4096, 2560], P(('dp', 'mp'))
- grad_tokens: float32 [4096, 2560], P(('dp', 'mp'))
- grad_norm: float32 [], replicated
- grad_query: float32 [2560, 2560], P('dp', 'mp')
- grad_keyval: float32 [2, 2560, 640], P(None, 'dp', 'mp')
- grad_output: float32 [2560, 2560], P('dp', 'mp')
- grad_gateup: float32 [2, 2560, 7168], P(None, 'dp', 'mp')
- grad_down: float32 [2560, 7168], P('dp', 'mp')
- grad_gains: float32 [2, 2560], P(None, 'dp')
- next_first_query: float32 [2560, 2560], P('dp', 'mp')
- next_first_keyval: float32 [2, 2560, 640], P(None, 'dp', 'mp')
- next_first_output: float32 [2560, 2560], P('dp', 'mp')
- next_first_gateup: float32 [2, 2560, 7168], P(None, 'dp', 'mp')
- next_first_down: float32 [2560, 7168], P('dp', 'mp')
- next_first_gains: float32 [2, 2560], P(None, 'dp')
- next_second_query: float32 [2560, 2560], P('dp', 'mp')
- next_second_keyval: float32 [2, 2560, 640], P(None, 'dp', 'mp')
- next_second_output: float32 [2560, 2560], P('dp', 'mp')
- next_second_gateup: float32 [2, 2560, 7168], P(None, 'dp', 'mp')
- next_second_down: float32 [2560, 7168], P('dp', 'mp')
- next_second_gains: float32 [2, 2560], P(None, 'dp')
- step_query: float32 [2560, 2560], P('dp', 'mp')
- step_keyval: float32 [2, 2560, 640], P(None, 'dp', 'mp')
- step_output: float32 [2560, 2560], P('dp', 'mp')
- step_gateup: float32 [2, 2560, 7168], P(None, 'dp', 'mp')
- step_down: float32 [2560, 7168], P('dp', 'mp')
- step_gains: float32 [2, 2560], P(None, 'dp')
Inputs may be any that keep to these rules, and one draw needn't show every extreme that they name: `offsets`: the distance of each token from the first token of its document; documents are runs of consecutive tokens of the stream, so each offset is 0 or one more than the previous token's, and the first token's is 0; a document has 1 to 800 tokens, and some document has exactly 800.
All inputs are finite; a program needn't handle non-finite values.
Results may differ from a plain program's by a relative error of at most 0.025.
Values may be sent and summed in bfloat16 or wider, within the bound.
No kernel may reach another device: no remote copies, remote signals or barrier semaphores. Data moves between devices by JAX's collectives and lax.ppermute only.
A program may use at most 512 MiB of HBM per device.

v0:
```python
import math

import jax
import jax.numpy as jnp
from jax import lax
from jax.sharding import PartitionSpec as P

MODEL_WIDTH = 2560
QUERY_HEAD_COUNT = 32
KEY_VALUE_HEADS = 8
HEAD_SIZE = 80
HIDDEN_UNITS = 7168
DOC_MAX = 800
STEP = 10


eps_norm = 1e-05
rope_base = 1000000.0
beta_first = 0.9
beta_second = 0.95
learn_rate = 0.02
weight_decay = 0.1
adam_eps = 1e-08
masked_score = -1e30


def shifted(block, axis, distance):
    devices = range(lax.axis_size(axis))
    route = [(i - distance, i) for i in devices if i - distance in devices]
    return lax.ppermute(block, axis, route)


def rope_tables(positions):
    half = HEAD_SIZE // 2
    freqs = rope_base ** (-(jnp.arange(half).astype(jnp.float32) * 2.0 / HEAD_SIZE))
    angle = positions.astype(jnp.float32)[:, None] * freqs[None, :]
    return (jnp.cos(angle), jnp.sin(angle))


def apply_rotation(value_rows, cosine_table, sine_table):
    half = value_rows.shape[-1] // 2
    first_half = value_rows[..., :half]
    second_half = value_rows[..., half:]
    cos_wide = cosine_table[:, None, :]
    sin_wide = sine_table[:, None, :]
    return jnp.concatenate(
        [
            first_half * cos_wide - second_half * sin_wide,
            second_half * cos_wide + first_half * sin_wide,
        ],
        axis=-1,
    )


def unrotate(grads, cosine_table, sine_table):
    half = grads.shape[-1] // 2
    first_half = grads[..., :half]
    second_half = grads[..., half:]
    cos_wide = cosine_table[:, None, :]
    sin_wide = sine_table[:, None, :]
    return jnp.concatenate(
        [
            first_half * cos_wide + second_half * sin_wide,
            second_half * cos_wide - first_half * sin_wide,
        ],
        axis=-1,
    )


def norm_back(incoming, unit_rows, inverse_root, gain):
    scaled = incoming * gain
    return inverse_root * (
        scaled - unit_rows * jnp.mean(scaled * unit_rows, axis=-1, keepdims=True)
    )


def contract_last(left_side, weight):
    return lax.dot_general(
        left_side, weight, (((1,), (1,)), ((), ())), preferred_element_type=jnp.float32
    )


def spread_rows(rows_local):
    return lax.all_gather(rows_local, "mp", axis=0, tiled=True)


def gather_grads(rows_local):
    return lax.all_gather(rows_local, "mp", axis=0, tiled=True)


def pass_keys(stacked):
    return shifted(stacked, "dp", 1)


def return_grads(partial_terms):
    return shifted(partial_terms.astype(jnp.bfloat16), "dp", -1).astype(partial_terms.dtype)


def branch_sum(activation, weight):
    return lax.psum_scatter(
        contract_last(activation, weight).astype(jnp.bfloat16),
        "mp",
        scatter_dimension=0,
        tiled=True,
    ).astype(jnp.float32)


def input_sum(pairs):
    summed = contract_last(pairs[0][0], pairs[0][1])
    for grad_rows, weight in pairs[1:]:
        addend = contract_last(grad_rows, weight)
        summed = summed + addend
    return lax.psum_scatter(
        summed.astype(jnp.bfloat16), "mp", scatter_dimension=0, tiled=True
    ).astype(jnp.float32)


def weight_terms(pairs):
    pieces = [
        lax.dot_general(
            left_side, right_side, (((0,), (0,)), ((), ())), preferred_element_type=jnp.float32
        )
        for left_side, right_side in pairs
    ]
    return jnp.concatenate(pieces, axis=1)


def adamw(param, grad, first, second):
    first_new = beta_first * first + (1.0 - beta_first) * grad
    second_new = beta_second * second + (1.0 - beta_second) * grad * grad
    first_hat = first_new / (1.0 - beta_first**STEP)
    second_hat = second_new / (1.0 - beta_second**STEP)
    change = -learn_rate * (first_hat / (jnp.sqrt(second_hat) + adam_eps) + weight_decay * param)
    return (first_new, second_new, change)


def on_device(
    tokens,
    upstream,
    offsets,
    query_weight,
    keyval_weight,
    output_weight,
    gateup_weight,
    down_weight,
    norm_gains,
    first_query,
    first_keyval,
    first_output,
    first_gateup,
    first_down,
    first_gains,
    second_query,
    second_keyval,
    second_output,
    second_gateup,
    second_down,
    second_gains,
):
    low_type = jnp.bfloat16
    wide_type = jnp.float32
    query_full, keyval_full, output_full, gateup_full, down_full, gains_full = (
        lax.all_gather(query_weight.astype(low_type), "dp", axis=0, tiled=True),
        lax.all_gather(keyval_weight.astype(low_type), "dp", axis=1, tiled=True),
        lax.all_gather(output_weight.astype(low_type), "dp", axis=0, tiled=True),
        lax.all_gather(gateup_weight.astype(low_type), "dp", axis=1, tiled=True),
        lax.all_gather(down_weight.astype(low_type), "dp", axis=0, tiled=True),
        lax.all_gather(norm_gains.astype(low_type), "dp", axis=1, tiled=True),
    )
    gain_values = gains_full.astype(wide_type)
    rows_owned = query_weight.shape[0]
    inputs = tokens.astype(wide_type)
    inverse_one = lax.rsqrt(jnp.mean(inputs * inputs, axis=-1, keepdims=True) + eps_norm)
    unit_one = inputs * inverse_one
    normed_one = spread_rows((unit_one * gain_values[0]).astype(low_type))
    row_total = normed_one.shape[0]
    query_heads = query_full.shape[1] // HEAD_SIZE
    kv_heads = keyval_full.shape[2] // HEAD_SIZE
    head_group = query_heads // kv_heads
    kv_width = kv_heads * HEAD_SIZE
    query_width = query_heads * HEAD_SIZE
    scale = HEAD_SIZE ** (-0.5)
    cosine_table, sine_table = rope_tables(offsets)
    query_rows = apply_rotation(
        jnp.dot(normed_one, query_full, preferred_element_type=wide_type).reshape(
            row_total, query_heads, HEAD_SIZE
        ),
        cosine_table,
        sine_table,
    ).astype(low_type)
    key_rows = apply_rotation(
        jnp.dot(normed_one, keyval_full[0], preferred_element_type=wide_type).reshape(
            row_total, kv_heads, HEAD_SIZE
        ),
        cosine_table,
        sine_table,
    ).astype(low_type)
    value_rows = jnp.dot(normed_one, keyval_full[1], preferred_element_type=wide_type).astype(
        low_type
    )
    flat_keys = key_rows.reshape(row_total, kv_width)
    here = lax.axis_index("dp")
    count = lax.axis_size("dp")
    reach = min((DOC_MAX + row_total - 2) // row_total, count - 1)
    held = [jnp.stack([flat_keys, value_rows])]
    for step in range(reach):
        held.append(pass_keys(held[-1]))
    owners = [(here - step) * row_total for step in range(reach + 1)]
    window = jnp.concatenate(held, axis=1)
    key_total = window.shape[1]
    window_pos = jnp.concatenate(
        [start + jnp.arange(row_total, dtype=jnp.int32) for start in owners]
    )
    items = (
        window[0].reshape(1, key_total, kv_heads, HEAD_SIZE),
        window[1].reshape(1, key_total, kv_heads, HEAD_SIZE),
        window_pos.reshape(1, key_total),
    )
    grouped_heads = query_rows.reshape(row_total, kv_heads, head_group, HEAD_SIZE)
    query_pos = here * row_total + jnp.arange(row_total, dtype=jnp.int32)
    doc_first = query_pos - offsets

    def masked_scores(block_keys, key_pos):
        raw = (
            jnp.einsum(
                "tgrd,ngd->tgrn", grouped_heads, block_keys, preferred_element_type=wide_type
            )
            * scale
        )
        allowed = (key_pos[None, :] <= query_pos[:, None]) & (
            key_pos[None, :] >= doc_first[:, None]
        )
        allowed = allowed[:, None, None, :]
        return (jnp.where(allowed, raw, masked_score), allowed)

    def forward_step(state_now, item):
        running_max, running_sum, running_out = state_now
        block_keys, block_values, key_pos = item
        scores, allowed = masked_scores(block_keys, key_pos)
        new_max = jnp.maximum(running_max, jnp.max(scores, axis=-1))
        rescale = jnp.exp(running_max - new_max)
        probs = jnp.where(allowed, jnp.exp(scores - new_max[..., None]), 0.0)
        running_sum = running_sum * rescale + jnp.sum(probs, axis=-1)
        running_out = running_out * rescale[..., None] + jnp.einsum(
            "tgrn,ngd->tgrd", probs.astype(low_type), block_values, preferred_element_type=wide_type
        )
        return ((new_max, running_sum, running_out), None)

    start_state = (
        jnp.full((row_total, kv_heads, head_group), masked_score, wide_type),
        jnp.zeros((row_total, kv_heads, head_group), wide_type),
        jnp.zeros((row_total, kv_heads, head_group, HEAD_SIZE), wide_type),
    )
    (running_max, running_sum, running_out), unused = lax.scan(forward_step, start_state, items)
    attended = running_out / running_sum[..., None]
    log_total = running_max + jnp.log(running_sum)
    attended_low = attended.reshape(row_total, query_width).astype(low_type)
    middle = inputs + branch_sum(attended_low, output_full)
    inverse_two = lax.rsqrt(jnp.mean(middle * middle, axis=-1, keepdims=True) + eps_norm)
    unit_two = middle * inverse_two
    normed_two = spread_rows((unit_two * gain_values[1]).astype(low_type))
    gate = jnp.dot(normed_two, gateup_full[0], preferred_element_type=wide_type)
    upward = jnp.dot(normed_two, gateup_full[1], preferred_element_type=wide_type)
    sigma = jax.nn.sigmoid(gate)
    hidden = (gate * sigma * upward).astype(low_type)
    block_out = (middle + branch_sum(hidden, down_full)).astype(low_type)
    out_rows = gather_grads(upstream)
    grad_hidden = jnp.dot(out_rows, down_full, preferred_element_type=wide_type)
    grad_gate = (grad_hidden * upward * sigma * (1.0 + gate * (1.0 - sigma))).astype(low_type)
    grad_up = (grad_hidden * gate * sigma).astype(low_type)
    ffn_pairs = ((normed_two, grad_gate), (normed_two, grad_up), (out_rows, hidden))
    grad_normed_two = input_sum(((grad_gate, gateup_full[0]), (grad_up, gateup_full[1])))
    gain_two = jnp.sum(grad_normed_two * unit_two, axis=0)
    grad_middle = upstream.astype(wide_type) + norm_back(
        grad_normed_two, unit_two, inverse_two, gain_values[1]
    )
    branch_grad = gather_grads(grad_middle.astype(low_type))
    grad_attended = jnp.dot(branch_grad, output_full, preferred_element_type=wide_type).astype(
        low_type
    )
    grad_out4 = grad_attended.reshape(row_total, kv_heads, head_group, HEAD_SIZE)
    delta = jnp.sum(grad_out4.astype(wide_type) * attended, axis=-1)

    def backward_step(grad_query_acc, item):
        block_keys, block_values, key_pos = item
        scores, allowed = masked_scores(block_keys, key_pos)
        probs = jnp.where(allowed, jnp.exp(scores - log_total[..., None]), 0.0)
        grad_probs = jnp.einsum(
            "tgrd,ngd->tgrn", grad_out4, block_values, preferred_element_type=wide_type
        )
        grad_scores = (probs * (grad_probs - delta[..., None])).astype(low_type)
        grad_query_acc = grad_query_acc + jnp.einsum(
            "tgrn,ngd->tgrd", grad_scores, block_keys, preferred_element_type=wide_type
        )
        grad_keys = (
            jnp.einsum(
                "tgrn,tgrd->ngd", grad_scores, grouped_heads, preferred_element_type=wide_type
            )
            * scale
        )
        grad_values = jnp.einsum(
            "tgrn,tgrd->ngd", probs.astype(low_type), grad_out4, preferred_element_type=wide_type
        )
        stacked = jnp.concatenate(
            [grad_keys.reshape(key_total, kv_width), grad_values.reshape(key_total, kv_width)],
            axis=1,
        )
        return (grad_query_acc, stacked)

    grad_rotated, key_terms = lax.scan(
        backward_step, jnp.zeros((row_total, kv_heads, head_group, HEAD_SIZE), wide_type), items
    )
    pieces = key_terms.reshape(reach + 1, row_total, 2 * kv_width)
    travel = pieces[reach]
    for step in range(reach, 0, -1):
        travel = return_grads(travel) + pieces[step - 1]
    grad_query_low = (
        unrotate(
            (grad_rotated * scale).reshape(row_total, query_heads, HEAD_SIZE),
            cosine_table,
            sine_table,
        )
        .reshape(row_total, query_width)
        .astype(low_type)
    )
    grad_key_low = (
        unrotate(
            travel[:, :kv_width].reshape(row_total, kv_heads, HEAD_SIZE), cosine_table, sine_table
        )
        .reshape(row_total, kv_width)
        .astype(low_type)
    )
    grad_value_low = travel[:, kv_width:].astype(low_type)
    attn_pairs = (
        (normed_one, grad_query_low),
        (normed_one, grad_key_low),
        (normed_one, grad_value_low),
        (branch_grad, attended_low),
    )
    grad_normed_one = input_sum(
        (
            (grad_query_low, query_full),
            (grad_key_low, keyval_full[0]),
            (grad_value_low, keyval_full[1]),
        )
    )
    gain_one = jnp.sum(grad_normed_one * unit_one, axis=0)
    grad_tokens = grad_middle + norm_back(grad_normed_one, unit_one, inverse_one, gain_values[0])
    gain_part = jnp.stack([gain_one, gain_two])
    gain_total = lax.psum(gain_part, ("dp", "mp"))
    all_shares = lax.psum_scatter(
        weight_terms(attn_pairs + ffn_pairs).astype(jnp.bfloat16),
        "dp",
        scatter_dimension=0,
        tiled=True,
    ).astype(jnp.float32)
    ffn_local = gateup_full.shape[2]
    edge_two = query_width + kv_width
    edge_three = edge_two + kv_width
    edge_four = edge_three + query_width
    edge_five = edge_four + ffn_local
    edge_six = edge_five + ffn_local
    grad_query = all_shares[:, :query_width]
    grad_keyval = jnp.stack(
        [all_shares[:, query_width:edge_two], all_shares[:, edge_two:edge_three]]
    )
    grad_output = all_shares[:, edge_three:edge_four]
    grad_gateup = jnp.stack([all_shares[:, edge_four:edge_five], all_shares[:, edge_five:edge_six]])
    grad_down = all_shares[:, edge_six:]
    owned_square = jnp.sum(all_shares * all_shares)
    weight_square = lax.psum(owned_square, ("dp", "mp"))
    grad_norm = jnp.sqrt(weight_square + jnp.sum(gain_total * gain_total))
    grad_gains = lax.dynamic_slice_in_dim(gain_total, here * rows_owned, rows_owned, 1)
    clipping_bound = math.sqrt(
        MODEL_WIDTH
        * (2 * QUERY_HEAD_COUNT * HEAD_SIZE + 2 * KEY_VALUE_HEADS * HEAD_SIZE + 3 * HIDDEN_UNITS)
        + 2 * MODEL_WIDTH
    )
    clip = jnp.minimum(1.0, clipping_bound / (grad_norm + 1e-06))
    params = (query_weight, keyval_weight, output_weight, gateup_weight, down_weight, norm_gains)
    firsts = (first_query, first_keyval, first_output, first_gateup, first_down, first_gains)
    seconds = (second_query, second_keyval, second_output, second_gateup, second_down, second_gains)
    grads = (grad_query, grad_keyval, grad_output, grad_gateup, grad_down, grad_gains)
    states = [
        adamw(params[index], grads[index] * clip, firsts[index], seconds[index])
        for index in range(6)
    ]
    return (
        block_out,
        grad_tokens,
        grad_norm,
        grads[0],
        grads[1],
        grads[2],
        grads[3],
        grads[4],
        grads[5],
        states[0][0],
        states[1][0],
        states[2][0],
        states[3][0],
        states[4][0],
        states[5][0],
        states[0][1],
        states[1][1],
        states[2][1],
        states[3][1],
        states[4][1],
        states[5][1],
        states[0][2],
        states[1][2],
        states[2][2],
        states[3][2],
        states[4][2],
        states[5][2],
    )


def solution(mesh):
    placed = (
        P(("dp", "mp"), None),
        P(("dp", "mp"), None),
        P("dp"),
        P("dp", "mp"),
        P(None, "dp", "mp"),
        P("dp", "mp"),
        P(None, "dp", "mp"),
        P("dp", "mp"),
        P(None, "dp"),
        P("dp", "mp"),
        P(None, "dp", "mp"),
        P("dp", "mp"),
        P(None, "dp", "mp"),
        P("dp", "mp"),
        P(None, "dp"),
        P("dp", "mp"),
        P(None, "dp", "mp"),
        P("dp", "mp"),
        P(None, "dp", "mp"),
        P("dp", "mp"),
        P(None, "dp"),
    )
    return jax.shard_map(
        on_device,
        mesh=mesh,
        in_specs=placed,
        out_specs=(
            P(("dp", "mp"), None),
            P(("dp", "mp"), None),
            P(),
            P("dp", "mp"),
            P(None, "dp", "mp"),
            P("dp", "mp"),
            P(None, "dp", "mp"),
            P("dp", "mp"),
            P(None, "dp"),
            P("dp", "mp"),
            P(None, "dp", "mp"),
            P("dp", "mp"),
            P(None, "dp", "mp"),
            P("dp", "mp"),
            P(None, "dp"),
            P("dp", "mp"),
            P(None, "dp", "mp"),
            P("dp", "mp"),
            P(None, "dp", "mp"),
            P("dp", "mp"),
            P(None, "dp"),
            P("dp", "mp"),
            P(None, "dp", "mp"),
            P("dp", "mp"),
            P(None, "dp", "mp"),
            P("dp", "mp"),
            P(None, "dp"),
        ),
        check_vma=False,
    )
```

profile of v0, /device:TPU:0, one launch (start us, length us, event | category | flops | bytes accessed | tf_op | source)
XLA Modules:
  0.0 1752.1 jit_solution(11172559242877106371)
XLA Ops:
  10.1 27.8 %all-gather = bf16[8,320,2]{1,2,0:T(2,128)(2,1)S(1)} all-gather(bf16[1,320,2]{1,2,0:T(2,128)(2,1)S(1)} %convert_bitcast_fusion), channel_id=1, replica_groups=mesh['dp'=8,'mp'=4] {'dp'}, dimensions={0}, use_global_device_ids=true | all-gather | bytes 11520 | tf_op jit(solution)/shard_map/all_gather | solution.py:168
  42.8 25.5 %all-gather.13.cloned.1.call-done = bf16[2,2560,160]{2,0,1:T(2,128)(2,1)} async-done(((bf16[2,320,160]{2,0,1:T(2,128)(2,1)}), bf16[2,2560,160]{2,0,1:T(2,128)(2,1)}) %all-gather.13.cloned.1.call-update) | async-done | bytes 1638416 | tf_op jit(solution)/shard_map/all_gather | solution.py:164
  102.2 11.4 collective-permute-done
  124.4 41.2 %all-gather.15.cloned.1.call-done = bf16[2560,640]{1,0:T(8,128)(2,1)} async-done(((bf16[320,640]{1,0:T(8,128)(2,1)}), bf16[2560,640]{1,0:T(8,128)(2,1)}) %all-gather.15.cloned.1.call-update) | async-done | bytes 3276816 | tf_op jit(solution)/shard_map/all_gather | solution.py:163
  169.8 10.9 fusion.85
  180.7 10.8 fusion.2
  191.6 12.1 fusion.86
  203.7 25.5 %all-gather.17.cloned.1.call-done = bf16[2560,640]{1,0:T(8,128)(2,1)} async-done(((bf16[320,640]{1,0:T(8,128)(2,1)}), bf16[2560,640]{1,0:T(8,128)(2,1)}) %all-gather.17.cloned.1.call-update) | async-done | bytes 3276816 | tf_op jit(solution)/shard_map/all_gather | solution.py:165
  234.9 33.2 %reduce-scatter.8.cloned.1.call-done = bf16[128,2560]{1,0:T(8,128)(2,1)} async-done(((bf16[512,2560]{1,0:T(8,128)(2,1)}), bf16[128,2560]{1,0:T(8,128)(2,1)}) %reduce-scatter.8.cloned.1.call-update) | async-done | bytes 655376 | tf_op jit(solution)/shard_map/reduce_scatter | solution.py:100
  278.6 18.7 %all-gather.19.cloned.1.call-done = bf16[512,2560]{1,0:T(8,128)(2,1)} async-done(((bf16[128,2560]{1,0:T(8,128)(2,1)}), bf16[512,2560]{1,0:T(8,128)(2,1)}) %all-gather.19.cloned.1.call-update) | async-done | bytes 2621456 | tf_op jit(solution)/shard_map/all_gather | solution.py:84
  297.3 354.9 %all-gather.21.cloned.1.call-done = bf16[2,2560,1792]{2,1,0:T(8,128)(2,1)} async-done(((bf16[2,320,1792]{2,1,0:T(8,128)(2,1)}), bf16[2,2560,1792]{2,1,0:T(8,128)(2,1)}) %all-gather.21.cloned.1.call-update) | async-done | bytes 18350096 | tf_op jit(solution)/shard_map/all_gather | solution.py:166
  652.2 11.3 fusion.16
  679.4 137.9 %all-gather.23.cloned.1.call-done = bf16[2560,1792]{1,0:T(8,128)(2,1)} async-done(((bf16[320,1792]{1,0:T(8,128)(2,1)}), bf16[2560,1792]{1,0:T(8,128)(2,1)}) %all-gather.23.cloned.1.call-update) | async-done | bytes 9175056 | tf_op jit(solution)/shard_map/all_gather | solution.py:167
  817.3 13.6 multiply_convert_fusion
  849.6 32.9 %reduce-scatter.12.cloned.1.call-done = bf16[128,2560]{1,0:T(8,128)(2,1)} async-done(((bf16[512,2560]{1,0:T(8,128)(2,1)}), bf16[128,2560]{1,0:T(8,128)(2,1)}) %reduce-scatter.12.cloned.1.call-update) | async-done | bytes 655376 | tf_op jit(solution)/shard_map/reduce_scatter | solution.py:113
  886.8 25.7 %all-gather.27.cloned.1.call-done = bf16[512,2560]{1,0:T(8,128)(2,1)} async-done(((bf16[128,2560]{1,0:T(8,128)(2,1)}), bf16[512,2560]{1,0:T(8,128)(2,1)}) %all-gather.27.cloned.1.call-update) | async-done | bytes 2621456 | tf_op jit(solution)/shard_map/all_gather | solution.py:88
  919.2 11.8 fusion.7
  931.0 16.6 fusion.1
  964.0 10.1 collective-permute-done.2
  991.2 10.0 convolution_convert_fusion.5
  1036.9 44.4 %copy.224 = bf16[2560,6976]{1,0:T(8,128)(2,1)} copy(bf16[2560,6976]{0,1:T(8,128)(2,1)} %fusion.14) | data formatting | bytes 71434240
  1093.2 564.3 %reduce-scatter.16.cloned.1.call-done = bf16[320,6976]{1,0:T(8,128)(2,1)} async-done(((bf16[2560,6976]{1,0:T(8,128)(2,1)}), bf16[320,6976]{1,0:T(8,128)(2,1)}) %reduce-scatter.16.cloned.1.call-update) | async-done | bytes 4464656 | tf_op jit(solution)/shard_map/reduce_scatter | solution.py:351
  1666.8 40.1 %all-reduce = (f32[]{:T(128)}, f32[2,2560]{1,0:T(2,128)S(1)}) all-reduce(f32[]{:T(128)} %multiply_reduce_fusion, f32[2,2560]{1,0:T(2,128)S(1)} %pad_maximum_fusion.10), channel_id=1, replica_groups=mesh['dp'=8,'mp'=4] {'dp','mp'}, use_global_device_ids=true, to_apply=%region_13.14 | all-reduce | flops 5121 | bytes 40968 | tf_op jit(solution)/shard_map/psum | solution.py:371
  1720.1 14.1 add_multiply_fusion
  (256 shorter events, 229.8 us)
Async XLA Ops:
  7.2 32.2 %copy-start.1 = (bf16[128,2560]{1,0:T(8,128)(2,1)S(1)}, bf16[128,2560]{1,0:T(8,128)(2,1)}, u32[]{:S(2)}) copy-start(bf16[128,2560]{1,0:T(8,128)(2,1)} %param.21) | copy-start | bytes 1966084
  7.2 33.4 %copy-start.16 = (f32[320,640]{1,0:T(8,128)S(1)}, f32[320,640]{1,0:T(8,128)}, u32[]{:S(2)}) copy-start(f32[320,640]{1,0:T(8,128)} %param.24) | copy-start | bytes 2457604
  7.2 61.1 %all-gather.13.cloned.1.call-start = ((), (), s32[]{:S(2)}) async-start(), calls=%async_computation.6 | async-start | bytes 2949120 | tf_op jit(solution)/shard_map/all_gather | solution.py:164
  8.4 33.0 %copy-start.18 = (f32[320,640]{1,0:T(8,128)S(1)}, f32[320,640]{1,0:T(8,128)}, u32[]{:S(2)}) copy-start(f32[320,640]{1,0:T(8,128)} %param.26) | copy-start | bytes 2457604
  9.4 85.2 %all-gather.11.cloned.1.call-start = ((), (), s32[]{:S(2)}) async-start(), calls=%async_computation.5 | async-start | bytes 3276800 | tf_op jit(solution)/shard_map/all_gather | solution.py:84
  40.5 125.1 %all-gather.15.cloned.1.call-start = ((), (), s32[]{:S(2)}) async-start(), calls=%async_computation.7 | async-start | bytes 3686400 | tf_op jit(solution)/shard_map/all_gather | solution.py:163
  41.4 187.7 %all-gather.17.cloned.1.call-start = ((), (), s32[]{:S(2)}) async-start(), calls=%async_computation.8 | async-start | bytes 3686400 | tf_op jit(solution)/shard_map/all_gather | solution.py:165
  42.3 225.7 %reduce-scatter.8.cloned.1.call-start = ((), (), s32[]{:S(2)}) async-start(), calls=%async_computation.9 | async-start | bytes 3276800 | tf_op jit(solution)/shard_map/reduce_scatter | solution.py:100
  98.8 14.9 collective-permute-start
  113.7 9.7 collective-permute-start.1
  234.8 62.5 %all-gather.19.cloned.1.call-start = ((), (), s32[]{:S(2)}) async-start(), calls=%async_computation.10 | async-start | bytes 3276800 | tf_op jit(solution)/shard_map/all_gather | solution.py:84
  271.6 380.6 %all-gather.21.cloned.1.call-start = ((), (), s32[]{:S(2)}) async-start(), calls=%async_computation.11 | async-start | bytes 20643840 | tf_op jit(solution)/shard_map/all_gather | solution.py:166
  275.6 403.8 %all-gather.25.cloned.1.call-start = ((), (), s32[]{:S(2)}) async-start(), calls=%async_computation.14 | async-start | bytes 3276800 | tf_op jit(solution)/shard_map/all_gather | solution.py:88
  276.4 540.9 %all-gather.23.cloned.1.call-start = ((), (), s32[]{:S(2)}) async-start(), calls=%async_computation.12 | async-start | bytes 10321920 | tf_op jit(solution)/shard_map/all_gather | solution.py:167
  278.4 604.2 %reduce-scatter.12.cloned.1.call-start = ((), (), s32[]{:S(2)}) async-start(), calls=%async_computation.15 | async-start | bytes 3276800 | tf_op jit(solution)/shard_map/reduce_scatter | solution.py:113
  849.6 33.0 %copy-start.3 = (bf16[128,2560]{1,0:T(8,128)(2,1)S(1)}, bf16[128,2560]{1,0:T(8,128)(2,1)}, u32[]{:S(2)}) copy-start(bf16[128,2560]{1,0:T(8,128)(2,1)} %reduce-scatter.8.cloned.1.call-done) | copy-start | bytes 1966084
  849.6 34.7 %copy-start.11 = (bf16[128,2560]{1,0:T(8,128)(2,1)S(1)}, bf16[128,2560]{1,0:T(8,128)(2,1)}, u32[]{:S(2)}) copy-start(bf16[128,2560]{1,0:T(8,128)(2,1)} %param.22) | copy-start | bytes 1966084
  849.6 62.9 %all-gather.27.cloned.1.call-start = ((), (), s32[]{:S(2)}) async-start(), calls=%async_computation.16 | async-start | bytes 3276800 | tf_op jit(solution)/shard_map/all_gather | solution.py:88
  886.7 201.0 %reduce-scatter.14.cloned.1.call-start = ((), (), s32[]{:S(2)}) async-start(), calls=%async_computation.17 | async-start | bytes 3276800 | tf_op jit(solution)/shard_map/reduce_scatter | solution.py:113
  962.4 11.8 collective-permute-start.2
  974.3 11.5 collective-permute-start.3
  989.7 99.7 %reduce-scatter.10.cloned.1.call-start = ((), (), s32[]{:S(2)}) async-start(), calls=%async_computation.13 | async-start | bytes 3276800 | tf_op jit(solution)/shard_map/reduce_scatter | solution.py:100
  1001.2 656.2 %reduce-scatter.16.cloned.1.call-start = ((), (), s32[]{:S(2)}) async-start(), calls=%async_computation.18 | async-start | bytes 40550400 | tf_op jit(solution)/shard_map/reduce_scatter | solution.py:351
  1662.9 45.9 %copy-start.25 = (f32[2,320,160]{2,1,0:T(8,128)S(1)}, f32[2,320,160]{2,1,0:T(8,128)}, u32[]{:S(2)}) copy-start(f32[2,320,160]{2,1,0:T(8,128)} %copy.210) | copy-start | bytes 1228804
  (58 other events, 413.0 us)
Sparse Core Ops, SparseCore 0:
  10.8 57.4 all-gather.12
  70.4 24.1 all-gather.10
  97.3 68.2 all-gather.14
  168.2 60.8 all-gather.16
  234.9 33.0 reduce-scatter.7
  271.8 25.5 all-gather.18
  299.5 352.6 all-gather.20
  653.8 25.5 all-gather.24
  682.4 134.8 all-gather.22
  849.7 32.8 reduce-scatter.11
  886.9 25.5 all-gather.26
  989.9 34.9 reduce-scatter.13
  1028.1 34.6 reduce-scatter.9
  1081.5 575.9 reduce-scatter.15
where the time goes:
time: 1760 us; the launch traced here: 1750 us
  waiting for transfers between devices  1310 us (74%)
  matrix products  182 us (10%)
  local copies, waits for them, and re-layouts  90.2 us (5%)
  other arithmetic  73.4 us (4%)
  blocking collectives  67.8 us (4%)
    reduce_scatter x1, waiting for transfers between devices, on_device(): lax.psum_scatter(weight_terms(attn_pairs + ffn_pairs).astype(jnp.bfloat16...  564 us
    all_gather x1, waiting for transfers between devices, on_device(): lax.all_gather(gateup_weight.astype(low_type), 'dp', axis=1, tiled=True)  355 us
    all_gather x1, waiting for transfers between devices, on_device(): lax.all_gather(down_weight.astype(low_type), 'dp', axis=0, tiled=True)  138 us
    unnamed x138, local copies, waits for them, and re-layouts  76.4 us
    all_gather x1, waiting for transfers between devices, on_device(): lax.all_gather(query_weight.astype(low_type), 'dp', axis=0, tiled=True)  41.2 us
    psum x1, blocking collectives, on_device(): weight_square = lax.psum(owned_square, ('dp', 'mp'))  40.1 us
    dot_general x7, matrix products, contract_last(): lax.dot_general(left_side, weight, (((1,), (1,)), ((), ())), preferred_el...  39.8 us
  transfers between devices with their start and end apart: 18, of which 16 were waited for; matrix products, arithmetic and copies ran while one was open for 11% of the time, Pallas kernels for 0%

commit v1 on v0

v1 whole, which is shorter than its diff:
```python
import functools
import math

import jax
import jax.numpy as jnp
from jax import lax
from jax.experimental import pallas as pl
from jax.experimental.pallas import tpu as pltpu
from jax.sharding import PartitionSpec as P

MODEL_WIDTH = 2560
QUERY_HEAD_COUNT = 32
KEY_VALUE_HEADS = 8
HEAD_SIZE = 80
HIDDEN_UNITS = 7168
STEP = 10

eps_norm = 1e-05
rope_base = 1000000.0
beta_first = 0.9
beta_second = 0.95
learn_rate = 0.02
weight_decay = 0.1
adam_eps = 1e-08
masked_score = -1e30

low_type = jnp.bfloat16
wide_type = jnp.float32

HALF = HEAD_SIZE // 2
GROUP = QUERY_HEAD_COUNT // KEY_VALUE_HEADS
QROWS = GROUP * HEAD_SIZE
BOTH = 2 * HEAD_SIZE
EXP_SCALE = (HEAD_SIZE ** (-0.5)) * math.log2(math.e)
SCALE = HEAD_SIZE ** (-0.5)
AXES = ("dp", "mp")


def hop(block, move):
    dp_size, mp_size = lax.axis_size("dp"), lax.axis_size("mp")
    route = []
    for d in range(dp_size):
        for m in range(mp_size):
            target = move(d, m)
            if target is not None:
                route.append((d * mp_size + m, target[0] * mp_size + target[1]))
    return lax.ppermute(block, AXES, route)


def hop_core(block):
    return hop(block, lambda d, m: (d, m ^ 1))


def hop_x(block):
    return hop(block, lambda d, m: (d, m ^ 2))


def hop_low(block):
    return hop(block, lambda d, m: (d ^ 2, m))


def hop_y(block):
    return hop(block, lambda d, m: (d ^ 1, m))


def hop_ring(block):
    size = lax.axis_size("dp")
    return hop(block, lambda d, m: ((d + 4) % size, m))


def to_next(block, flip):
    size = lax.axis_size("dp")
    return hop(block, lambda d, m: ((d + 4) ^ flip, m) if d + 4 < size else None)


def to_previous(block, flip):
    return hop(block, lambda d, m: ((d - 4) ^ flip, m) if d >= 4 else None)


def bits():
    d = lax.axis_index("dp")
    m = lax.axis_index("mp")
    return d // 4, (d // 2) % 2, d % 2, m // 2, m % 2


def choose(bit, if_zero, if_one):
    return jnp.where(bit == 0, if_zero, if_one)


def ordered(bit, mine, other, axis):
    return choose(
        bit,
        jnp.concatenate([mine, other], axis=axis),
        jnp.concatenate([other, mine], axis=axis),
    )


def gather_rows(own):
    half = own.shape[0] // 2
    across = hop_x(own)
    along = hop_low(own)
    first = hop_x(along[:half])
    second = hop_low(across[half:])
    four = jnp.stack([own, across, along, jnp.concatenate([first, second], axis=0)])
    return jnp.stack([four, hop_core(four)])


def scatter_rows(mine, theirs):
    got = hop_core(theirs.astype(low_type))
    total = mine + got.astype(wide_type)
    half = total.shape[1] // 2
    low_total = total.astype(low_type)
    first = hop_x(low_total[3, :half])
    second = hop_low(low_total[3, half:])
    low_part = jnp.concatenate(
        [(total[2, :half] + first.astype(wide_type)).astype(low_type), low_total[2, half:]], axis=0
    )
    x_part = jnp.concatenate(
        [low_total[1, :half], (total[1, half:] + second.astype(wide_type)).astype(low_type)], axis=0
    )
    return total[0] + hop_x(x_part).astype(wide_type) + hop_low(low_part).astype(wide_type)


def gather_weight(own, other):
    h, l, y, _, _ = bits()
    ring = lax.axis_size("dp") // 4
    pair = ordered(l, own[None], hop_low(other)[None], 0)
    rows, columns = own.shape
    full = jnp.zeros((ring, 2, 2, rows, columns), own.dtype)

    def put(full, block, at_h, at_y):
        return lax.dynamic_update_slice(full, block[None, :, None], (at_h, 0, at_y, 0, 0))

    full = put(full, pair, h, y)
    travel = pair
    held = [(pair, h)]
    for step in range(1, ring):
        travel = hop_ring(travel)
        held.append((travel, (h - step) % ring))
    for index, (block, at_h) in enumerate(held):
        if index > 0:
            full = put(full, block, at_h, y)
        full = put(full, hop_y(block), at_h, 1 - y)
    return full.reshape(ring * 4 * rows, columns)


def reduce_weight(pairs):
    h, l, y, _, _ = bits()
    ring = lax.axis_size("dp") // 4

    def product(index_y, index_h=None):
        parts = []
        for left, right in pairs:
            width, count = left.shape
            blocks = left.reshape(ring, 2, 2, width // (4 * ring), count)
            rows = lax.dynamic_index_in_dim(blocks, index_y, 2, keepdims=False)
            if index_h is not None:
                rows = lax.dynamic_index_in_dim(rows, index_h, 0, keepdims=False)
            lead = rows.shape[:-1]
            out = jnp.dot(
                rows.reshape(-1, count), right, preferred_element_type=wide_type
            )
            parts.append(out.reshape(*lead, right.shape[1]))
        return parts[0] if len(parts) == 1 else jnp.concatenate(parts, axis=-1)

    got = hop_y(product(1 - y).astype(low_type))

    def term(index_h):
        there = lax.dynamic_index_in_dim(got, index_h, 0, keepdims=False)
        return product(y, index_h) + there.astype(wide_type)

    travel = term((h - 1) % ring)
    for step in range(1, ring):
        travel = hop_ring(travel.astype(low_type)).astype(wide_type) + term((h - 1 - step) % ring)
    mine = lax.dynamic_index_in_dim(travel, l, 0, keepdims=False)
    theirs = lax.dynamic_index_in_dim(travel, 1 - l, 0, keepdims=False)
    return mine, hop_low(theirs.astype(low_type)).astype(wide_type)


def sum_all(value):
    ring = lax.axis_size("dp") // 4
    for step in (hop_core, hop_x, hop_low, hop_y):
        value = value + step(value)
    travel = value
    for _ in range(1, ring):
        travel = hop_ring(travel)
        value = value + travel
    return value


def whole_gains(own):
    h, l, y, _, _ = bits()
    ring = lax.axis_size("dp") // 4
    pair = ordered(l, own[:, None], hop_low(own)[:, None], 1)
    quad = ordered(y, pair[:, :, None], hop_y(pair)[:, :, None], 2)
    full = jnp.zeros((own.shape[0], ring, 2, 2, own.shape[1]), own.dtype)
    travel = quad
    for step in range(ring):
        if step > 0:
            travel = hop_ring(travel)
        full = lax.dynamic_update_slice(full, travel[:, None], (0, (h - step) % ring, 0, 0, 0))
    return full.reshape(own.shape[0], -1)


def norm_back(incoming, unit_rows, inverse_root, gain):
    scaled = incoming * gain
    return inverse_root * (
        scaled - unit_rows * jnp.mean(scaled * unit_rows, axis=-1, keepdims=True)
    )


def contract_last(left_side, weight):
    return lax.dot_general(
        left_side, weight, (((1,), (1,)), ((), ())), preferred_element_type=wide_type
    )


def branch_sum(activation, weight):
    rows = activation.shape[0] // 2

    def part(index):
        out = contract_last(activation[index * rows : (index + 1) * rows], weight)
        return out.reshape(4, rows // 4, weight.shape[0])

    return scatter_rows(part(0), part(1))


def first_norm(inputs, gain):
    inverse = lax.rsqrt(jnp.mean(inputs * inputs, axis=-1, keepdims=True) + eps_norm)
    return inputs * inverse, inverse


def project_body(x_ref, g_ref, w_ref, cos_ref, sin_ref, a_ref, q_ref, kv_ref):
    rows = x_ref.shape[0] * x_ref.shape[2]
    width = x_ref.shape[3]
    x = x_ref[...].astype(wide_type).reshape(rows, width)
    unit = x * lax.rsqrt(jnp.mean(x * x, axis=-1, keepdims=True) + eps_norm)
    normed = (unit * g_ref[...]).astype(low_type)
    a_ref[...] = normed.reshape(a_ref.shape)
    flat = lax.dot_general(
        w_ref[...], normed, (((0,), (1,)), ((), ())), preferred_element_type=wide_type
    )
    cos, sin = cos_ref[0], sin_ref[0]

    def rotated(start):
        first = flat[start : start + HALF]
        second = flat[start + HALF : start + HEAD_SIZE]
        return jnp.concatenate(
            [first * cos - second * sin, second * cos + first * sin], axis=0
        ).astype(low_type)

    for head in range(GROUP):
        q_ref[0, :, head * rows : (head + 1) * rows] = rotated(head * HEAD_SIZE)
    kv_ref[0] = jnp.concatenate(
        [rotated(QROWS), flat[QROWS + HEAD_SIZE :].astype(low_type)], axis=0
    )


def project(rows4, gain, weight, cos, sin):
    _, tiles, per, width = rows4.shape
    wide = 2 * per
    return pl.pallas_call(
        project_body,
        grid=(tiles,),
        in_specs=[
            pl.BlockSpec((2, 1, per, width), lambda t: (0, t, 0, 0)),
            pl.BlockSpec((1, width), lambda t: (0, 0)),
            pl.BlockSpec(weight.shape, lambda t: (0, 0)),
            pl.BlockSpec((1, HALF, wide), lambda t: (t, 0, 0)),
            pl.BlockSpec((1, HALF, wide), lambda t: (t, 0, 0)),
        ],
        out_specs=[
            pl.BlockSpec((2, 1, per, width), lambda t: (0, t, 0, 0)),
            pl.BlockSpec((1, HEAD_SIZE, GROUP * wide), lambda t: (t, 0, 0)),
            pl.BlockSpec((1, BOTH, wide), lambda t: (t, 0, 0)),
        ],
        out_shape=[
            jax.ShapeDtypeStruct(rows4.shape, low_type),
            jax.ShapeDtypeStruct((tiles, HEAD_SIZE, GROUP * wide), low_type),
            jax.ShapeDtypeStruct((tiles, BOTH, wide), low_type),
        ],
        compiler_params=pltpu.CompilerParams(vmem_limit_bytes=48 * 2**20),
        cost_estimate=pl.CostEstimate(
            flops=2 * tiles * wide * width * weight.shape[1],
            bytes_accessed=2 * (2 * tiles * wide * width + weight.size),
            transcendentals=0,
        ),
    )(rows4, gain, weight, cos, sin)


def attend_body(
    seen_ref, base_ref, q_ref, kv_ref, pos_ref, start_ref, local_ref,
    o_ref, ot_ref, lse_ref, top_ref, sum_ref, acc_ref,
):
    tile = pl.program_id(0)
    key_tiles = kv_ref.shape[0]
    top_ref[...] = jnp.full(top_ref.shape, masked_score, wide_type)
    sum_ref[...] = jnp.zeros(sum_ref.shape, wide_type)
    acc_ref[...] = jnp.zeros(acc_ref.shape, wide_type)

    def step(k, carry):
        @pl.when(seen_ref[tile * key_tiles + k] != 0)
        def _():
            keys = kv_ref[k, :HEAD_SIZE]
            values = kv_ref[k, HEAD_SIZE:]
            raw = lax.dot_general(
                keys, q_ref[0], (((0,), (0,)), ((), ())), preferred_element_type=wide_type
            )
            key_pos = base_ref[k] + local_ref[...]
            allowed = (key_pos <= pos_ref[0]) & (key_pos >= start_ref[0])
            raw = jnp.where(allowed, raw, masked_score)
            top_old = top_ref[...]
            top = jnp.maximum(top_old, jnp.max(raw, axis=0, keepdims=True))
            shrink = jnp.exp2((top_old - top) * EXP_SCALE)
            probs = jnp.where(allowed, jnp.exp2((raw - top) * EXP_SCALE), 0.0)
            sum_ref[...] = sum_ref[...] * shrink + jnp.sum(probs, axis=0, keepdims=True)
            acc_ref[...] = acc_ref[...] * shrink + jnp.dot(
                values, probs.astype(low_type), preferred_element_type=wide_type
            )
            top_ref[...] = top

        return carry

    lax.fori_loop(0, key_tiles, step, 0)
    out = acc_ref[...] / sum_ref[...]
    ot_ref[0] = out
    lse_ref[0] = top_ref[...] * EXP_SCALE + jnp.log2(sum_ref[...])
    rows = out.shape[1] // GROUP
    stacked = jnp.concatenate(
        [out[:, head * rows : (head + 1) * rows] for head in range(GROUP)], axis=0
    )
    o_ref[...] = stacked.T.astype(low_type).reshape(o_ref.shape)


def attend(seen, base, q, kv, pos, start, local):
    tiles, _, columns = q.shape
    key_tiles, _, wide = kv.shape
    per = wide // 2
    pairs = tiles * 3 * columns * wide
    return pl.pallas_call(
        attend_body,
        grid=(tiles,),
        in_specs=[
            pl.BlockSpec(memory_space=pltpu.SMEM),
            pl.BlockSpec(memory_space=pltpu.SMEM),
            pl.BlockSpec((1, HEAD_SIZE, columns), lambda t: (t, 0, 0)),
            pl.BlockSpec(kv.shape, lambda t: (0, 0, 0)),
            pl.BlockSpec((1, 1, columns), lambda t: (t, 0, 0)),
            pl.BlockSpec((1, 1, columns), lambda t: (t, 0, 0)),
            pl.BlockSpec(local.shape, lambda t: (0, 0)),
        ],
        out_specs=[
            pl.BlockSpec((2, 1, per, QROWS), lambda t: (0, t, 0, 0)),
            pl.BlockSpec((1, HEAD_SIZE, columns), lambda t: (t, 0, 0)),
            pl.BlockSpec((1, 1, columns), lambda t: (t, 0, 0)),
        ],
        out_shape=[
            jax.ShapeDtypeStruct((2, tiles, per, QROWS), low_type),
            jax.ShapeDtypeStruct((tiles, HEAD_SIZE, columns), wide_type),
            jax.ShapeDtypeStruct((tiles, 1, columns), wide_type),
        ],
        scratch_shapes=[
            pltpu.VMEM((1, columns), wide_type),
            pltpu.VMEM((1, columns), wide_type),
            pltpu.VMEM((HEAD_SIZE, columns), wide_type),
        ],
        compiler_params=pltpu.CompilerParams(vmem_limit_bytes=48 * 2**20),
        cost_estimate=pl.CostEstimate(
            flops=4 * pairs * 256, bytes_accessed=8 * q.size, transcendentals=pairs
        ),
    )(seen, base, q, kv, pos, start, local)


def attend_back_body(
    seen_ref, base_ref, q_ref, kv_ref, pos_ref, start_ref, local_ref,
    go_ref, ot_ref, lse_ref, cos_ref, sin_ref, dq_ref, dkv_ref, acc_ref,
):
    tile = pl.program_id(0)
    key_tiles = kv_ref.shape[0]

    @pl.when(tile == 0)
    def _():
        dkv_ref[...] = jnp.zeros(dkv_ref.shape, wide_type)

    rows = q_ref.shape[2] // GROUP
    turned = go_ref[...].reshape(rows, QROWS).astype(wide_type).T
    grad_wide = jnp.concatenate(
        [turned[head * HEAD_SIZE : (head + 1) * HEAD_SIZE] for head in range(GROUP)], axis=1
    )
    delta = jnp.sum(grad_wide * ot_ref[0], axis=0, keepdims=True)
    grad_out = grad_wide.astype(low_type)
    acc_ref[...] = jnp.zeros(acc_ref.shape, wide_type)

    def step(k, carry):
        @pl.when(seen_ref[tile * key_tiles + k] != 0)
        def _():
            keys = kv_ref[k, :HEAD_SIZE]
            values = kv_ref[k, HEAD_SIZE:]
            raw = lax.dot_general(
                keys, q_ref[0], (((0,), (0,)), ((), ())), preferred_element_type=wide_type
            )
            key_pos = base_ref[k] + local_ref[...]
            allowed = (key_pos <= pos_ref[0]) & (key_pos >= start_ref[0])
            probs = jnp.where(allowed, jnp.exp2(raw * EXP_SCALE - lse_ref[0]), 0.0)
            grad_probs = lax.dot_general(
                values, grad_out, (((0,), (0,)), ((), ())), preferred_element_type=wide_type
            )
            grad_scores = (probs * (grad_probs - delta)).astype(low_type)
            acc_ref[...] += jnp.dot(keys, grad_scores, preferred_element_type=wide_type)
            grad_keys = lax.dot_general(
                q_ref[0], grad_scores, (((1,), (1,)), ((), ())), preferred_element_type=wide_type
            )
            grad_values = lax.dot_general(
                grad_out,
                probs.astype(low_type),
                (((1,), (1,)), ((), ())),
                preferred_element_type=wide_type,
            )
            dkv_ref[k, :HEAD_SIZE] += grad_keys * SCALE
            dkv_ref[k, HEAD_SIZE:] += grad_values

        return carry

    lax.fori_loop(0, key_tiles, step, 0)
    cos, sin = cos_ref[0], sin_ref[0]
    for head in range(GROUP):
        part = acc_ref[:, head * rows : (head + 1) * rows] * SCALE
        first, second = part[:HALF], part[HALF:]
        dq_ref[0, head * HEAD_SIZE : (head + 1) * HEAD_SIZE] = jnp.concatenate(
            [first * cos + second * sin, second * cos - first * sin], axis=0
        ).astype(low_type)


def attend_back(seen, base, q, kv, pos, start, local, grad_out, out_turned, lse, cos, sin):
    tiles, _, columns = q.shape
    key_tiles, _, wide = kv.shape
    per = wide // 2
    pairs = tiles * 3 * columns * wide
    return pl.pallas_call(
        attend_back_body,
        grid=(tiles,),
        in_specs=[
            pl.BlockSpec(memory_space=pltpu.SMEM),
            pl.BlockSpec(memory_space=pltpu.SMEM),
            pl.BlockSpec((1, HEAD_SIZE, columns), lambda t: (t, 0, 0)),
            pl.BlockSpec(kv.shape, lambda t: (0, 0, 0)),
            pl.BlockSpec((1, 1, columns), lambda t: (t, 0, 0)),
            pl.BlockSpec((1, 1, columns), lambda t: (t, 0, 0)),
            pl.BlockSpec(local.shape, lambda t: (0, 0)),
            pl.BlockSpec((2, 1, per, QROWS), lambda t: (0, t, 0, 0)),
            pl.BlockSpec((1, HEAD_SIZE, columns), lambda t: (t, 0, 0)),
            pl.BlockSpec((1, 1, columns), lambda t: (t, 0, 0)),
            pl.BlockSpec((1, HALF, wide), lambda t: (t, 0, 0)),
            pl.BlockSpec((1, HALF, wide), lambda t: (t, 0, 0)),
        ],
        out_specs=[
            pl.BlockSpec((1, QROWS, wide), lambda t: (t, 0, 0)),
            pl.BlockSpec(kv.shape, lambda t: (0, 0, 0)),
        ],
        out_shape=[
            jax.ShapeDtypeStruct((tiles, QROWS, wide), low_type),
            jax.ShapeDtypeStruct(kv.shape, wide_type),
        ],
        scratch_shapes=[pltpu.VMEM((HEAD_SIZE, columns), wide_type)],
        compiler_params=pltpu.CompilerParams(vmem_limit_bytes=48 * 2**20),
        cost_estimate=pl.CostEstimate(
            flops=10 * pairs * 256, bytes_accessed=16 * q.size, transcendentals=pairs
        ),
    )(seen, base, q, kv, pos, start, local, grad_out, out_turned, lse, cos, sin)


def finish_body(dq_ref, dkv_ref, cos_ref, sin_ref, out_ref):
    cos, sin = cos_ref[0], sin_ref[0]
    first, second = dkv_ref[0, :HALF], dkv_ref[0, HALF:HEAD_SIZE]
    turned = jnp.concatenate(
        [
            dq_ref[0].astype(wide_type),
            first * cos + second * sin,
            second * cos - first * sin,
            dkv_ref[0, HEAD_SIZE:],
        ],
        axis=0,
    )
    out_ref[...] = turned.T.astype(low_type).reshape(out_ref.shape)


def finish(dq, dkv, cos, sin):
    tiles, _, wide = dq.shape
    per = wide // 2
    return pl.pallas_call(
        finish_body,
        grid=(tiles,),
        in_specs=[
            pl.BlockSpec((1, QROWS, wide), lambda t: (t, 0, 0)),
            pl.BlockSpec((1, BOTH, wide), lambda t: (t, 0, 0)),
            pl.BlockSpec((1, HALF, wide), lambda t: (t, 0, 0)),
            pl.BlockSpec((1, HALF, wide), lambda t: (t, 0, 0)),
        ],
        out_specs=pl.BlockSpec((2, 1, per, QROWS + BOTH), lambda t: (0, t, 0, 0)),
        out_shape=jax.ShapeDtypeStruct((2, tiles, per, QROWS + BOTH), low_type),
        compiler_params=pltpu.CompilerParams(vmem_limit_bytes=48 * 2**20),
    )(dq, dkv, cos, sin)


def adamw(param, grad, first, second):
    first_new = beta_first * first + (1.0 - beta_first) * grad
    second_new = beta_second * second + (1.0 - beta_second) * grad * grad
    first_hat = first_new / (1.0 - beta_first**STEP)
    second_hat = second_new / (1.0 - beta_second**STEP)
    change = -learn_rate * (first_hat / (jnp.sqrt(second_hat) + adam_eps) + weight_decay * param)
    return (first_new, second_new, change)


def on_device(
    tokens,
    upstream,
    offsets,
    query_weight,
    keyval_weight,
    output_weight,
    gateup_weight,
    down_weight,
    norm_gains,
    first_query,
    first_keyval,
    first_output,
    first_gateup,
    first_down,
    first_gains,
    second_query,
    second_keyval,
    second_output,
    second_gateup,
    second_down,
    second_gains,
):
    h, l, y, xbit, cbit = bits()
    block_rows = offsets.shape[0]
    per = tokens.shape[0]
    width = tokens.shape[1]
    wide = 2 * per
    count = 8 * per
    hidden_part = down_weight.shape[1] // 2

    rows4 = gather_rows(tokens)
    gains = whole_gains(norm_gains.astype(low_type)).astype(wide_type)

    def halves(array, axis=-1):
        size = array.shape[axis] // 2
        return (
            lax.slice_in_dim(array, 0, size, axis=axis),
            lax.slice_in_dim(array, size, 2 * size, axis=axis),
        )

    def split(arrays):
        lower = jnp.concatenate([halves(a)[0].astype(low_type) for a in arrays], axis=-1)
        upper = jnp.concatenate([halves(a)[1].astype(low_type) for a in arrays], axis=-1)
        return choose(l, lower, upper), choose(l, upper, lower)

    qkv_full = gather_weight(*split([query_weight, keyval_weight[0], keyval_weight[1]]))
    output_full = gather_weight(*split([output_weight]))
    gate_full = gather_weight(*split([gateup_weight[0]]))
    up_full = gather_weight(*split([gateup_weight[1]]))
    down_full = gather_weight(*split([down_weight]))

    def relative(own):
        four = own.reshape(2, 2, per)
        four = choose(xbit, four, four[::-1])
        return choose(cbit, four, four[:, ::-1])

    offset_tiles = jnp.concatenate(
        [relative(offsets), relative(hop_low(offsets))], axis=0
    ).reshape(4, wide)
    lane = jnp.arange(wide, dtype=jnp.int32)
    local = choose(cbit, lane, lane ^ per)
    mine = jnp.arange(4, dtype=jnp.int32)

    def bases(group_h, group_y, low_bits, x_bits):
        block = 4 * group_h + 2 * low_bits + group_y
        return block * block_rows + x_bits * wide

    low_bits, x_bits = l ^ (mine // 2), xbit ^ (mine % 2)
    own_base = bases(h, y, low_bits, x_bits)
    one = jnp.ones((2,), jnp.int32)
    key_base = jnp.concatenate(
        [
            own_base,
            bases(h, 1 - y, low_bits, x_bits),
            bases(h - 1, y, one, x_bits[:2]),
            bases(h - 1, 1 - y, one, x_bits[:2]),
        ]
    ).astype(jnp.int32)
    query_pos = own_base[:, None] + local[None, :]
    doc_start = query_pos - offset_tiles
    seen = (
        (key_base[None, :] <= own_base[:, None] + wide - 1)
        & (key_base[None, :] + wide - 1 >= jnp.min(doc_start, axis=1, keepdims=True))
    ).astype(jnp.int32).reshape(-1)
    spread = lambda a: jnp.tile(a, (1, GROUP)).reshape(4, 1, GROUP * wide)
    query_lanes, start_lanes = spread(query_pos), spread(doc_start)
    local_column = local.reshape(wide, 1)
    freqs = rope_base ** (-(jnp.arange(HALF).astype(wide_type) * 2.0 / HEAD_SIZE))
    angle = freqs[None, :, None] * offset_tiles.astype(wide_type)[:, None, :]
    cos, sin = jnp.cos(angle), jnp.sin(angle)

    normed4, q_turned, kv_own = project(rows4, gains[0:1], qkv_full, cos, sin)
    normed_one = normed4.reshape(count, width)

    def last_block(tiles):
        return choose(l, tiles[2:], tiles[:2])

    near = last_block(kv_own)
    kv = jnp.concatenate(
        [kv_own, hop_y(kv_own), to_next(near, 0), to_next(near, 1)], axis=0
    )
    layout = (seen, key_base, q_turned, kv, query_lanes, start_lanes, local_column)
    attended4, out_turned, lse = attend(*layout)
    attended_low = attended4.reshape(count, QROWS)

    inputs = tokens.astype(wide_type)
    inverse_one = lax.rsqrt(jnp.mean(inputs * inputs, axis=-1, keepdims=True) + eps_norm)
    unit_one = inputs * inverse_one
    middle = inputs + branch_sum(attended_low, output_full)
    inverse_two = lax.rsqrt(jnp.mean(middle * middle, axis=-1, keepdims=True) + eps_norm)
    unit_two = middle * inverse_two
    normed_two = gather_rows((unit_two * gains[1]).astype(low_type)).reshape(count, width)
    out_rows = gather_rows(upstream).reshape(count, width)

    gate = jnp.dot(normed_two, gate_full, preferred_element_type=wide_type)
    upward = jnp.dot(normed_two, up_full, preferred_element_type=wide_type)
    sigma = jax.nn.sigmoid(gate)
    hidden = (gate * sigma * upward).astype(low_type)
    down_share = reduce_weight([(out_rows.T, hidden)])
    grad_hidden = jnp.dot(out_rows, down_full, preferred_element_type=wide_type)
    grad_gate = (grad_hidden * upward * sigma * (1.0 + gate * (1.0 - sigma))).astype(low_type)
    grad_up = (grad_hidden * gate * sigma).astype(low_type)
    half = count // 2

    def ffn_part(index):
        rows = slice(index * half, (index + 1) * half)
        out = contract_last(grad_gate[rows], gate_full) + contract_last(grad_up[rows], up_full)
        return out.reshape(4, per, width)

    grad_normed_two = scatter_rows(ffn_part(0), ffn_part(1))
    block_out = (middle + branch_sum(hidden, down_full)).astype(low_type)
    turned_two = normed_two.T
    gate_share = reduce_weight([(turned_two, grad_gate)])
    up_share = reduce_weight([(turned_two, grad_up)])
    gain_two = jnp.sum(grad_normed_two * unit_two, axis=0)
    grad_middle = upstream.astype(wide_type) + norm_back(
        grad_normed_two, unit_two, inverse_two, gains[1]
    )
    branch_grad = gather_rows(grad_middle.astype(low_type)).reshape(count, width)
    grad_attended = jnp.dot(branch_grad, output_full, preferred_element_type=wide_type).astype(
        low_type
    )
    dq_turned, dkv_all = attend_back(
        *layout, grad_attended.reshape(2, 4, per, QROWS), out_turned, lse, cos, sin
    )
    dkv_sent = dkv_all.astype(low_type)
    dkv_own = dkv_all[:4] + hop_y(dkv_sent[4:8]).astype(wide_type)
    dkv_late = to_previous(dkv_sent[8:10], 0).astype(wide_type) + to_previous(
        dkv_sent[10:12], 1
    ).astype(wide_type)
    nothing = jnp.zeros_like(dkv_late)
    dkv_own = dkv_own + choose(
        l,
        jnp.concatenate([nothing, dkv_late], axis=0),
        jnp.concatenate([dkv_late, nothing], axis=0),
    )
    dqkv = finish(dq_turned, dkv_own, cos, sin).reshape(count, QROWS + BOTH)
    grad_normed_one = branch_sum(dqkv, qkv_full)
    attn_share = reduce_weight([(normed_one.T, dqkv), (branch_grad.T, attended_low)])
    gain_one = jnp.sum(grad_normed_one * unit_one, axis=0)
    grad_tokens = grad_middle + norm_back(grad_normed_one, unit_one, inverse_one, gains[0])
    gain_total = sum_all(jnp.stack([gain_one, gain_two]))

    def joined(share, start, stop):
        return ordered(l, share[0][:, start:stop], share[1][:, start:stop], 1)

    edge_one = QROWS + HEAD_SIZE
    edge_two = QROWS + BOTH
    edge_three = edge_two + QROWS
    grad_query = joined(attn_share, 0, QROWS)
    grad_keyval = jnp.stack(
        [joined(attn_share, QROWS, edge_one), joined(attn_share, edge_one, edge_two)]
    )
    grad_output = joined(attn_share, edge_two, edge_three)
    grad_gateup = jnp.stack(
        [joined(gate_share, 0, hidden_part), joined(up_share, 0, hidden_part)]
    )
    grad_down = joined(down_share, 0, hidden_part)
    squares = [
        jnp.sum(part * part)
        for share in (down_share, gate_share, up_share, attn_share)
        for part in share
    ]
    weight_square = sum_all(functools.reduce(jnp.add, squares).reshape(1, 1))[0, 0]
    grad_norm = jnp.sqrt(weight_square + jnp.sum(gain_total * gain_total))
    rows_owned = query_weight.shape[0]
    grad_gains = lax.dynamic_slice_in_dim(
        gain_total, lax.axis_index("dp") * rows_owned, rows_owned, 1
    )
    clipping_bound = math.sqrt(
        MODEL_WIDTH
        * (2 * QUERY_HEAD_COUNT * HEAD_SIZE + 2 * KEY_VALUE_HEADS * HEAD_SIZE + 3 * HIDDEN_UNITS)
        + 2 * MODEL_WIDTH
    )
    clip = jnp.minimum(1.0, clipping_bound / (grad_norm + 1e-06))
    params = (query_weight, keyval_weight, output_weight, gateup_weight, down_weight, norm_gains)
    firsts = (first_query, first_keyval, first_output, first_gateup, first_down, first_gains)
    seconds = (second_query, second_keyval, second_output, second_gateup, second_down, second_gains)
    grads = (grad_query, grad_keyval, grad_output, grad_gateup, grad_down, grad_gains)
    states = [
        adamw(params[index], grads[index] * clip, firsts[index], seconds[index])
        for index in range(6)
    ]
    return (
        block_out,
        grad_tokens,
        grad_norm,
        *grads,
        *[state[0] for state in states],
        *[state[1] for state in states],
        *[state[2] for state in states],
    )


def solution(mesh):
    weights = (
        P("dp", "mp"),
        P(None, "dp", "mp"),
        P("dp", "mp"),
        P(None, "dp", "mp"),
        P("dp", "mp"),
        P(None, "dp"),
    )
    rows = P(("dp", "mp"), None)
    return jax.shard_map(
        on_device,
        mesh=mesh,
        in_specs=(rows, rows, P("dp"), *weights, *weights, *weights),
        out_specs=(rows, rows, P(), *weights, *weights, *weights, *weights),
        check_vma=False,
    )
```

time: 1760 us -> 1100 us (0.62)
  waiting for transfers between devices: 1310 us -> 499 us
  starting transfers between devices: 11.7 us -> 133 us
  blocking collectives: 67.8 us -> 0 us
  other arithmetic: 73.4 us -> 138 us
  matrix products: 182 us -> 120 us
  local copies, waits for them, and re-layouts: 90.2 us -> 148 us
  Pallas kernels: 0 us -> 32.3 us
    all_gather x9 -> x0, waiting for transfers between devices: 645 us -> none  [the longest x1 355 us: on_device(): lax.all_gather(gateup_weight.astype(low_type), 'dp', axis=1, tiled=True)]
    reduce_scatter x5 -> x0, waiting for transfers between devices: 630 us -> none  [the longest x1 564 us: on_device(): lax.psum_scatter(weight_terms(attn_pairs + ffn_pairs).astype(jnp.bfloat16...]
    ppermute x4 -> x92, waiting for transfers between devices: 32.7 us -> 499 us  [hop(): return lax.ppermute(block, AXES, route)]
    ppermute x4 -> x92, starting transfers between devices: 10.9 us -> 133 us  [hop(): return lax.ppermute(block, AXES, route)]
    dot_general x18 -> x17, matrix products: 124 us -> 58.8 us  [the longest x15 38.1 us: product(): jnp.dot(rows.reshape(-1, count), right, preferred_element_type=wide_type)]
    unnamed x138 -> x252, local copies, waits for them, and re-layouts: 76.4 us -> 29 us
    reshape x0 -> x6, local copies, waits for them, and re-layouts: none -> 43.5 us  [the longest x2 11.3 us: gather_weight(): return full.reshape(ring * 4 * rows, columns)]
    dynamic_update_slice x0 -> x18, local copies, waits for them, and re-layouts: none -> 41.5 us  [the longest x16 41.5 us: put(): lax.dynamic_update_slice(full, block[None, :, None], (at_h, 0, at_y, 0, 0))]
  transfers between devices with their start and end apart: 18 -> 92, of which waited for: 16 -> 44; matrix products, arithmetic and copies ran while one was open for 11% -> 28% of each run, Pallas kernels for 0% -> 1%
where the time goes in v1:
time: 1100 us; the launch traced here: 1080 us
  waiting for transfers between devices  499 us (45%)
  local copies, waits for them, and re-layouts  148 us (13%)
  other arithmetic  138 us (13%)
  starting transfers between devices  133 us (12%)
  matrix products  120 us (11%)
  Pallas kernels  32.3 us (3%)
  between operations  13.5 us (1%)
    ppermute x92, waiting for transfers between devices, hop(): return lax.ppermute(block, AXES, route)  499 us
    ppermute x92, starting transfers between devices, hop(): return lax.ppermute(block, AXES, route)  133 us
    dot_general x10, matrix products, contract_last(): lax.dot_general(left_side, weight, (((1,), (1,)), ((), ())), preferred_el...  45.5 us
    dynamic_update_slice x16, local copies, waits for them, and re-layouts, put(): lax.dynamic_update_slice(full, block[None, :, None], (at_h, 0, at_y, 0, 0))  41.5 us
    dot_general x15, matrix products, product(): jnp.dot(rows.reshape(-1, count), right, preferred_element_type=wide_type)  38.1 us
    unnamed x252, local copies, waits for them, and re-layouts  29 us
    mul x6, other arithmetic, adamw(): -learn_rate  26.4 us
    another operation x8, other arithmetic, gather_rows(): return jnp.stack([four, hop_core(four)])  26.3 us
  transfers between devices with their start and end apart: 92, of which 44 were waited for; matrix products, arithmetic and copies ran while one was open for 28% of the time, Pallas kernels for 1%

profile of v1, /device:TPU:0, one launch (start us, length us, event | category | flops | bytes accessed | tf_op | source)
XLA Modules:
  0.0 1082.7 jit_solution(12111007629695025120)
XLA Ops:
  68.6 30.9 %collective-permute-done.11 = bf16[2,320,480]{2,1,0:T(8,128)(2,1)} collective-permute-done((bf16[2,320,480]{2,1,0:T(8,128)(2,1)}, bf16[2,320,480]{2,1,0:T(8,128)(2,1)}, u32[]{:S(2)}, u32[]{:S(2)}) %collective-permute-start.11) | collective-permute-done | bytes 614432 | tf_op jit(solution)/shard_map/ppermute | solution.py:47
  132.4 17.9 %dynamic_update_slice.75 = bf16[2,2,2,320,320]{3,2,1,0,4:T(2,128)(2,1)} dynamic-update-slice(bf16[2,2,2,320,320]{3,2,1,0,4:T(2,128)(2,1)} %copy.110, bf16[1,2,1,320,320]{3,2,1,0,4:T(2,128)(2,1)} %copy.111, s32[]{:T(128)S(6)} %select_n.631, s32[]{:T(128)} %constant.582.clone.1, s32[]{:T(128)S(6)} %select_n.642, s32[]{:T(128)} %constant.582.clone.1, s32[]{:T(128)} %constant.582.clone.1) | dynamic-update-slice | bytes 819204 | tf_op jit(solution)/shard_map/dynamic_update_slice | solution.py:132
  178.3 11.0 %shard_map.413 = (bf16[2,4,128,320]{3,2,1,0:T(8,128)(2,1)S(1)}, f32[4,80,1024]{2,1,0:T(8,128)S(1)}, f32[4,1,1024]{2,1,0:T(1,128)S(1)}) custom-call(s32[48]{0:T(128)S(1)} %copy-done.19, s32[12]{0:T(128)S(1)} %copy-done.17, bf16[4,80,1024]{2,1,0:T(8,128)(2,1)S(1)} %get-tuple-element.35.q_ref, ...), custom_call_target="tpu_custom_call" | custom-call | flops 3221225472 | bytes 2621440 | tf_op jit(solution)/shard_map/pallas_call | solution.py:340
  252.8 14.2 %collective-permute-done.48 = bf16[128,2560]{1,0:T(8,128)(2,1)} collective-permute-done((bf16[128,2560]{1,0:T(8,128)(2,1)}, bf16[128,2560]{1,0:T(8,128)(2,1)}, u32[]{:S(2)}, u32[]{:S(2)}) %collective-permute-start.48) | collective-permute-done | bytes 655392 | tf_op jit(solution)/shard_map/ppermute | solution.py:47
  324.0 25.5 %collective-permute-done.24 = bf16[128,2560]{1,0:T(8,128)(2,1)S(1)} collective-permute-done((bf16[128,2560]{1,0:T(8,128)(2,1)S(1)}, bf16[128,2560]{1,0:T(8,128)(2,1)S(1)}, u32[]{:S(2)}, u32[]{:S(2)}) %collective-permute-start.24) | collective-permute-done | bytes 655392 | tf_op jit(solution)/shard_map/ppermute | solution.py:47
  353.3 31.7 %collective-permute-done.40 = bf16[2,320,896]{2,1,0:T(8,128)(2,1)S(1)} collective-permute-done((bf16[2,320,896]{2,1,0:T(8,128)(2,1)}, bf16[2,320,896]{2,1,0:T(8,128)(2,1)S(1)}, u32[]{:S(2)}, u32[]{:S(2)}) %collective-permute-start.40) | collective-permute-done | bytes 1146912 | tf_op jit(solution)/shard_map/ppermute | solution.py:47
  388.2 20.3 %collective-permute-done.32 = bf16[2,320,896]{2,1,0:T(8,128)(2,1)S(1)} collective-permute-done((bf16[2,320,896]{2,1,0:T(8,128)(2,1)S(1)}, bf16[2,320,896]{2,1,0:T(8,128)(2,1)S(1)}, u32[]{:S(2)}, u32[]{:S(2)}) %collective-permute-start.32) | collective-permute-done | bytes 1146912 | tf_op jit(solution)/shard_map/ppermute | solution.py:47
  411.3 11.3 %collective-permute-done.26 = bf16[128,2560]{1,0:T(8,128)(2,1)S(1)} collective-permute-done((bf16[128,2560]{1,0:T(8,128)(2,1)S(1)}, bf16[128,2560]{1,0:T(8,128)(2,1)S(1)}, u32[]{:S(2)}, u32[]{:S(2)}) %collective-permute-start.26) | collective-permute-done | bytes 655392 | tf_op jit(solution)/shard_map/ppermute | solution.py:47
  440.2 21.9 %collective-permute-done.33 = bf16[2,320,896]{2,1,0:T(8,128)(2,1)S(1)} collective-permute-done((bf16[2,320,896]{2,1,0:T(8,128)(2,1)S(1)}, bf16[2,320,896]{2,1,0:T(8,128)(2,1)S(1)}, u32[]{:S(2)}, u32[]{:S(2)}) %collective-permute-start.33) | collective-permute-done | bytes 1146912 | tf_op jit(solution)/shard_map/ppermute | solution.py:47
  505.2 10.2 fusion.205
  515.4 10.4 multiply_convert_fusion.1
  590.5 11.4 %collective-permute-done.56 = bf16[128,2560]{1,0:T(8,128)(2,1)S(1)} collective-permute-done((bf16[128,2560]{1,0:T(8,128)(2,1)S(1)}, bf16[128,2560]{1,0:T(8,128)(2,1)S(1)}, u32[]{:S(2)}, u32[]{:S(2)}) %collective-permute-start.56) | collective-permute-done | bytes 655392 | tf_op jit(solution)/shard_map/ppermute | solution.py:47
  633.6 11.6 %collective-permute-done.58 = bf16[128,2560]{1,0:T(8,128)(2,1)S(1)} collective-permute-done((bf16[128,2560]{1,0:T(8,128)(2,1)S(1)}, bf16[128,2560]{1,0:T(8,128)(2,1)S(1)}, u32[]{:S(2)}, u32[]{:S(2)}) %collective-permute-start.58) | collective-permute-done | bytes 655392 | tf_op jit(solution)/shard_map/ppermute | solution.py:47
  653.0 13.9 %collective-permute-done.60 = bf16[64,2560]{1,0:T(8,128)(2,1)S(1)} collective-permute-done((bf16[64,2560]{1,0:T(8,128)(2,1)S(1)}, bf16[64,2560]{1,0:T(8,128)(2,1)S(1)}, u32[]{:S(2)}, u32[]{:S(2)}) %collective-permute-start.60) | collective-permute-done | bytes 327712 | tf_op jit(solution)/shard_map/ppermute | solution.py:47
  667.7 27.4 %collective-permute-done.73 = bf16[2,2,320,896]{3,2,1,0:T(8,128)(2,1)} collective-permute-done((bf16[2,2,320,896]{3,2,1,0:T(8,128)(2,1)}, bf16[2,2,320,896]{3,2,1,0:T(8,128)(2,1)}, u32[]{:S(2)}, u32[]{:S(2)}) %collective-permute-start.73) | collective-permute-done | bytes 2293792 | tf_op jit(solution)/shard_map/ppermute | solution.py:47
  702.8 25.1 %collective-permute-done.71 = bf16[2,320,896]{2,1,0:T(8,128)(2,1)S(1)} collective-permute-done((bf16[2,320,896]{2,1,0:T(8,128)(2,1)S(1)}, bf16[2,320,896]{2,1,0:T(8,128)(2,1)S(1)}, u32[]{:S(2)}, u32[]{:S(2)}) %collective-permute-start.71) | collective-permute-done | bytes 1146912 | tf_op jit(solution)/shard_map/ppermute | solution.py:47
  730.4 22.2 %collective-permute-done.77 = bf16[2,320,896]{2,1,0:T(8,128)(2,1)S(1)} collective-permute-done((bf16[2,320,896]{2,1,0:T(8,128)(2,1)S(1)}, bf16[2,320,896]{2,1,0:T(8,128)(2,1)S(1)}, u32[]{:S(2)}, u32[]{:S(2)}) %collective-permute-start.77) | collective-permute-done | bytes 1146912 | tf_op jit(solution)/shard_map/ppermute | solution.py:47
  754.3 18.9 %collective-permute-done.74 = bf16[2,320,896]{2,1,0:T(8,128)(2,1)S(1)} collective-permute-done((bf16[2,320,896]{2,1,0:T(8,128)(2,1)S(1)}, bf16[2,320,896]{2,1,0:T(8,128)(2,1)S(1)}, u32[]{:S(2)}, u32[]{:S(2)}) %collective-permute-start.74) | collective-permute-done | bytes 1146912 | tf_op jit(solution)/shard_map/ppermute | solution.py:47
  781.8 15.8 %collective-permute-done.78 = bf16[320,896]{1,0:T(8,128)(2,1)S(1)} collective-permute-done((bf16[320,896]{1,0:T(8,128)(2,1)S(1)}, bf16[320,896]{1,0:T(8,128)(2,1)S(1)}, u32[]{:S(2)}, u32[]{:S(2)}) %collective-permute-start.78) | collective-permute-done | bytes 573472 | tf_op jit(solution)/shard_map/ppermute | solution.py:47
  816.5 12.7 %shard_map.414 = (bf16[4,320,256]{2,1,0:T(8,128)(2,1)S(1)}, f32[12,160,256]{2,1,0:T(8,128)}) custom-call(s32[48]{0:T(128)S(1)} %copy-done.20, s32[12]{0:T(128)S(1)} %copy-done.18, bf16[4,80,1024]{2,1,0:T(8,128)(2,1)S(1)} %copy-done.22, bf16[12,160,256]{2,1,0:T(8,128)(2,1)S(1)} %copy-done.13, s32[4,1,1024]{2,1,0:T(1,128)S(1)} %tile.17.pos_ref, ...), custom_call_target="tpu_custom_call" | custom-call | flops 8053063680 | bytes 5242880 | tf_op jit(solution)/shard_map/pallas_call | solution.py:439
  892.9 41.6 %collective-permute-done.79 = bf16[2,2,320,800]{3,2,1,0:T(8,128)(2,1)S(1)} collective-permute-done((bf16[2,2,320,800]{3,2,1,0:T(8,128)(2,1)S(1)}, bf16[2,2,320,800]{3,2,1,0:T(8,128)(2,1)S(1)}, u32[]{:S(2)}, u32[]{:S(2)}) %collective-permute-start.79) | collective-permute-done | bytes 2048032 | tf_op jit(solution)/shard_map/ppermute | solution.py:47
  944.2 45.8 %collective-permute-done.80 = bf16[2,320,800]{2,1,0:T(8,128)(2,1)S(1)} collective-permute-done((bf16[2,320,800]{2,1,0:T(8,128)(2,1)S(1)}, bf16[2,320,800]{2,1,0:T(8,128)(2,1)S(1)}, u32[]{:S(2)}, u32[]{:S(2)}) %collective-permute-start.80) | collective-permute-done | bytes 1024032 | tf_op jit(solution)/shard_map/ppermute | solution.py:47
  994.2 12.3 %collective-permute-done.81 = bf16[320,800]{1,0:T(8,128)(2,1)S(1)} collective-permute-done((bf16[320,800]{1,0:T(8,128)(2,1)}, bf16[320,800]{1,0:T(8,128)(2,1)S(1)}, u32[]{:S(2)}, u32[]{:S(2)}) %collective-permute-start.81) | collective-permute-done | bytes 512032 | tf_op jit(solution)/shard_map/ppermute | solution.py:47
  1065.2 11.2 %add_multiply_fusion = (f32[2,320,1792]{2,1,0:T(8,128)}, f32[2,320,1792]{2,1,0:T(8,128)}, f32[2,320,1792]{2,1,0:T(8,128)}, f32[2,320,1792]{2,1,0:T(8,128)}) fusion(f32[2,320,1792]{2,1,0:T(8,128)S(1)} %bitcast.529, f32[]{:T(128)S(6)} %min.3, f32[2,320,1792]{2,1,0:T(8,128)} %param.39, f32[2,320,1792]{2,1,0:T(8,128)} %param.33, ...), kind=kLoop, calls=%fused_computation.13 | loop fusion | flops 18350080 | bytes 36700164 | tf_op jit(solution)/shard_map/mul | solution.py:510
  (652 shorter events, 594.0 us)
Async XLA Ops:
  46.5 110.5 %collective-permute-start.5 = (bf16[4,128,2560]{2,1,0:T(8,128)(2,1)}, bf16[4,128,2560]{2,1,0:T(8,128)(2,1)}, u32[]{:S(2)}, u32[]{:S(2)}) collective-permute-start(bf16[4,128,2560]{2,1,0:T(8,128)(2,1)} %get-tuple-element.180), channel_id=1, source_target_pairs={{0,1},{1,0},{2,3},{3,2},{4,5},{5,4},{6,7},{7,6},{8,9},{9,8},{10,11... | collective-permute-start | bytes 7864328 | tf_op jit(solution)/shard_map/ppermute | solution.py:47
  63.9 53.6 %collective-permute-start.10 = (bf16[2,320,480]{2,1,0:T(8,128)(2,1)}, bf16[2,320,480]{2,1,0:T(8,128)(2,1)}, u32[]{:S(2)}, u32[]{:S(2)}) collective-permute-start(bf16[2,320,480]{2,1,0:T(8,128)(2,1)} %maximum_select_fusion.12), channel_id=1, source_target_pairs={{0,4},{1,5},{2,6},{3,7},{4,0},{5,1},{6,2},{7,3},{8,12},{9,13},{10,... | collective-permute-start | bytes 1843208 | tf_op jit(solution)/shard_map/ppermute | solution.py:47
  99.5 56.4 %collective-permute-start.12 = (bf16[2,320,480]{2,1,0:T(8,128)(2,1)}, bf16[2,320,480]{2,1,0:T(8,128)(2,1)}, u32[]{:S(2)}, u32[]{:S(2)}) collective-permute-start(bf16[2,320,480]{2,1,0:T(8,128)(2,1)} %collective-permute-done.11), channel_id=1, source_target_pairs={{0,4},{1,5},{2,6},{3,7},{4,0},{5,1},{6,2},{7,3},{8,12},{9,13},{10,... | collective-permute-start | bytes 1843208 | tf_op jit(solution)/shard_map/ppermute | solution.py:47
  192.3 94.9 %collective-permute-start.20 = (bf16[4,128,2560]{2,1,0:T(8,128)(2,1)}, bf16[4,128,2560]{2,1,0:T(8,128)(2,1)}, u32[]{:S(2)}, u32[]{:S(2)}) collective-permute-start(bf16[4,128,2560]{2,1,0:T(8,128)(2,1)} %convolution_convert_fusion.2), channel_id=1, source_target_pairs={{0,1},{1,0},{2,3},{3,2},{4,5},{5,4},{6,7},{7,6},{8,9},{9,8},{10,11... | collective-permute-start | bytes 7864328 | tf_op jit(solution)/shard_map/ppermute | solution.py:47
  229.9 83.3 %collective-permute-start.35 = (bf16[2,320,896]{2,1,0:T(8,128)(2,1)}, bf16[2,320,896]{2,1,0:T(8,128)(2,1)}, u32[]{:S(2)}, u32[]{:S(2)}) collective-permute-start(bf16[2,320,896]{2,1,0:T(8,128)(2,1)} %maximum_select_fusion.6), channel_id=1, source_target_pairs={{0,4},{1,5},{2,6},{3,7},{4,0},{5,1},{6,2},{7,3},{8,12},{9,13},{10,... | collective-permute-start | bytes 3440648 | tf_op jit(solution)/shard_map/ppermute | solution.py:47
  240.5 76.6 %collective-permute-start.36 = (bf16[2,320,896]{2,1,0:T(8,128)(2,1)}, bf16[2,320,896]{2,1,0:T(8,128)(2,1)}, u32[]{:S(2)}, u32[]{:S(2)}) collective-permute-start(bf16[2,320,896]{2,1,0:T(8,128)(2,1)} %maximum_select_fusion.6), channel_id=1, source_target_pairs={{0,16},{1,17},{2,18},{3,19},{4,20},{5,21},{6,22},{7,23},{8,24},{9,... | collective-permute-start | bytes 3440648 | tf_op jit(solution)/shard_map/ppermute | solution.py:47
  306.3 78.6 %collective-permute-start.40 = (bf16[2,320,896]{2,1,0:T(8,128)(2,1)}, bf16[2,320,896]{2,1,0:T(8,128)(2,1)S(1)}, u32[]{:S(2)}, u32[]{:S(2)}) collective-permute-start(bf16[2,320,896]{2,1,0:T(8,128)(2,1)} %maximum_select_fusion.8), channel_id=1, source_target_pairs={{0,16},{1,17},{2,18},{3,19},{4,20},{5,21},{6,22},{7,23},{8,24},{9,... | collective-permute-start | bytes 3440648 | tf_op jit(solution)/shard_map/ppermute | solution.py:47
  317.1 68.9 %collective-permute-start.31 = (bf16[2,320,896]{2,1,0:T(8,128)(2,1)S(1)}, bf16[2,320,896]{2,1,0:T(8,128)(2,1)S(1)}, u32[]{:S(2)}, u32[]{:S(2)}) collective-permute-start(bf16[2,320,896]{2,1,0:T(8,128)(2,1)S(1)} %copy-done.79), channel_id=1, source_target_pairs={{0,4},{1,5},{2,6},{3,7},{4,0},{5,1},{6,2},{7,3},{8,12},{9,13},{10,... | collective-permute-start | bytes 3440648 | tf_op jit(solution)/shard_map/ppermute | solution.py:47
  321.6 87.0 %collective-permute-start.32 = (bf16[2,320,896]{2,1,0:T(8,128)(2,1)S(1)}, bf16[2,320,896]{2,1,0:T(8,128)(2,1)S(1)}, u32[]{:S(2)}, u32[]{:S(2)}) collective-permute-start(bf16[2,320,896]{2,1,0:T(8,128)(2,1)S(1)} %copy-done.79), channel_id=1, source_target_pairs={{0,16},{1,17},{2,18},{3,19},{4,20},{5,21},{6,22},{7,23},{8,24},{9,... | collective-permute-start | bytes 3440648 | tf_op jit(solution)/shard_map/ppermute | solution.py:47
  349.5 112.8 %collective-permute-start.51 = (bf16[4,128,2560]{2,1,0:T(8,128)(2,1)S(1)}, bf16[4,128,2560]{2,1,0:T(8,128)(2,1)S(1)}, u32[]{:S(2)}, u32[]{:S(2)}) collective-permute-start(bf16[4,128,2560]{2,1,0:T(8,128)(2,1)S(1)} %copy-done.56), channel_id=1, source_target_pairs={{0,1},{1,0},{2,3},{3,2},{4,5},{5,4},{6,7},{7,6},{8,9},{9,8},{10,11... | collective-permute-start | bytes 7864328 | tf_op jit(solution)/shard_map/ppermute | solution.py:47
  351.8 58.7 %collective-permute-start.25 = (bf16[128,2560]{1,0:T(8,128)(2,1)S(1)}, bf16[128,2560]{1,0:T(8,128)(2,1)S(1)}, u32[]{:S(2)}, u32[]{:S(2)}) collective-permute-start(bf16[128,2560]{1,0:T(8,128)(2,1)S(1)} %multiply_convert_fusion.3), channel_id=1, source_target_pairs={{0,2},{1,3},{2,0},{3,1},{4,6},{5,7},{6,4},{7,5},{8,10},{9,11},{10,... | collective-permute-start | bytes 1966088 | tf_op jit(solution)/shard_map/ppermute | solution.py:47
  434.9 57.8 %collective-permute-start.29 = (bf16[4,128,2560]{2,1,0:T(8,128)(2,1)}, bf16[4,128,2560]{2,1,0:T(8,128)(2,1)}, u32[]{:S(2)}, u32[]{:S(2)}) collective-permute-start(bf16[4,128,2560]{2,1,0:T(8,128)(2,1)} %get-tuple-element.174), channel_id=1, source_target_pairs={{0,1},{1,0},{2,3},{3,2},{4,5},{5,4},{6,7},{7,6},{8,9},{9,8},{10,11... | collective-permute-start | bytes 7864328 | tf_op jit(solution)/shard_map/ppermute | solution.py:47
  544.7 76.9 %collective-permute-start.70 = (bf16[2,2,320,896]{3,2,1,0:T(8,128)(2,1)}, bf16[2,2,320,896]{3,2,1,0:T(8,128)(2,1)}, u32[]{:S(2)}, u32[]{:S(2)}) collective-permute-start(bf16[2,2,320,896]{3,2,1,0:T(8,128)(2,1)} %fusion.25), channel_id=1, source_target_pairs={{0,4},{1,5},{2,6},{3,7},{4,0},{5,1},{6,2},{7,3},{8,12},{9,13},{10,... | collective-permute-start | bytes 6881288 | tf_op jit(solution)/shard_map/ppermute | solution.py:47
  550.6 96.3 %collective-permute-start.76 = (bf16[2,2,320,896]{3,2,1,0:T(8,128)(2,1)}, bf16[2,2,320,896]{3,2,1,0:T(8,128)(2,1)}, u32[]{:S(2)}, u32[]{:S(2)}) collective-permute-start(bf16[2,2,320,896]{3,2,1,0:T(8,128)(2,1)} %fusion.31), channel_id=1, source_target_pairs={{0,4},{1,5},{2,6},{3,7},{4,0},{5,1},{6,2},{7,3},{8,12},{9,13},{10,... | collective-permute-start | bytes 6881288 | tf_op jit(solution)/shard_map/ppermute | solution.py:47
  604.0 91.1 %collective-permute-start.73 = (bf16[2,2,320,896]{3,2,1,0:T(8,128)(2,1)}, bf16[2,2,320,896]{3,2,1,0:T(8,128)(2,1)}, u32[]{:S(2)}, u32[]{:S(2)}) collective-permute-start(bf16[2,2,320,896]{3,2,1,0:T(8,128)(2,1)} %fusion.28), channel_id=1, source_target_pairs={{0,4},{1,5},{2,6},{3,7},{4,0},{5,1},{6,2},{7,3},{8,12},{9,13},{10,... | collective-permute-start | bytes 6881288 | tf_op jit(solution)/shard_map/ppermute | solution.py:47
  624.6 103.3 %collective-permute-start.71 = (bf16[2,320,896]{2,1,0:T(8,128)(2,1)S(1)}, bf16[2,320,896]{2,1,0:T(8,128)(2,1)S(1)}, u32[]{:S(2)}, u32[]{:S(2)}) collective-permute-start(bf16[2,320,896]{2,1,0:T(8,128)(2,1)S(1)} %fusion.24), channel_id=1, source_target_pairs={{0,16},{1,17},{2,18},{3,19},{4,20},{5,21},{6,22},{7,23},{8,24},{9,... | collective-permute-start | bytes 3440648 | tf_op jit(solution)/shard_map/ppermute | solution.py:47
  649.7 102.8 %collective-permute-start.77 = (bf16[2,320,896]{2,1,0:T(8,128)(2,1)S(1)}, bf16[2,320,896]{2,1,0:T(8,128)(2,1)S(1)}, u32[]{:S(2)}, u32[]{:S(2)}) collective-permute-start(bf16[2,320,896]{2,1,0:T(8,128)(2,1)S(1)} %fusion.20), channel_id=1, source_target_pairs={{0,16},{1,17},{2,18},{3,19},{4,20},{5,21},{6,22},{7,23},{8,24},{9,... | collective-permute-start | bytes 3440648 | tf_op jit(solution)/shard_map/ppermute | solution.py:47
  667.6 131.2 %collective-permute-start.61 = (bf16[4,128,2560]{2,1,0:T(8,128)(2,1)S(1)}, bf16[4,128,2560]{2,1,0:T(8,128)(2,1)S(1)}, u32[]{:S(2)}, u32[]{:S(2)}) collective-permute-start(bf16[4,128,2560]{2,1,0:T(8,128)(2,1)S(1)} %get-tuple-element.162), channel_id=1, source_target_pairs={{0,1},{1,0},{2,3},{3,2},{4,5},{5,4},{6,7},{7,6},{8,9},{9,8},{10,11... | collective-permute-start | bytes 7864328 | tf_op jit(solution)/shard_map/ppermute | solution.py:47
  697.9 75.3 %collective-permute-start.74 = (bf16[2,320,896]{2,1,0:T(8,128)(2,1)S(1)}, bf16[2,320,896]{2,1,0:T(8,128)(2,1)S(1)}, u32[]{:S(2)}, u32[]{:S(2)}) collective-permute-start(bf16[2,320,896]{2,1,0:T(8,128)(2,1)S(1)} %fusion.22), channel_id=1, source_target_pairs={{0,16},{1,17},{2,18},{3,19},{4,20},{5,21},{6,22},{7,23},{8,24},{9,... | collective-permute-start | bytes 3440648 | tf_op jit(solution)/shard_map/ppermute | solution.py:47
  730.4 105.8 %collective-permute-start.72 = (bf16[320,896]{1,0:T(8,128)(2,1)}, bf16[320,896]{1,0:T(8,128)(2,1)}, u32[]{:S(2)}, u32[]{:S(2)}) collective-permute-start(bf16[320,896]{1,0:T(8,128)(2,1)} %fusion.131), channel_id=1, source_target_pairs={{0,8},{1,9},{2,10},{3,11},{4,12},{5,13},{6,14},{7,15},{8,0},{9,1},... | collective-permute-start | bytes 1720328 | tf_op jit(solution)/shard_map/ppermute | solution.py:47
  775.8 68.7 %collective-permute-start.75 = (bf16[320,896]{1,0:T(8,128)(2,1)}, bf16[320,896]{1,0:T(8,128)(2,1)}, u32[]{:S(2)}, u32[]{:S(2)}) collective-permute-start(bf16[320,896]{1,0:T(8,128)(2,1)} %fusion.132), channel_id=1, source_target_pairs={{0,8},{1,9},{2,10},{3,11},{4,12},{5,13},{6,14},{7,15},{8,0},{9,1},... | collective-permute-start | bytes 1720328 | tf_op jit(solution)/shard_map/ppermute | solution.py:47
  934.9 55.1 %collective-permute-start.80 = (bf16[2,320,800]{2,1,0:T(8,128)(2,1)S(1)}, bf16[2,320,800]{2,1,0:T(8,128)(2,1)S(1)}, u32[]{:S(2)}, u32[]{:S(2)}) collective-permute-start(bf16[2,320,800]{2,1,0:T(8,128)(2,1)S(1)} %fusion.17), channel_id=1, source_target_pairs={{0,16},{1,17},{2,18},{3,19},{4,20},{5,21},{6,22},{7,23},{8,24},{9,... | collective-permute-start | bytes 3072008 | tf_op jit(solution)/shard_map/ppermute | solution.py:47
  941.4 68.7 %collective-permute-start.69 = (bf16[128,2560]{1,0:T(8,128)(2,1)}, bf16[128,2560]{1,0:T(8,128)(2,1)S(1)}, u32[]{:S(2)}, u32[]{:S(2)}) collective-permute-start(bf16[128,2560]{1,0:T(8,128)(2,1)} %pad_maximum_fusion.17), channel_id=1, source_target_pairs={{0,8},{1,9},{2,10},{3,11},{4,12},{5,13},{6,14},{7,15},{8,0},{9,1},... | collective-permute-start | bytes 1966088 | tf_op jit(solution)/shard_map/ppermute | solution.py:47
  942.7 67.4 %collective-permute-start.67 = (bf16[128,2560]{1,0:T(8,128)(2,1)}, bf16[128,2560]{1,0:T(8,128)(2,1)}, u32[]{:S(2)}, u32[]{:S(2)}) collective-permute-start(bf16[128,2560]{1,0:T(8,128)(2,1)} %pad_maximum_fusion.16), channel_id=1, source_target_pairs={{0,2},{1,3},{2,0},{3,1},{4,6},{5,7},{6,4},{7,5},{8,10},{9,11},{10,... | collective-permute-start | bytes 1966088 | tf_op jit(solution)/shard_map/ppermute | solution.py:47
  (189 other events, 3046.0 us)

commit v2 on v1

v2 whole, which is shorter than its diff:
```python
import functools
import math

import jax
import jax.numpy as jnp
from jax import lax
from jax.experimental import pallas as pl
from jax.experimental.pallas import tpu as pltpu
from jax.sharding import PartitionSpec as P

MODEL_WIDTH = 2560
QUERY_HEAD_COUNT = 32
KEY_VALUE_HEADS = 8
HEAD_SIZE = 80
HIDDEN_UNITS = 7168
STEP = 10

eps_norm = 1e-05
rope_base = 1000000.0
beta_first = 0.9
beta_second = 0.95
learn_rate = 0.02
weight_decay = 0.1
adam_eps = 1e-08
masked_score = -1e30

low_type = jnp.bfloat16
wide_type = jnp.float32

HALF = HEAD_SIZE // 2
GROUP = QUERY_HEAD_COUNT // KEY_VALUE_HEADS
QROWS = GROUP * HEAD_SIZE
BOTH = 2 * HEAD_SIZE
EDGE = QROWS + BOTH
EXP_SCALE = (HEAD_SIZE ** (-0.5)) * math.log2(math.e)
SCALE = HEAD_SIZE ** (-0.5)
AXES = ("dp", "mp")


def hop(block, move):
    dp_size, mp_size = lax.axis_size("dp"), lax.axis_size("mp")
    route = []
    for d in range(dp_size):
        for m in range(mp_size):
            target = move(d, m)
            if target is not None:
                route.append((d * mp_size + m, target[0] * mp_size + target[1]))
    return lax.ppermute(block, AXES, route)


def hop_core(block):
    return hop(block, lambda d, m: (d, m ^ 1))


def hop_x(block):
    return hop(block, lambda d, m: (d, m ^ 2))


def hop_low(block):
    return hop(block, lambda d, m: (d ^ 2, m))


def hop_y(block):
    return hop(block, lambda d, m: (d ^ 1, m))


def hop_ring(block):
    size = lax.axis_size("dp")
    return hop(block, lambda d, m: ((d + 4) % size, m))


def to_next(block, flip):
    size = lax.axis_size("dp")

    def move(d, m):
        if d + 4 >= size or (flip and d % 2 == 0):
            return None
        return (d + 4) ^ flip, m

    return hop(block, move)


def to_previous(block, flip):
    def move(d, m):
        if d < 4 or (flip and d % 2 == 1):
            return None
        return (d - 4) ^ flip, m

    return hop(block, move)


def bits():
    d = lax.axis_index("dp")
    m = lax.axis_index("mp")
    return d // 4, (d // 2) % 2, d % 2, m // 2, m % 2


def choose(bit, if_zero, if_one):
    return jnp.where(bit == 0, if_zero, if_one)


def ordered(bit, mine, other, axis):
    return choose(
        bit,
        jnp.concatenate([mine, other], axis=axis),
        jnp.concatenate([other, mine], axis=axis),
    )


def keep_body(held_ref, out_ref):
    out_ref[...] = held_ref[...]


class Windows:
    def __init__(self, held):
        self.held = held

    def __call__(self, *arrays):
        *given, held = lax.optimization_barrier((*arrays, self.held))
        self.held = pl.pallas_call(
            keep_body,
            out_shape=jax.ShapeDtypeStruct(held.shape, held.dtype),
            cost_estimate=pl.CostEstimate(flops=10**12, bytes_accessed=0, transcendentals=0),
        )(held)
        return given


def rest_of_ring(first):
    blocks = [first]
    for _ in range(lax.axis_size("dp") // 4 - 2):
        blocks.append(hop_ring(blocks[-1]))
    return blocks


def sum_all(value):
    ring = lax.axis_size("dp") // 4
    for step in (hop_core, hop_x, hop_low, hop_y):
        value = value + step(value)
    travel = value
    for _ in range(1, ring):
        travel = hop_ring(travel)
        value = value + travel
    return value


def norm_back(incoming, unit_rows, inverse_root, gain):
    scaled = incoming * gain
    return inverse_root * (
        scaled - unit_rows * jnp.mean(scaled * unit_rows, axis=-1, keepdims=True)
    )


VMEM_LIMIT = 56 * 2**20


def call(body, grid, in_specs, out_specs, out_shape, scratch=(), flops=0):
    return pl.pallas_call(
        body,
        grid=grid,
        in_specs=in_specs,
        out_specs=out_specs,
        out_shape=out_shape,
        scratch_shapes=list(scratch),
        compiler_params=pltpu.CompilerParams(vmem_limit_bytes=VMEM_LIMIT),
        cost_estimate=pl.CostEstimate(flops=flops, bytes_accessed=0, transcendentals=0),
    )


def shape(dims, kind):
    return jax.ShapeDtypeStruct(dims, kind)


def whole(array):
    zeros = (0,) * array.ndim
    return pl.BlockSpec(array.shape, lambda *_: zeros)


def tile_of(*dims):
    rest = (0,) * (len(dims) - 1)
    return pl.BlockSpec(dims, lambda t: (t, *rest))


def dot(left, right, left_dim, right_dim):
    return lax.dot_general(
        left, right, (((left_dim,), (right_dim,)), ((), ())), preferred_element_type=wide_type
    )


def any_spec():
    return pl.BlockSpec(memory_space=pl.ANY)


def smem_spec():
    return pl.BlockSpec(memory_space=pltpu.SMEM)


class Pieces:
    def __init__(self, blocks, places):
        self.blocks = blocks
        self.places = places
        _, self.rows, self.columns = blocks[0].shape

    def count(self):
        return 1 + len(self.blocks)

    def specs(self):
        return [smem_spec()] + [any_spec()] * len(self.blocks)

    def values(self):
        return [self.places, *self.blocks]

    def scratch(self):
        number = 2 * len(self.blocks)
        return [
            pltpu.VMEM((number * self.rows, self.columns), low_type),
            pltpu.SemaphoreType.DMA((number,)),
        ]


def load_pieces(refs, scratch):
    place_ref, *block_refs = refs
    weight_ref, sem_ref = scratch
    copies = []
    for index, block_ref in enumerate(block_refs):
        rows = block_ref.shape[1]
        for part in range(2):
            number = 2 * index + part
            start = pl.multiple_of(place_ref[number] * rows, rows & -rows)
            copies.append(
                pltpu.make_async_copy(
                    block_ref.at[part], weight_ref.at[pl.ds(start, rows)], sem_ref.at[number]
                )
            )
    for copy in copies:
        copy.start()
    for copy in copies:
        copy.wait()


def halves_body(bit_ref, weight_ref, own_ref, other_ref):
    size = own_ref.shape[1]
    for out_ref, which in ((own_ref, bit_ref[0]), (other_ref, 1 - bit_ref[0])):
        start = pl.multiple_of(which * size, size & -size)
        out_ref[...] = weight_ref[:, pl.ds(start, size)].astype(low_type)


def halves(bit, weight, layer=None):
    rows, columns = weight.shape[-2:]
    step = rows // 5
    if layer is None:
        spec = pl.BlockSpec((step, columns), lambda i: (i, 0))
    else:
        spec = pl.BlockSpec((pl.squeezed, step, columns), lambda i: (layer, i, 0))
    half = pl.BlockSpec((step, columns // 2), lambda i: (i, 0))
    return call(
        halves_body,
        (5,),
        [smem_spec(), spec],
        [half, half],
        [shape((rows, columns // 2), low_type)] * 2,
    )(bit.astype(jnp.int32).reshape(1), weight)


def pack_body(*refs):
    *parts, out_ref = refs
    start = 0
    for part in parts:
        if len(part.shape) == 2:
            out_ref[start] = part[...]
            start += 1
        else:
            out_ref[start : start + part.shape[0]] = part[...]
            start += part.shape[0]


def pack(*parts):
    rows, width = parts[0].shape[-2:]
    step = width // 4
    specs, number = [], 0
    for part in parts:
        if part.ndim == 2:
            specs.append(pl.BlockSpec((rows, step), lambda n: (0, n)))
            number += 1
        else:
            specs.append(pl.BlockSpec((part.shape[0], rows, step), lambda n: (0, 0, n)))
            number += part.shape[0]
    return call(
        pack_body,
        (4,),
        specs,
        pl.BlockSpec((number, rows, step), lambda n: (0, 0, n)),
        shape((number, rows, width), parts[0].dtype),
    )(*parts)


def both_cores(near_ref, far_ref):
    return jnp.concatenate([near_ref[0], far_ref[0]], axis=0)


def project_body(count, x_ref, xc_ref, cos_ref, sin_ref, *refs):
    pieces = refs[:count]
    at_ref, q_ref, kv_ref, g_ref, w_ref, sem_ref = refs[count:]

    @pl.when(pl.program_id(0) == 0)
    def _():
        load_pieces(pieces, (w_ref, sem_ref))
        turned = w_ref[:, 384:].astype(wide_type).T
        g_ref[...] = turned[EDGE - 384 : EDGE - 384 + 2]

    x = both_cores(x_ref, xc_ref).astype(wide_type)
    rows = x.shape[0]
    unit = x * lax.rsqrt(jnp.mean(x * x, axis=-1, keepdims=True) + eps_norm)
    normed = (unit * g_ref[0:1]).astype(low_type)
    at_ref[...] = normed.T
    flat = dot(w_ref[...], normed, 0, 1)
    cos, sin = cos_ref[0], sin_ref[0]

    def rotated(start):
        first = flat[start : start + HALF]
        second = flat[start + HALF : start + HEAD_SIZE]
        return jnp.concatenate(
            [first * cos - second * sin, second * cos + first * sin], axis=0
        ).astype(low_type)

    for head in range(GROUP):
        q_ref[0, :, head * rows : (head + 1) * rows] = rotated(head * HEAD_SIZE)
    kv_ref[0] = jnp.concatenate(
        [rotated(QROWS), flat[QROWS + HEAD_SIZE : EDGE].astype(low_type)], axis=0
    )


def project(near, far, weight, cos, sin):
    tiles, per, width = near.shape
    wide = 2 * per
    return call(
        functools.partial(project_body, weight.count()),
        (tiles,),
        [
            tile_of(1, per, width),
            tile_of(1, per, width),
            tile_of(1, HALF, wide),
            tile_of(1, HALF, wide),
            *weight.specs(),
        ],
        [
            pl.BlockSpec((width, wide), lambda t: (0, t)),
            tile_of(1, HEAD_SIZE, GROUP * wide),
            tile_of(1, BOTH, wide),
            pl.BlockSpec((2, width), lambda t: (0, 0)),
        ],
        [
            shape((width, tiles * wide), low_type),
            shape((tiles, HEAD_SIZE, GROUP * wide), low_type),
            shape((tiles, BOTH, wide), low_type),
            shape((2, width), wide_type),
        ],
        weight.scratch(),
    )(near, far, cos, sin, *weight.values())


def load_keys(kv_refs, kv_ref, sem_ref):
    copies, start = [], 0
    for index, part in enumerate(kv_refs):
        size = part.shape[0]
        copies.append(
            pltpu.make_async_copy(part, kv_ref.at[start : start + size], sem_ref.at[index])
        )
        start += size
    for copy in copies:
        copy.start()
    for copy in copies:
        copy.wait()


def attend_body(count, seen_ref, base_ref, q_ref, pos_ref, start_ref, local_ref, *refs):
    kv_parts, pieces = refs[:4], refs[4 : 4 + count]
    o_ref, ot_ref, lse_ref, near_ref, far_ref = refs[4 + count : 9 + count]
    top_ref, sum_ref, acc_ref, kv_ref, kv_sem, w_ref, sem_ref = refs[9 + count :]
    tile = pl.program_id(0)
    key_tiles = kv_ref.shape[0]

    @pl.when(tile == 0)
    def _():
        load_keys(kv_parts, kv_ref, kv_sem)
        load_pieces(pieces, (w_ref, sem_ref))

    top_ref[...] = jnp.full(top_ref.shape, masked_score, wide_type)
    sum_ref[...] = jnp.zeros(sum_ref.shape, wide_type)
    acc_ref[...] = jnp.zeros(acc_ref.shape, wide_type)

    def step(k, carry):
        @pl.when(seen_ref[tile * key_tiles + k] != 0)
        def _():
            raw = dot(kv_ref[k, :HEAD_SIZE], q_ref[0], 0, 0)
            key_pos = base_ref[k] + local_ref[...]
            allowed = (key_pos <= pos_ref[0]) & (key_pos >= start_ref[0])
            raw = jnp.where(allowed, raw, masked_score)
            top_old = top_ref[...]
            top = jnp.maximum(top_old, jnp.max(raw, axis=0, keepdims=True))
            shrink = jnp.exp2((top_old - top) * EXP_SCALE)
            probs = jnp.where(allowed, jnp.exp2((raw - top) * EXP_SCALE), 0.0)
            sum_ref[...] = sum_ref[...] * shrink + jnp.sum(probs, axis=0, keepdims=True)
            acc_ref[...] = acc_ref[...] * shrink + dot(
                kv_ref[k, HEAD_SIZE:], probs.astype(low_type), 1, 0
            )
            top_ref[...] = top

        return carry

    lax.fori_loop(0, key_tiles, step, 0)
    out = acc_ref[...] / sum_ref[...]
    ot_ref[0] = out
    lse_ref[0] = top_ref[...] * EXP_SCALE + jnp.log2(sum_ref[...])
    rows = out.shape[1] // GROUP
    stacked = jnp.concatenate(
        [out[:, head * rows : (head + 1) * rows] for head in range(GROUP)], axis=0
    )
    attended = stacked.T.astype(low_type)
    o_ref[0] = attended
    branch = dot(attended, w_ref[...], 1, 1)
    near_ref[0] = branch[: rows // 2].astype(low_type)
    far_ref[0] = branch[rows // 2 :].astype(low_type)


def key_scratch(kv):
    number = sum(part.shape[0] for part in kv)
    return [
        pltpu.VMEM((number, *kv[0].shape[1:]), low_type),
        pltpu.SemaphoreType.DMA((len(kv),)),
    ]


def attend(layout, kv, weight):
    seen, base, q, pos, start, local = layout
    tiles, _, columns = q.shape
    wide = kv[0].shape[2]
    width = 2 * len(weight.blocks) * weight.rows
    return call(
        functools.partial(attend_body, weight.count()),
        (tiles,),
        [
            smem_spec(),
            smem_spec(),
            tile_of(1, HEAD_SIZE, columns),
            tile_of(1, 1, columns),
            tile_of(1, 1, columns),
            whole(local),
            *[any_spec()] * 4,
            *weight.specs(),
        ],
        [
            tile_of(1, wide, QROWS),
            tile_of(1, HEAD_SIZE, columns),
            tile_of(1, 1, columns),
            tile_of(1, wide // 2, width),
            tile_of(1, wide // 2, width),
        ],
        [
            shape((tiles, wide, QROWS), low_type),
            shape((tiles, HEAD_SIZE, columns), wide_type),
            shape((tiles, 1, columns), wide_type),
            shape((tiles, wide // 2, width), low_type),
            shape((tiles, wide // 2, width), low_type),
        ],
        [
            pltpu.VMEM((1, columns), wide_type),
            pltpu.VMEM((1, columns), wide_type),
            pltpu.VMEM((HEAD_SIZE, columns), wide_type),
            *key_scratch(kv),
            *weight.scratch(),
        ],
    )(*layout, *kv, *weight.values())


def attend_back_body(
    count, seen_ref, base_ref, q_ref, pos_ref, start_ref, local_ref,
    z_ref, zc_ref, ot_ref, lse_ref, cos_ref, sin_ref, *refs,
):
    kv_parts, pieces = refs[:4], refs[4 : 4 + count]
    dq_ref, *dkv_parts = refs[4 + count : 9 + count]
    acc_ref, dkv_ref, kv_ref, kv_sem, w_ref, sem_ref = refs[9 + count :]
    tile = pl.program_id(0)
    key_tiles = kv_ref.shape[0]

    @pl.when(tile == 0)
    def _():
        load_keys(kv_parts, kv_ref, kv_sem)
        load_pieces(pieces, (w_ref, sem_ref))
        dkv_ref[...] = jnp.zeros(dkv_ref.shape, wide_type)

    rows = q_ref.shape[2] // GROUP
    turned = dot(w_ref[...], both_cores(z_ref, zc_ref), 0, 1).astype(low_type)
    grad_out = jnp.concatenate(
        [turned[head * HEAD_SIZE : (head + 1) * HEAD_SIZE] for head in range(GROUP)], axis=1
    )
    delta = jnp.sum(grad_out.astype(wide_type) * ot_ref[0], axis=0, keepdims=True)
    acc_ref[...] = jnp.zeros(acc_ref.shape, wide_type)

    def step(k, carry):
        @pl.when(seen_ref[tile * key_tiles + k] != 0)
        def _():
            raw = dot(kv_ref[k, :HEAD_SIZE], q_ref[0], 0, 0)
            key_pos = base_ref[k] + local_ref[...]
            allowed = (key_pos <= pos_ref[0]) & (key_pos >= start_ref[0])
            probs = jnp.where(allowed, jnp.exp2(raw * EXP_SCALE - lse_ref[0]), 0.0)
            grad_probs = dot(kv_ref[k, HEAD_SIZE:], grad_out, 0, 0)
            grad_scores = (probs * (grad_probs - delta)).astype(low_type)
            acc_ref[...] += dot(kv_ref[k, :HEAD_SIZE], grad_scores, 1, 0)
            dkv_ref[k, :HEAD_SIZE] += dot(q_ref[0], grad_scores, 1, 1) * SCALE
            dkv_ref[k, HEAD_SIZE:] += dot(grad_out, probs.astype(low_type), 1, 1)

        return carry

    lax.fori_loop(0, key_tiles, step, 0)
    cos, sin = cos_ref[0], sin_ref[0]
    for head in range(GROUP):
        part = acc_ref[:, head * rows : (head + 1) * rows] * SCALE
        first, second = part[:HALF], part[HALF:]
        dq_ref[0, head * HEAD_SIZE : (head + 1) * HEAD_SIZE] = jnp.concatenate(
            [first * cos + second * sin, second * cos - first * sin], axis=0
        ).astype(low_type)

    @pl.when(tile == pl.num_programs(0) - 1)
    def _():
        start = 0
        for part in dkv_parts:
            size = part.shape[0]
            part[...] = dkv_ref[start : start + size].astype(part.dtype)
            start += size


def attend_back(layout, kv, weight, near, far, out_turned, lse, cos, sin):
    seen, base, q, pos, start, local = layout
    tiles, _, columns = q.shape
    wide = kv[0].shape[2]
    width = near.shape[2]
    kinds = (wide_type, low_type, low_type, low_type)
    held = key_scratch(kv)
    return call(
        functools.partial(attend_back_body, weight.count()),
        (tiles,),
        [
            smem_spec(),
            smem_spec(),
            tile_of(1, HEAD_SIZE, columns),
            tile_of(1, 1, columns),
            tile_of(1, 1, columns),
            whole(local),
            tile_of(1, wide // 2, width),
            tile_of(1, wide // 2, width),
            tile_of(1, HEAD_SIZE, columns),
            tile_of(1, 1, columns),
            tile_of(1, HALF, wide),
            tile_of(1, HALF, wide),
            *[any_spec()] * 4,
            *weight.specs(),
        ],
        [tile_of(1, QROWS, wide)] + [whole(part) for part in kv],
        [shape((tiles, QROWS, wide), low_type)]
        + [shape(part.shape, kind) for part, kind in zip(kv, kinds)],
        [
            pltpu.VMEM((HEAD_SIZE, columns), wide_type),
            pltpu.VMEM(held[0].shape, wide_type),
            *held,
            *weight.scratch(),
        ],
    )(*layout, near, far, out_turned, lse, cos, sin, *kv, *weight.values())


def finish_body(late_ref, dq_ref, own_ref, y_ref, a_ref, b_ref, cos_ref, sin_ref, out_ref):
    late = (pl.program_id(0) // 2 == late_ref[0]).astype(wide_type)
    total = own_ref[0] + y_ref[0].astype(wide_type)
    total = total + late * (a_ref[0].astype(wide_type) + b_ref[0].astype(wide_type))
    cos, sin = cos_ref[0], sin_ref[0]
    first, second = total[:HALF], total[HALF:HEAD_SIZE]
    turned = jnp.concatenate(
        [
            dq_ref[0].astype(wide_type),
            first * cos + second * sin,
            second * cos - first * sin,
            total[HEAD_SIZE:],
            jnp.zeros((2, total.shape[1]), wide_type),
        ],
        axis=0,
    )
    out_ref[0] = turned.T.astype(low_type)


def finish(late, dq, own, from_y, from_a, from_b, cos, sin):
    tiles, _, wide = dq.shape
    return call(
        finish_body,
        (tiles,),
        [
            smem_spec(),
            tile_of(1, QROWS, wide),
            tile_of(1, BOTH, wide),
            tile_of(1, BOTH, wide),
            pl.BlockSpec((1, BOTH, wide), lambda t: (t % 2, 0, 0)),
            pl.BlockSpec((1, BOTH, wide), lambda t: (t % 2, 0, 0)),
            tile_of(1, HALF, wide),
            tile_of(1, HALF, wide),
        ],
        tile_of(1, wide, EDGE + 2),
        shape((tiles, wide, EDGE + 2), low_type),
    )(late, dq, own, from_y, from_a, from_b, cos, sin)


def turn_body(near_ref, far_ref, out_ref):
    out_ref[...] = both_cores(near_ref, far_ref).T


def turn(near, far):
    tiles, per, width = near.shape
    return call(
        turn_body,
        (tiles,),
        [tile_of(1, per, width), tile_of(1, per, width)],
        pl.BlockSpec((width, 2 * per), lambda t: (0, t)),
        shape((width, 2 * per * tiles), low_type),
    )(near, far)


def ffn_body(count, near_ref, far_ref, *refs):
    gate_pieces, up_pieces = refs[:count], refs[count : 2 * count]
    at_ref, hid_ref, one_ref, two_ref, gate_ref, gate_sem, up_ref, up_sem = refs[2 * count :]

    @pl.when(pl.program_id(0) == 0)
    def _():
        load_pieces(gate_pieces, (gate_ref, gate_sem))
        load_pieces(up_pieces, (up_ref, up_sem))

    normed = both_cores(near_ref, far_ref)
    at_ref[...] = normed.T
    gate = dot(normed, gate_ref[...], 1, 0)
    upward = dot(normed, up_ref[...], 1, 0)
    sigma = 1.0 / (1.0 + jnp.exp(-gate))
    passed = gate * sigma
    hid_ref[0] = (passed * upward).astype(low_type)
    one_ref[0] = upward * sigma * (1.0 + gate * (1.0 - sigma))
    two_ref[0] = passed


def ffn(near, far, gate_weight, up_weight):
    tiles, per, width = near.shape
    wide = 2 * per
    hidden = gate_weight.columns
    return call(
        functools.partial(ffn_body, gate_weight.count()),
        (tiles,),
        [
            tile_of(1, per, width),
            tile_of(1, per, width),
            *gate_weight.specs(),
            *up_weight.specs(),
        ],
        [
            pl.BlockSpec((width, wide), lambda t: (0, t)),
            tile_of(1, wide, hidden),
            tile_of(1, wide, hidden),
            tile_of(1, wide, hidden),
        ],
        [
            shape((width, tiles * wide), low_type),
            shape((tiles, wide, hidden), low_type),
            shape((tiles, wide, hidden), wide_type),
            shape((tiles, wide, hidden), wide_type),
        ],
        gate_weight.scratch() + up_weight.scratch(),
    )(near, far, *gate_weight.values(), *up_weight.values())


def ffn_back_body(count, near_ref, far_ref, one_ref, two_ref, *refs):
    dgate_ref, dup_ref, w_ref, sem_ref = refs[count:]

    @pl.when(pl.program_id(0) == 0)
    def _():
        load_pieces(refs[:count], (w_ref, sem_ref))

    grad_hidden = dot(both_cores(near_ref, far_ref), w_ref[...], 1, 0)
    dgate_ref[0] = (grad_hidden * one_ref[0]).astype(low_type)
    dup_ref[0] = (grad_hidden * two_ref[0]).astype(low_type)


def ffn_back(near, far, weight, one, two):
    tiles, per, width = near.shape
    wide = 2 * per
    hidden = weight.columns
    part = tile_of(1, wide, hidden)
    return call(
        functools.partial(ffn_back_body, weight.count()),
        (tiles,),
        [tile_of(1, per, width), tile_of(1, per, width), part, part, *weight.specs()],
        [part, part],
        [shape((tiles, wide, hidden), low_type)] * 2,
        weight.scratch(),
    )(near, far, one, two, *weight.values())


def put_blocks(total, out_refs):
    for index, out_ref in enumerate(out_refs):
        out_ref[...] = total[index].astype(out_ref.dtype)


def block_outputs(per, width, step):
    spec = pl.BlockSpec((per, step), lambda n: (0, n))
    kinds = (wide_type, low_type, low_type, low_type)
    return [spec] * 4, [shape((per, width), kind) for kind in kinds]


def combine_body(near_ref, got_ref, *out_refs):
    put_blocks(near_ref[...].astype(wide_type) + got_ref[...].astype(wide_type), out_refs)


def combine(near, got):
    blocks, per, width = near.shape
    step = 512
    spec = pl.BlockSpec((blocks, per, step), lambda n: (0, 0, n))
    out_specs, out_shape = block_outputs(per, width, step)
    return call(combine_body, (width // step,), [spec, spec], out_specs, out_shape)(near, got)


def branch_body(lefts, count, with_got, *refs):
    left_refs, refs = refs[:lefts], refs[lefts:]
    pieces, refs = [refs[i * count : (i + 1) * count] for i in range(lefts)], refs[lefts * count :]
    got_ref, refs = (refs[0], refs[1:]) if with_got else (None, refs)
    outs, scratch = refs[: -2 * lefts], refs[-2 * lefts :]
    step = outs[0].shape[-1]

    @pl.when(pl.program_id(0) == 0)
    def _():
        for index in range(lefts):
            load_pieces(pieces[index], scratch[2 * index : 2 * index + 2])

    start = pl.multiple_of(pl.program_id(0) * step, step)
    total = None
    for index in range(lefts):
        left = left_refs[index][...]
        rows = left.shape[0] * left.shape[2]
        weight = scratch[2 * index][pl.ds(start, step), :]
        term = dot(left.reshape(rows, left.shape[3]), weight, 1, 1)
        total = term if total is None else total + term
    total = total.reshape(4, total.shape[0] // 4, step)
    if got_ref is None:
        outs[0][...] = total.astype(low_type)
    else:
        put_blocks(total + got_ref[...].astype(wide_type), outs)


def branch(pairs, core, got=None):
    step = 512
    specs, lefts, weight_specs, weights, scratch = [], [], [], [], []
    for left, weight in pairs:
        tiles, wide, inner = left.shape
        lefts.append(left.reshape(tiles, 2, wide // 2, inner))
        specs.append(pl.BlockSpec((tiles, 1, wide // 2, inner), lambda n: (0, core, 0, 0)))
        weight_specs += weight.specs()
        weights += weight.values()
        scratch += weight.scratch()
    width = 2 * len(weight.blocks) * weight.rows
    per = wide // 2
    block = pl.BlockSpec((tiles, per, step), lambda n: (0, 0, n))
    if got is None:
        out_specs, out_shape = [block], [shape((tiles, per, width), low_type)]
    else:
        out_specs, out_shape = block_outputs(per, width, step)
    outs = call(
        functools.partial(branch_body, len(pairs), weight.count(), got is not None),
        (width // step,),
        specs + weight_specs + ([] if got is None else [block]),
        out_specs,
        out_shape,
        scratch,
    )(*lefts, *weights, *([] if got is None else [got]))
    return outs[0] if got is None else outs


def weight_body(count, index_ref, first_ref, second_ref, right_ref, *refs):
    left = jnp.concatenate([first_ref[0], second_ref[0]], axis=0)
    total = dot(left, right_ref[...], 1, 0)
    rows = total.shape[0] // 2
    for part in range(2):
        block = total[part * rows : (part + 1) * rows]
        for position in range(count):
            block = block + refs[2 * position + part][0].astype(wide_type)
        refs[-1][part] = block.astype(refs[-1].dtype)


def weight_rows(turned, right, places, addends, kind):
    tokens = turned.shape[1]
    columns = right.shape[-1]
    blocks = lax.axis_size("dp")
    rows = turned.shape[0] // blocks
    number = len(places)
    flat = [jnp.asarray(p, jnp.int32) for p in places]

    def named(offset, part, last):
        return pl.BlockSpec(
            (1, rows, last), lambda i, index: (index[offset + 2 * i + part], 0, 0)
        )

    specs = [
        named(0, 0, tokens),
        named(0, 1, tokens),
        pl.BlockSpec((tokens, columns), lambda i, index: (0, 0)),
    ]
    given = []
    for position, (array, where) in enumerate(addends):
        flat += [jnp.asarray(p, jnp.int32) for p in where]
        for part in range(2):
            specs.append(named((position + 1) * number, part, columns))
            given.append(array)
    left = turned.reshape(blocks, rows, tokens)
    return pl.pallas_call(
        functools.partial(weight_body, len(addends)),
        grid_spec=pltpu.PrefetchScalarGridSpec(
            num_scalar_prefetch=1,
            grid=(number // 2,),
            in_specs=specs,
            out_specs=pl.BlockSpec((2, rows, columns), lambda i, index: (i, 0, 0)),
        ),
        out_shape=shape((number, rows, columns), kind),
        compiler_params=pltpu.CompilerParams(vmem_limit_bytes=VMEM_LIMIT),
        cost_estimate=pl.CostEstimate(flops=0, bytes_accessed=0, transcendentals=0),
    )(jnp.stack(flat), left, left, right.reshape(tokens, columns), *given)


def share_first(turned, right):
    _, _, y, _, _ = bits()
    ring = lax.axis_size("dp") // 4
    places = [4 * g + 2 * b + (1 - y) for g in range(ring) for b in range(2)]
    return weight_rows(turned, right, places, [], low_type)


def share_term(turned, right, got, step, travel=None):
    h, l, y, _, _ = bits()
    ring = lax.axis_size("dp") // 4
    group = (h - 1 - step) % ring
    last = step == ring - 1
    order = [l, 1 - l] if last else [0, 1]
    places = [4 * group + 2 * b + y for b in order]
    addends = [(got, [2 * group + b for b in order])]
    if travel is not None:
        addends.append((travel, order))
    return weight_rows(turned, right, places, addends, wide_type if last else low_type)


def share_rest(turned, right, got, term):
    ring = lax.axis_size("dp") // 4
    travel = hop_ring(term)
    for step in range(1, ring - 1):
        travel = hop_ring(share_term(turned, right, got, step, travel))
    return travel


def share_third(turned, right, got, travel):
    ring = lax.axis_size("dp") // 4
    own = share_term(turned, right, got, ring - 1, travel)
    return own[0], own[1].astype(low_type)


def adamw(param, grad, first, second):
    first_new = beta_first * first + (1.0 - beta_first) * grad
    second_new = beta_second * second + (1.0 - beta_second) * grad * grad
    first_hat = first_new / (1.0 - beta_first**STEP)
    second_hat = second_new / (1.0 - beta_second**STEP)
    change = -learn_rate * (first_hat / (jnp.sqrt(second_hat) + adam_eps) + weight_decay * param)
    return (first_new, second_new, change)


def on_device(
    tokens,
    upstream,
    offsets,
    query_weight,
    keyval_weight,
    output_weight,
    gateup_weight,
    down_weight,
    norm_gains,
    first_query,
    first_keyval,
    first_output,
    first_gateup,
    first_down,
    first_gains,
    second_query,
    second_keyval,
    second_output,
    second_gateup,
    second_down,
    second_gains,
):
    h, l, y, xbit, cbit = bits()
    pin = Windows(norm_gains)
    ring = lax.axis_size("dp") // 4
    block_rows = offsets.shape[0]
    per, width = tokens.shape
    wide = 2 * per

    def split(bit, arrays, more=()):
        lower, upper = [], []
        for array in arrays:
            half = array.shape[-1] // 2
            lower.append(array[:, :half].astype(low_type))
            upper.append(array[:, half:].astype(low_type))
        lower = jnp.concatenate([*lower, *more], axis=1)
        upper = jnp.concatenate([*upper, *more], axis=1)
        return choose(bit, lower, upper), choose(bit, upper, lower)

    def paired(own, other):
        return ordered(l, own[None], other[None], 0)

    places = jnp.stack(
        [
            4 * ((h - step) % ring) + 2 * b + (y ^ flip)
            for step in range(ring)
            for flip in range(2)
            for b in range(2)
        ]
    ).astype(jnp.int32)

    def legs(pair, pair_y, rings, rings_y):
        blocks = [pair, pair_y]
        for block, block_y in zip(rings, rings_y):
            blocks += [block, block_y]
        return Pieces(blocks, places)

    def arrived(own, *others):
        for other in others:
            own = own + other.astype(wide_type)
        return own

    def onward(block, corner):
        return (block.astype(wide_type) + corner.astype(wide_type)).astype(low_type)

    gain_columns = norm_gains.astype(low_type).T
    q_own, q_other = split(
        l, [query_weight, keyval_weight[0], keyval_weight[1]], [gain_columns]
    )
    o_own, o_other = split(l, [output_weight])
    q_other, o_other, other_offsets = hop_low(q_other), hop_low(o_other), hop_low(offsets)

    q_other, o_other, other_offsets, bit, own_rows = pin(
        q_other, o_other, other_offsets, l, tokens
    )
    q_pair = paired(q_own, q_other)
    q_ring, q_y = hop_ring(q_pair), hop_y(q_pair)
    tx, tz = hop_x(own_rows), hop_low(own_rows)
    o_pair = paired(o_own, o_other)
    g_own, g_other = halves(bit, gateup_weight, 0)

    def relative(own):
        four = own.reshape(2, 2, per)
        four = choose(xbit, four, four[::-1])
        return choose(cbit, four, four[:, ::-1])

    offset_tiles = jnp.concatenate([relative(offsets), relative(other_offsets)], axis=0)
    offset_tiles = offset_tiles.reshape(4, wide)
    lane = jnp.arange(wide, dtype=jnp.int32)
    local = choose(cbit, lane, lane ^ per)
    mine = jnp.arange(4, dtype=jnp.int32)

    def bases(group_h, group_y, low_bits, x_bits):
        block = 4 * group_h + 2 * low_bits + group_y
        return block * block_rows + x_bits * wide

    low_bits, x_bits = l ^ (mine // 2), xbit ^ (mine % 2)
    own_base = bases(h, y, low_bits, x_bits)
    one = jnp.ones((2,), jnp.int32)
    key_base = jnp.concatenate(
        [
            own_base,
            bases(h, 1 - y, low_bits, x_bits),
            bases(h - 1, y, one, x_bits[:2]),
            bases(h - 1, 1 - y, one, x_bits[:2]),
        ]
    ).astype(jnp.int32)
    query_pos = own_base[:, None] + local[None, :]
    doc_start = query_pos - offset_tiles
    seen = (
        (key_base[None, :] <= own_base[:, None] + wide - 1)
        & (key_base[None, :] + wide - 1 >= jnp.min(doc_start, axis=1, keepdims=True))
    ).astype(jnp.int32).reshape(-1)
    spread = lambda a: jnp.tile(a, (1, GROUP)).reshape(4, 1, GROUP * wide)
    query_lanes, start_lanes = spread(query_pos), spread(doc_start)
    local_column = local.reshape(wide, 1)
    freqs = rope_base ** (-(jnp.arange(HALF).astype(wide_type) * 2.0 / HEAD_SIZE))
    angle = freqs[None, :, None] * offset_tiles.astype(wide_type)[:, None, :]
    cos, sin = jnp.cos(angle), jnp.sin(angle)

    tx, tz, g_other = pin(tx, tz, g_other)
    tf = hop_x(tz)
    g_other = hop_low(g_other)

    tf, q_y, bit, up_own = pin(tf, q_y, bit, upstream)
    near = pack(own_rows, tx, tz, tf)
    far = hop_core(near)
    u_own, u_other = halves(bit, gateup_weight, 1)

    far, q_ring, g_other, u_other, o_pair, up_own = pin(
        far, q_ring, g_other, u_other, o_pair, up_own
    )
    q_far = rest_of_ring(q_ring)
    q_far_y = [hop_y(block) for block in q_far]
    o_ring = hop_ring(o_pair)
    u_other = hop_low(u_other)
    ux = hop_x(up_own)
    g_pair = paired(g_own, g_other)

    up_own, o_pair, *q_far_y = pin(up_own, o_pair, *q_far_y)
    qkv_full = legs(q_pair, q_y, q_far, q_far_y)
    turned_one, q_turned, kv_own, gains = project(near, far, qkv_full, cos, sin)
    uz, o_y = hop_low(up_own), hop_y(o_pair)

    kv_own, o_y, o_ring, u_other, ux, bit = pin(kv_own, o_y, o_ring, u_other, ux, bit)
    late = choose(l, kv_own[2:], kv_own[:2])
    kv_a, kv_b, kv_y = to_next(late, 0), to_next(late, 1), hop_y(kv_own)
    o_far = rest_of_ring(o_ring)
    o_far_y = [hop_y(block) for block in o_far]
    d_own, d_other = halves(bit, down_weight)
    u_pair = paired(u_own, u_other)

    kv_y, kv_a, kv_b, uz, g_pair, d_other, *o_far_y = pin(
        kv_y, kv_a, kv_b, uz, g_pair, d_other, *o_far_y
    )
    g_ring, g_y = hop_ring(g_pair), hop_y(g_pair)
    d_other = hop_low(d_other)
    uf = hop_x(uz)
    output_full = legs(o_pair, o_y, o_far, o_far_y)
    layout = (seen, key_base, q_turned, query_lanes, start_lanes, local_column)
    kv = (kv_own, kv_y, kv_a, kv_b)
    attended, out_turned, lse, branch_near, branch_far = attend(layout, kv, output_full)
    z_got = hop_core(branch_far)

    z_got, g_y, uf, u_pair = pin(z_got, g_y, uf, u_pair)
    z_own, z_x, z_low, z_corner = combine(branch_near, z_got)
    zc, zx = hop_x(z_corner), hop_x(z_x)
    u_y = hop_y(u_pair)
    inputs = tokens.astype(wide_type)
    inverse_one = lax.rsqrt(jnp.mean(inputs * inputs, axis=-1, keepdims=True) + eps_norm)
    unit_one = inputs * inverse_one

    zc, g_ring, u_pair, uf = pin(zc, g_ring, u_pair, uf)
    zz = hop_low(onward(z_low, zc))
    g_far = rest_of_ring(g_ring)
    u_ring = hop_ring(u_pair)
    near_up = pack(up_own, ux, uz, uf)

    zx, zz, u_y, near_up, d_other = pin(zx, zz, u_y, near_up, d_other)
    g_far_y = [hop_y(block) for block in g_far]
    middle = inputs + arrived(z_own, zx, zz)
    inverse_two = lax.rsqrt(jnp.mean(middle * middle, axis=-1, keepdims=True) + eps_norm)
    unit_two = middle * inverse_two
    own_two = (unit_two * gains[1]).astype(low_type)
    az, ax = hop_low(own_two), hop_x(own_two)
    far_up = hop_core(near_up)
    d_pair = paired(d_own, d_other)

    ax, az, d_pair, far_up = pin(ax, az, d_pair, far_up)
    af = hop_x(az)
    d_y = hop_y(d_pair)

    af, *g_far_y = pin(af, *g_far_y)
    gate_full = legs(g_pair, g_y, g_far, g_far_y)
    near_two = pack(own_two, ax, az, af)
    far_two = hop_core(near_two)

    far_two, u_ring, d_y, d_pair = pin(far_two, u_ring, d_y, d_pair)
    u_far = rest_of_ring(u_ring)
    u_far_y = [hop_y(block) for block in u_far]
    d_ring = hop_ring(d_pair)
    turned_up = turn(near_up, far_up)

    turned_up, *u_far_y = pin(turned_up, *u_far_y)
    up_full = legs(u_pair, u_y, u_far, u_far_y)
    turned_two, hidden, first_factor, second_factor = ffn(
        near_two, far_two, gate_full, up_full
    )
    down_first = share_first(turned_up, hidden)

    d_ring, down_first = pin(d_ring, down_first)
    d_far = rest_of_ring(d_ring)
    d_far_y = [hop_y(block) for block in d_far]

    down_first, hidden, *d_far_y = pin(down_first, hidden, *d_far_y)
    down_sent = hop_y(down_first)
    down_full = legs(d_pair, d_y, d_far, d_far_y)
    grad_gate, grad_up = ffn_back(near_up, far_up, down_full, first_factor, second_factor)
    ffn_pairs = [(grad_gate, gate_full), (grad_up, up_full)]
    s_got = hop_core(branch(ffn_pairs, 1))
    gate_first = share_first(turned_two, grad_gate)

    s_got, grad_up, gate_first = pin(s_got, grad_up, gate_first)
    s_own, s_x, s_low, s_corner = branch(ffn_pairs, 0, s_got)
    sc, sx = hop_x(s_corner), hop_x(s_x)

    sc, grad_up = pin(sc, grad_up)
    sz = hop_low(onward(s_low, sc))
    up_first = share_first(turned_two, grad_up)

    sx, sz, down_got, gate_first, up_first, hidden = pin(
        sx, sz, down_sent, gate_first, up_first, hidden
    )
    grad_normed_two = arrived(s_own, sx, sz)
    gain_two = jnp.sum(grad_normed_two * unit_two, axis=0)
    grad_middle = upstream.astype(wide_type) + norm_back(
        grad_normed_two, unit_two, inverse_two, gains[1]
    )
    own_three = grad_middle.astype(low_type)
    bz, bx = hop_low(own_three), hop_x(own_three)
    gate_sent = hop_y(gate_first)
    down_travel = share_rest(
        turned_up, hidden, down_got, share_term(turned_up, hidden, down_got, 0)
    )

    bx, bz = pin(bx, bz)
    bf = hop_x(bz)

    (bf,) = pin(bf)
    near_three = pack(own_three, bx, bz, bf)
    far_three = hop_core(near_three)

    far_three, gate_got, down_travel, up_first, grad_gate = pin(
        far_three, gate_sent, down_travel, up_first, grad_gate
    )
    up_sent = hop_y(up_first)
    gate_travel = share_rest(
        turned_two, grad_gate, gate_got, share_term(turned_two, grad_gate, gate_got, 0)
    )
    dq_turned, dkv_own, dkv_y, dkv_a, dkv_b = attend_back(
        layout, kv, output_full, near_three, far_three, out_turned, lse, cos, sin
    )

    dkv_y, dkv_a, dkv_b, near_three = pin(dkv_y, dkv_a, dkv_b, near_three)
    dkv_a, dkv_b, dkv_y = to_previous(dkv_a, 0), to_previous(dkv_b, 1), hop_y(dkv_y)
    turned_three = turn(near_three, far_three)
    output_first = share_first(turned_three, attended)

    dkv_y, dkv_a, dkv_b, output_first = pin(dkv_y, dkv_a, dkv_b, output_first)
    dqkv = finish(
        (1 - l).astype(jnp.int32).reshape(1), dq_turned, dkv_own, dkv_y, dkv_a, dkv_b, cos, sin
    )
    attn_pairs = [(dqkv, qkv_full)]
    r_got = hop_core(branch(attn_pairs, 1))
    output_sent = hop_y(output_first)
    qkv_sent = hop_y(share_first(turned_one, dqkv))

    r_got, up_got, gate_travel, hidden = pin(r_got, up_sent, gate_travel, hidden)
    r_own, r_x, r_low, r_corner = branch(attn_pairs, 0, r_got)
    rc, rx = hop_x(r_corner), hop_x(r_x)
    up_travel = share_rest(
        turned_two, grad_up, up_got, share_term(turned_two, grad_up, up_got, 0)
    )

    rc, output_got, hidden = pin(rc, output_sent, hidden)
    rz = hop_low(onward(r_low, rc))
    output_term = share_term(turned_three, attended, output_got, 0)
    down_mine, down_theirs = share_third(turned_up, hidden, down_got, down_travel)

    rx, rz, qkv_got, output_term, down_theirs, hidden = pin(
        rx, rz, qkv_sent, output_term, down_theirs, hidden
    )
    output_travel = share_rest(turned_three, attended, output_got, output_term)
    qkv_travel = share_rest(
        turned_one, dqkv, qkv_got, share_term(turned_one, dqkv, qkv_got, 0)
    )
    down_other = hop_low(down_theirs)
    down_pairs = [(hidden, down_full)]
    f_got = hop_core(branch(down_pairs, 1))
    gate_mine, gate_theirs = share_third(turned_two, grad_gate, gate_got, gate_travel)
    grad_normed_one = arrived(r_own, rx, rz)
    gain_one = jnp.sum(grad_normed_one * unit_one, axis=0)
    grad_tokens = grad_middle + norm_back(grad_normed_one, unit_one, inverse_one, gains[0])

    f_got, up_travel, gate_theirs, down_other = pin(f_got, up_travel, gate_theirs, down_other)
    gate_other = hop_low(gate_theirs)
    f_own, f_x, f_low, f_corner = branch(down_pairs, 0, f_got)
    fc, fx = hop_x(f_corner), hop_x(f_x)
    up_mine, up_theirs = share_third(turned_two, grad_up, up_got, up_travel)

    output_travel, qkv_travel, up_theirs, gate_other, fc = pin(
        output_travel, qkv_travel, up_theirs, gate_other, fc
    )
    qkv_mine, qkv_theirs = share_third(turned_one, dqkv, qkv_got, qkv_travel)
    qkv_other = hop_low(qkv_theirs)
    output_mine, output_theirs = share_third(turned_three, attended, output_got, output_travel)
    output_other = hop_low(output_theirs)
    up_other = hop_low(up_theirs)
    fz = hop_low(onward(f_low, fc))
    block_out = (middle + arrived(f_own, fx, fz)).astype(low_type)

    def joined(mine, other, start, stop):
        return ordered(l, mine[:, start:stop], other[:, start:stop].astype(wide_type), 1)

    edge_one = QROWS + HEAD_SIZE
    hidden_part = down_mine.shape[1]
    grad_query = joined(qkv_mine, qkv_other, 0, QROWS)
    grad_keyval = jnp.stack(
        [
            joined(qkv_mine, qkv_other, QROWS, edge_one),
            joined(qkv_mine, qkv_other, edge_one, EDGE),
        ]
    )
    grad_output = joined(output_mine, output_other, 0, QROWS)
    grad_gateup = jnp.stack(
        [
            joined(gate_mine, gate_other, 0, hidden_part),
            joined(up_mine, up_other, 0, hidden_part),
        ]
    )
    grad_down = joined(down_mine, down_other, 0, hidden_part)
    shares = (
        down_mine, down_other, gate_mine, gate_other, up_mine, up_other,
        output_mine, output_other, qkv_mine, qkv_other,
    )
    squares = [jnp.sum(jnp.square(part.astype(wide_type))) for part in shares]
    square_row = jnp.full((1, width), functools.reduce(jnp.add, squares) / width)
    totals = sum_all(jnp.concatenate([gain_one[None], gain_two[None], square_row], axis=0))
    gain_total = totals[:2]
    grad_norm = jnp.sqrt(totals[2, 0] * width + jnp.sum(gain_total * gain_total))
    rows_owned = query_weight.shape[0]
    grad_gains = lax.dynamic_slice_in_dim(
        gain_total, lax.axis_index("dp") * rows_owned, rows_owned, 1
    )
    clipping_bound = math.sqrt(
        MODEL_WIDTH
        * (2 * QUERY_HEAD_COUNT * HEAD_SIZE + 2 * KEY_VALUE_HEADS * HEAD_SIZE + 3 * HIDDEN_UNITS)
        + 2 * MODEL_WIDTH
    )
    clip = jnp.minimum(1.0, clipping_bound / (grad_norm + 1e-06))
    params = (query_weight, keyval_weight, output_weight, gateup_weight, down_weight, pin.held)
    firsts = (first_query, first_keyval, first_output, first_gateup, first_down, first_gains)
    seconds = (second_query, second_keyval, second_output, second_gateup, second_down, second_gains)
    grads = (grad_query, grad_keyval, grad_output, grad_gateup, grad_down, grad_gains)
    states = [
        adamw(params[index], grads[index] * clip, firsts[index], seconds[index])
        for index in range(6)
    ]
    return (
        block_out,
        grad_tokens,
        grad_norm,
        *grads,
        *[state[0] for state in states],
        *[state[1] for state in states],
        *[state[2] for state in states],
    )


def solution(mesh):
    weights = (
        P("dp", "mp"),
        P(None, "dp", "mp"),
        P("dp", "mp"),
        P(None, "dp", "mp"),
        P("dp", "mp"),
        P(None, "dp"),
    )
    rows = P(("dp", "mp"), None)
    return jax.shard_map(
        on_device,
        mesh=mesh,
        in_specs=(rows, rows, P("dp"), *weights, *weights, *weights),
        out_specs=(rows, rows, P(), *weights, *weights, *weights, *weights),
        check_vma=False,
    )
```

time: 1100 us -> 870 us (0.79)
  Pallas kernels: 32.3 us -> 309 us
  waiting for transfers between devices: 499 us -> 299 us
  matrix products: 120 us -> 0 us
  local copies, waits for them, and re-layouts: 148 us -> 34.1 us
  starting transfers between devices: 133 us -> 99.6 us
  other arithmetic: 138 us -> 108 us
    pallas_call x4 -> x66, Pallas kernels: 32.3 us -> 309 us  [the longest x15 81.5 us: weight_rows(): pl.pallas_call(functools.partial(weight_body, len(addends)), grid_spec=pl...]
    ppermute x92 -> x79, waiting for transfers between devices: 499 us -> 299 us  [hop(): return lax.ppermute(block, AXES, route)]
    dot_general x29 -> x0, matrix products: 120 us -> none  [the longest x10 45.5 us: contract_last(): lax.dot_general(left_side, weight, (((1,), (1,)), ((), ())), preferred_el...]
    reshape x6 -> x0, local copies, waits for them, and re-layouts: 43.5 us -> none  [the longest x2 11.3 us: gather_weight(): return full.reshape(ring * 4 * rows, columns)]
    dynamic_update_slice x18 -> x0, local copies, waits for them, and re-layouts: 41.5 us -> none  [the longest x16 41.5 us: put(): lax.dynamic_update_slice(full, block[None, :, None], (at_h, 0, at_y, 0, 0))]
    ppermute x92 -> x79, starting transfers between devices: 133 us -> 99.6 us  [hop(): return lax.ppermute(block, AXES, route)]
    another operation x17 -> x4, other arithmetic: 29.1 us -> 1.41 us  [the longest x2 1.32 us: weight_rows(): jnp.stack(flat)]
    unnamed x252 -> x157, local copies, waits for them, and re-layouts: 29 us -> 13.4 us
  transfers between devices with their start and end apart: 92 -> 79, of which waited for: 44 -> 39; matrix products, arithmetic and copies ran while one was open for 28% -> 11% of each run, Pallas kernels for 1% -> 32%
where the time goes in v2:
time: 870 us; the launch traced here: 861 us
  Pallas kernels  309 us (36%)
  waiting for transfers between devices  299 us (34%)
  other arithmetic  108 us (12%)
  starting transfers between devices  99.6 us (11%)
  local copies, waits for them, and re-layouts  34.1 us (4%)
  between operations  11 us (1%)
    ppermute x79, waiting for transfers between devices, hop(): return lax.ppermute(block, AXES, route)  299 us
    ppermute x79, starting transfers between devices, hop(): return lax.ppermute(block, AXES, route)  99.6 us
    pallas_call x15, Pallas kernels, weight_rows(): pl.pallas_call(functools.partial(weight_body, len(addends)), grid_spec=pl...  81.5 us
    pallas_call x6, Pallas kernels, branch(): call(functools.partial(branch_body, len(pairs), weight.count(), got is no...  59.5 us
    pallas_call x29, Pallas kernels, __call__(): pl.pallas_call(keep_body, out_shape=jax.ShapeDtypeStruct(held.shape, held...  37.1 us
    mul x6, other arithmetic, adamw(): -learn_rate  27 us
    select_n x19, other arithmetic, choose(): return jnp.where(bit == 0, if_zero, if_one)  20.5 us
    pallas_call x1, Pallas kernels, ffn(): call(functools.partial(ffn_body, gate_weight.count()), (tiles,), [tile_of...  19.8 us
  transfers between devices with their start and end apart: 79, of which 39 were waited for; matrix products, arithmetic and copies ran while one was open for 11% of the time, Pallas kernels for 32%

profile of v2, /device:TPU:0, one launch (start us, length us, event | category | flops | bytes accessed | tf_op | source)
XLA Modules:
  0.0 860.8 jit_solution(6993616295598546790)
XLA Ops:
  50.6 12.8 %collective-permute-done.5.refs_3_ = bf16[128,2560]{1,0:T(8,128)(2,1)} collective-permute-done((bf16[128,2560]{1,0:T(8,128)(2,1)}, bf16[128,2560]{1,0:T(8,128)(2,1)}, u32[]{:S(2)}, u32[]{:S(2)}) %collective-permute-start.5) | collective-permute-done | bytes 655392 | tf_op jit(solution)/shard_map/ppermute | solution.py:48
  94.2 10.4 %shard_map.419 = (bf16[2560,1024]{1,0:T(8,128)(2,1)}, bf16[4,80,1024]{2,1,0:T(8,128)(2,1)}, bf16[4,160,256]{2,1,0:T(8,128)(2,1)}, f32[2,2560]{1,0:T(2,128)}) custom-call(bf16[4,128,2560]{2,1,0:T(8,128)(2,1)} %shard_map.415.x_ref, bf16[4,128,2560]{2,1,0:T(8,128)(2,1)} %collective-permute-done.7.xc_ref, f32[4,40,256]{2,1,0:T(8,128)} %get-tuple-element.488.cos_ref, ...), custom_call_target="tpu_custom_call" | custom-call | tf_op jit(solution)/shard_map/pallas_call | solution.py:335
  137.1 18.5 %shard_map.423 = (bf16[4,256,320]{2,1,0:T(8,128)(2,1)}, f32[4,80,1024]{2,1,0:T(8,128)}, f32[4,1,1024]{2,1,0:T(1,128)}, bf16[4,128,2560]{2,1,0:T(8,128)(2,1)}, bf16[4,128,2560]{2,1,0:T(8,128)(2,1)}) custom-call(s32[48]{0:T(128)} %reshape.708.seen_ref, s32[12]{0:T(128)} %get-tuple-element.458.base_ref, bf16[4,80,1024]{2,1,0:T(8,128)(2,1)} %get-tuple-element.234.q_ref, ...), custom_call_target="tpu_custom_call" | custom-call | tf_op jit(solution)/shard_map/pallas_call | solution.py:438
  157.8 15.3 %collective-permute-done.22.refs_3_ = bf16[128,2560]{1,0:T(8,128)(2,1)} collective-permute-done((bf16[128,2560]{1,0:T(8,128)(2,1)}, bf16[128,2560]{1,0:T(8,128)(2,1)}, u32[]{:S(2)}, u32[]{:S(2)}) %collective-permute-start.22) | collective-permute-done | bytes 655392 | tf_op jit(solution)/shard_map/ppermute | solution.py:48
  186.8 10.0 %collective-permute-done.24 = bf16[128,2560]{1,0:T(8,128)(2,1)} collective-permute-done((bf16[128,2560]{1,0:T(8,128)(2,1)}, bf16[128,2560]{1,0:T(8,128)(2,1)}, u32[]{:S(2)}, u32[]{:S(2)}) %collective-permute-start.24) | collective-permute-done | bytes 655392 | tf_op jit(solution)/shard_map/ppermute | solution.py:48
  211.7 11.0 %collective-permute-done.26 = bf16[128,2560]{1,0:T(8,128)(2,1)} collective-permute-done((bf16[128,2560]{1,0:T(8,128)(2,1)}, bf16[128,2560]{1,0:T(8,128)(2,1)}, u32[]{:S(2)}, u32[]{:S(2)}) %collective-permute-start.26) | collective-permute-done | bytes 655392 | tf_op jit(solution)/shard_map/ppermute | solution.py:48
  238.4 11.3 %collective-permute-done.30.refs_2_ = bf16[128,2560]{1,0:T(8,128)(2,1)} collective-permute-done((bf16[128,2560]{1,0:T(8,128)(2,1)}, bf16[128,2560]{1,0:T(8,128)(2,1)}, u32[]{:S(2)}, u32[]{:S(2)}) %collective-permute-start.30) | collective-permute-done | bytes 655392 | tf_op jit(solution)/shard_map/ppermute | solution.py:48
  257.4 9.9 %collective-permute-start.36 = (bf16[2,320,896]{2,1,0:T(8,128)(2,1)}, bf16[2,320,896]{2,1,0:T(8,128)(2,1)}, u32[]{:S(2)}, u32[]{:S(2)}) collective-permute-start(bf16[2,320,896]{2,1,0:T(8,128)(2,1)} %maximum_select_fusion.5.refs_1_.refs_2_), channel_id=1, source_target_pairs={{0,4},{1,5},{2,6},{3,7},{4,0},{5,1},{6,2},{7,3},{8,12},{9,13},{10,... | collective-permute-start | bytes 3440648 | tf_op jit(solution)/shard_map/ppermute | solution.py:48
  272.6 12.4 %collective-permute-done.36.refs_2_.refs_3_ = bf16[2,320,896]{2,1,0:T(8,128)(2,1)} collective-permute-done((bf16[2,320,896]{2,1,0:T(8,128)(2,1)}, bf16[2,320,896]{2,1,0:T(8,128)(2,1)}, u32[]{:S(2)}, u32[]{:S(2)}) %collective-permute-start.36) | collective-permute-done | bytes 1146912 | tf_op jit(solution)/shard_map/ppermute | solution.py:48
  291.1 15.8 %collective-permute-done.37.refs_9_.refs_11_ = bf16[2,320,896]{2,1,0:T(8,128)(2,1)} collective-permute-done((bf16[2,320,896]{2,1,0:T(8,128)(2,1)}, bf16[2,320,896]{2,1,0:T(8,128)(2,1)}, u32[]{:S(2)}, u32[]{:S(2)}) %collective-permute-start.37) | collective-permute-done | bytes 1146912 | tf_op jit(solution)/shard_map/ppermute | solution.py:48
  308.2 19.8 %shard_map.435 = (bf16[2560,1024]{1,0:T(8,128)(2,1)}, bf16[4,256,896]{2,1,0:T(8,128)(2,1)}, f32[4,256,896]{2,1,0:T(8,128)}, f32[4,256,896]{2,1,0:T(8,128)}) custom-call(bf16[4,128,2560]{2,1,0:T(8,128)(2,1)} %shard_map.431.near_ref, bf16[4,128,2560]{2,1,0:T(8,128)(2,1)} %collective-permute-done.34.far_ref, ...), custom_call_target="tpu_custom_call" | custom-call | tf_op jit(solution)/shard_map/pallas_call | solution.py:648
  337.7 24.0 %collective-permute-done.39.refs_4_.refs_5_ = bf16[2,320,896]{2,1,0:T(8,128)(2,1)} collective-permute-done((bf16[2,320,896]{2,1,0:T(8,128)(2,1)}, bf16[2,320,896]{2,1,0:T(8,128)(2,1)}, u32[]{:S(2)}, u32[]{:S(2)}) %collective-permute-start.39) | collective-permute-done | bytes 1146912 | tf_op jit(solution)/shard_map/ppermute | solution.py:48
  361.7 12.4 %shard_map.439 = (bf16[4,256,896]{2,1,0:T(8,128)(2,1)}, bf16[4,256,896]{2,1,0:T(8,128)(2,1)}) custom-call(bf16[4,128,2560]{2,1,0:T(8,128)(2,1)} %shard_map.427.near_ref, bf16[4,128,2560]{2,1,0:T(8,128)(2,1)} %collective-permute-done.31.far_ref, f32[4,256,896]{2,1,0:T(8,128)} %get-tuple-element.295.one_ref, f32[4,256,896]{2,1,0:T(8,128)} %get-tuple-element.296.two_ref, ...), custom_call_target="tpu_custom_call" | custom-call | tf_op jit(solution)/shard_map/pallas_call | solution.py:690
  374.1 13.6 %shard_map.440 = bf16[4,128,2560]{2,1,0:T(8,128)(2,1)} custom-call(bf16[4,2,128,896]{3,2,1,0:T(8,128)(2,1)} %bitcast.157, bf16[4,2,128,896]{3,2,1,0:T(8,128)(2,1)} %bitcast.152, s32[8]{0:T(128)} %stack.58.refs_0_.refs_4_.refs_5_.refs_2_.refs_7_.refs_1_, bf16[2,320,896]{2,1,0:T(8,128)(2,1)} %maximum_select_fusion.3.refs_1_.refs_3_, ...), custom_call_target="tpu_custom_call" | custom-call | tf_op jit(solution)/shard_map/pallas_call | solution.py:767
  397.4 13.8 %shard_map.443 = (f32[128,2560]{1,0:T(8,128)}, bf16[128,2560]{1,0:T(8,128)(2,1)}, bf16[128,2560]{1,0:T(8,128)(2,1)}, bf16[128,2560]{1,0:T(8,128)(2,1)}) custom-call(bf16[4,2,128,896]{3,2,1,0:T(8,128)(2,1)} %bitcast.159, bf16[4,2,128,896]{3,2,1,0:T(8,128)(2,1)} %bitcast.153, s32[8]{0:T(128)} %stack.58.refs_0_.refs_4_.refs_5_.refs_2_.refs_7_.refs_1_, ...), custom_call_target="tpu_custom_call" | custom-call | tf_op jit(solution)/shard_map/pallas_call | solution.py:767
  414.6 14.5 %collective-permute-done.42 = bf16[128,2560]{1,0:T(8,128)(2,1)} collective-permute-done((bf16[128,2560]{1,0:T(8,128)(2,1)}, bf16[128,2560]{1,0:T(8,128)(2,1)}, u32[]{:S(2)}, u32[]{:S(2)}) %collective-permute-start.42) | collective-permute-done | bytes 655392 | tf_op jit(solution)/shard_map/ppermute | solution.py:48
  477.0 11.7 %collective-permute-done.47.refs_3_ = bf16[128,2560]{1,0:T(8,128)(2,1)} collective-permute-done((bf16[128,2560]{1,0:T(8,128)(2,1)}, bf16[128,2560]{1,0:T(8,128)(2,1)}, u32[]{:S(2)}, u32[]{:S(2)}) %collective-permute-start.47) | collective-permute-done | bytes 655392 | tf_op jit(solution)/shard_map/ppermute | solution.py:48
  494.1 16.2 %collective-permute-done.50.refs_2_.refs_3_ = bf16[2,320,896]{2,1,0:T(8,128)(2,1)} collective-permute-done((bf16[2,320,896]{2,1,0:T(8,128)(2,1)}, bf16[2,320,896]{2,1,0:T(8,128)(2,1)}, u32[]{:S(2)}, u32[]{:S(2)}) %collective-permute-start.50) | collective-permute-done | bytes 1146912 | tf_op jit(solution)/shard_map/ppermute | solution.py:48
  519.9 19.6 %shard_map.452 = (bf16[4,320,256]{2,1,0:T(8,128)(2,1)}, f32[4,160,256]{2,1,0:T(8,128)}, bf16[4,160,256]{2,1,0:T(8,128)(2,1)}, bf16[2,160,256]{2,1,0:T(8,128)(2,1)}, bf16[2,160,256]{2,1,0:T(8,128)(2,1)}) custom-call(s32[48]{0:T(128)} %reshape.708.seen_ref, s32[12]{0:T(128)} %get-tuple-element.458.base_ref, bf16[4,80,1024]{2,1,0:T(8,128)(2,1)} %get-tuple-element.234.q_ref, ...), custom_call_target="tpu_custom_call" | custom-call | tf_op jit(solution)/shard_map/pallas_call | solution.py:539
  556.2 20.6 %collective-permute-done.52.a_ref = bf16[2,160,256]{2,1,0:T(8,128)(2,1)} collective-permute-done((bf16[2,160,256]{2,1,0:T(8,128)(2,1)}, bf16[2,160,256]{2,1,0:T(8,128)(2,1)}, u32[]{:S(2)}, u32[]{:S(2)}) %collective-permute-start.52) | collective-permute-done | bytes 163872 | tf_op jit(solution)/shard_map/ppermute | solution.py:48
  657.1 11.4 %collective-permute-done.60 = bf16[128,2560]{1,0:T(8,128)(2,1)} collective-permute-done((bf16[128,2560]{1,0:T(8,128)(2,1)}, bf16[128,2560]{1,0:T(8,128)(2,1)}, u32[]{:S(2)}, u32[]{:S(2)}) %collective-permute-start.60) | collective-permute-done | bytes 655392 | tf_op jit(solution)/shard_map/ppermute | solution.py:48
  698.3 9.5 %shard_map.471 = (f32[128,2560]{1,0:T(8,128)}, bf16[128,2560]{1,0:T(8,128)(2,1)}, bf16[128,2560]{1,0:T(8,128)(2,1)}, bf16[128,2560]{1,0:T(8,128)(2,1)}) custom-call(bf16[4,2,128,896]{3,2,1,0:T(8,128)(2,1)} %bitcast.151, s32[8]{0:T(128)} %stack.58.refs_0_.refs_4_.refs_5_.refs_2_.refs_7_.refs_1_, bf16[2,320,896]{2,1,0:T(8,128)(2,1)} %maximum_select_fusion.5.refs_1_.refs_2_, ...), custom_call_target="tpu_custom_call" | custom-call | tf_op jit(solution)/shard_map/pallas_call | solution.py:767
  736.1 12.0 %collective-permute-done.68 = bf16[320,896]{1,0:T(8,128)(2,1)} collective-permute-done((bf16[320,896]{1,0:T(8,128)(2,1)}, bf16[320,896]{1,0:T(8,128)(2,1)}, u32[]{:S(2)}, u32[]{:S(2)}) %collective-permute-start.68) | collective-permute-done | bytes 573472 | tf_op jit(solution)/shard_map/ppermute | solution.py:48
  842.8 10.6 %add_multiply_fusion = (f32[2,320,1792]{2,1,0:T(8,128)}, f32[2,320,1792]{2,1,0:T(8,128)}, f32[2,320,1792]{2,1,0:T(8,128)}, f32[2,320,1792]{2,1,0:T(8,128)}) fusion(f32[2,320,1792]{2,1,0:T(8,128)S(1)} %bitcast.163, f32[]{:T(128)S(6)} %min_shard_map.3, f32[2,320,1792]{2,1,0:T(8,128)} %param.39, f32[2,320,1792]{2,1,0:T(8,128)} %param.33, ...), kind=kLoop, calls=%fused_computation.3 | loop fusion | flops 18350080 | bytes 36700164 | tf_op jit(solution)/shard_map/mul | solution.py:867
  (466 shorter events, 512.7 us)
Async XLA Ops:
  25.4 47.4 %collective-permute-start.8 = (bf16[2,320,482]{2,1,0:T(8,128)(2,1)}, bf16[2,320,482]{2,1,0:T(8,128)(2,1)}, u32[]{:S(2)}, u32[]{:S(2)}) collective-permute-start(bf16[2,320,482]{2,1,0:T(8,128)(2,1)} %maximum_select_fusion.8.refs_1_.refs_2_), channel_id=1, source_target_pairs={{0,16},{1,17},{2,18},{3,19},{4,20},{5,21},{6,22},{7,23},{8,24},{9,... | collective-permute-start | bytes 1850888 | tf_op jit(solution)/shard_map/ppermute | solution.py:48
  134.6 38.6 %collective-permute-start.21 = (bf16[2,320,896]{2,1,0:T(8,128)(2,1)}, bf16[2,320,896]{2,1,0:T(8,128)(2,1)}, u32[]{:S(2)}, u32[]{:S(2)}) collective-permute-start(bf16[2,320,896]{2,1,0:T(8,128)(2,1)} %maximum_select_fusion.3.refs_1_.refs_3_), channel_id=1, source_target_pairs={{0,4},{1,5},{2,6},{3,7},{4,0},{5,1},{6,2},{7,3},{8,12},{9,13},{10,... | collective-permute-start | bytes 3440648 | tf_op jit(solution)/shard_map/ppermute | solution.py:48
  136.1 50.8 %collective-permute-start.25 = (bf16[2,320,896]{2,1,0:T(8,128)(2,1)}, bf16[2,320,896]{2,1,0:T(8,128)(2,1)}, u32[]{:S(2)}, u32[]{:S(2)}) collective-permute-start(bf16[2,320,896]{2,1,0:T(8,128)(2,1)} %maximum_select_fusion.3.refs_1_.refs_3_), channel_id=1, source_target_pairs={{0,16},{1,17},{2,18},{3,19},{4,20},{5,21},{6,22},{7,23},{8,24},{9,... | collective-permute-start | bytes 3440648 | tf_op jit(solution)/shard_map/ppermute | solution.py:48
  157.6 49.9 %collective-permute-start.28 = (bf16[320,896]{1,0:T(8,128)(2,1)}, bf16[320,896]{1,0:T(8,128)(2,1)}, u32[]{:S(2)}, u32[]{:S(2)}) collective-permute-start(bf16[320,896]{1,0:T(8,128)(2,1)} %get-tuple-element.270), channel_id=1, source_target_pairs={{0,8},{1,9},{2,10},{3,11},{4,12},{5,13},{6,14},{7,15},{8,0},{9,1},... | collective-permute-start | bytes 1720328 | tf_op jit(solution)/shard_map/ppermute | solution.py:48
  200.4 66.8 %collective-permute-start.33 = (bf16[2,320,896]{2,1,0:T(8,128)(2,1)}, bf16[2,320,896]{2,1,0:T(8,128)(2,1)}, u32[]{:S(2)}, u32[]{:S(2)}) collective-permute-start(bf16[2,320,896]{2,1,0:T(8,128)(2,1)} %collective-permute-done.25.refs_3_.refs_5_), channel_id=1, source_target_pairs={{0,4},{1,5},{2,6},{3,7},{4,0},{5,1},{6,2},{7,3},{8,12},{9,13},{10,... | collective-permute-start | bytes 3440648 | tf_op jit(solution)/shard_map/ppermute | solution.py:48
  207.5 65.1 %collective-permute-start.35 = (bf16[2,320,896]{2,1,0:T(8,128)(2,1)}, bf16[2,320,896]{2,1,0:T(8,128)(2,1)}, u32[]{:S(2)}, u32[]{:S(2)}) collective-permute-start(bf16[2,320,896]{2,1,0:T(8,128)(2,1)} %maximum_select_fusion.4.refs_6_.refs_8_), channel_id=1, source_target_pairs={{0,16},{1,17},{2,18},{3,19},{4,20},{5,21},{6,22},{7,23},{8,24},{9,... | collective-permute-start | bytes 3440648 | tf_op jit(solution)/shard_map/ppermute | solution.py:48
  288.0 46.7 %collective-permute-start.38 = (bf16[2,320,896]{2,1,0:T(8,128)(2,1)}, bf16[2,320,896]{2,1,0:T(8,128)(2,1)}, u32[]{:S(2)}, u32[]{:S(2)}) collective-permute-start(bf16[2,320,896]{2,1,0:T(8,128)(2,1)} %maximum_select_fusion.5.refs_1_.refs_2_), channel_id=1, source_target_pairs={{0,16},{1,17},{2,18},{3,19},{4,20},{5,21},{6,22},{7,23},{8,24},{9,... | collective-permute-start | bytes 3440648 | tf_op jit(solution)/shard_map/ppermute | solution.py:48
  389.1 52.6 %collective-permute-start.44 = (bf16[4,320,896]{2,1,0:T(8,128)(2,1)}, bf16[4,320,896]{2,1,0:T(8,128)(2,1)}, u32[]{:S(2)}, u32[]{:S(2)}) collective-permute-start(bf16[4,320,896]{2,1,0:T(8,128)(2,1)} %shard_map.436), channel_id=1, source_target_pairs={{0,4},{1,5},{2,6},{3,7},{4,0},{5,1},{6,2},{7,3},{8,12},{9,13},{10,... | collective-permute-start | bytes 6881288 | tf_op jit(solution)/shard_map/ppermute | solution.py:48
  459.7 50.5 %collective-permute-start.50 = (bf16[2,320,896]{2,1,0:T(8,128)(2,1)}, bf16[2,320,896]{2,1,0:T(8,128)(2,1)}, u32[]{:S(2)}, u32[]{:S(2)}) collective-permute-start(bf16[2,320,896]{2,1,0:T(8,128)(2,1)} %shard_map.450), channel_id=1, source_target_pairs={{0,16},{1,17},{2,18},{3,19},{4,20},{5,21},{6,22},{7,23},{8,24},{9,... | collective-permute-start | bytes 3440648 | tf_op jit(solution)/shard_map/ppermute | solution.py:48
  462.0 49.0 %collective-permute-start.49 = (bf16[4,320,896]{2,1,0:T(8,128)(2,1)}, bf16[4,320,896]{2,1,0:T(8,128)(2,1)}, u32[]{:S(2)}, u32[]{:S(2)}) collective-permute-start(bf16[4,320,896]{2,1,0:T(8,128)(2,1)} %shard_map.441), channel_id=1, source_target_pairs={{0,4},{1,5},{2,6},{3,7},{4,0},{5,1},{6,2},{7,3},{8,12},{9,13},{10,... | collective-permute-start | bytes 6881288 | tf_op jit(solution)/shard_map/ppermute | solution.py:48
  516.3 81.5 %collective-permute-start.56 = (bf16[2,320,896]{2,1,0:T(8,128)(2,1)}, bf16[2,320,896]{2,1,0:T(8,128)(2,1)}, u32[]{:S(2)}, u32[]{:S(2)}) collective-permute-start(bf16[2,320,896]{2,1,0:T(8,128)(2,1)} %shard_map.459), channel_id=1, source_target_pairs={{0,16},{1,17},{2,18},{3,19},{4,20},{5,21},{6,22},{7,23},{8,24},{9,... | collective-permute-start | bytes 3440648 | tf_op jit(solution)/shard_map/ppermute | solution.py:48
  539.5 37.4 %collective-permute-start.51 = (bf16[4,160,256]{2,1,0:T(8,128)(2,1)}, bf16[4,160,256]{2,1,0:T(8,128)(2,1)}, u32[]{:S(2)}, u32[]{:S(2)}) collective-permute-start(bf16[4,160,256]{2,1,0:T(8,128)(2,1)} %get-tuple-element.344), channel_id=1, source_target_pairs={{0,4},{1,5},{2,6},{3,7},{4,0},{5,1},{6,2},{7,3},{8,12},{9,13},{10,... | collective-permute-start | bytes 983048 | tf_op jit(solution)/shard_map/ppermute | solution.py:48
  541.1 35.7 %collective-permute-start.52 = (bf16[2,160,256]{2,1,0:T(8,128)(2,1)}, bf16[2,160,256]{2,1,0:T(8,128)(2,1)}, u32[]{:S(2)}, u32[]{:S(2)}) collective-permute-start(bf16[2,160,256]{2,1,0:T(8,128)(2,1)} %get-tuple-element.345), channel_id=1, source_target_pairs={{16,0},{17,1},{18,2},{19,3},{20,4},{21,5},{22,6},{23,7},{24,8},{25... | collective-permute-start | bytes 491528 | tf_op jit(solution)/shard_map/ppermute | solution.py:48
  542.4 34.5 %collective-permute-start.53 = (bf16[2,160,256]{2,1,0:T(8,128)(2,1)}, bf16[2,160,256]{2,1,0:T(8,128)(2,1)}, u32[]{:S(2)}, u32[]{:S(2)}) collective-permute-start(bf16[2,160,256]{2,1,0:T(8,128)(2,1)} %get-tuple-element.346), channel_id=1, source_target_pairs={{16,4},{17,5},{18,6},{19,7},{24,12},{25,13},{26,14},{27,15}} | collective-permute-start | bytes 491528 | tf_op jit(solution)/shard_map/ppermute | solution.py:48
  551.0 54.6 %collective-permute-start.55 = (bf16[4,320,896]{2,1,0:T(8,128)(2,1)}, bf16[4,320,896]{2,1,0:T(8,128)(2,1)}, u32[]{:S(2)}, u32[]{:S(2)}) collective-permute-start(bf16[4,320,896]{2,1,0:T(8,128)(2,1)} %shard_map.445), channel_id=1, source_target_pairs={{0,4},{1,5},{2,6},{3,7},{4,0},{5,1},{6,2},{7,3},{8,12},{9,13},{10,... | collective-permute-start | bytes 6881288 | tf_op jit(solution)/shard_map/ppermute | solution.py:48
  588.8 48.0 %collective-permute-start.59 = (bf16[4,320,320]{2,1,0:T(8,128)(2,1)}, bf16[4,320,320]{2,1,0:T(8,128)(2,1)}, u32[]{:S(2)}, u32[]{:S(2)}) collective-permute-start(bf16[4,320,320]{2,1,0:T(8,128)(2,1)} %shard_map.455), channel_id=1, source_target_pairs={{0,4},{1,5},{2,6},{3,7},{4,0},{5,1},{6,2},{7,3},{8,12},{9,13},{10,... | collective-permute-start | bytes 2457608 | tf_op jit(solution)/shard_map/ppermute | solution.py:48
  597.8 59.3 %collective-permute-start.61 = (bf16[4,320,482]{2,1,0:T(8,128)(2,1)}, bf16[4,320,482]{2,1,0:T(8,128)(2,1)}, u32[]{:S(2)}, u32[]{:S(2)}) collective-permute-start(bf16[4,320,482]{2,1,0:T(8,128)(2,1)} %shard_map.463), channel_id=1, source_target_pairs={{0,4},{1,5},{2,6},{3,7},{4,0},{5,1},{6,2},{7,3},{8,12},{9,13},{10,... | collective-permute-start | bytes 3701768 | tf_op jit(solution)/shard_map/ppermute | solution.py:48
  611.0 80.3 %collective-permute-start.63 = (bf16[2,320,896]{2,1,0:T(8,128)(2,1)}, bf16[2,320,896]{2,1,0:T(8,128)(2,1)}, u32[]{:S(2)}, u32[]{:S(2)}) collective-permute-start(bf16[2,320,896]{2,1,0:T(8,128)(2,1)} %shard_map.468), channel_id=1, source_target_pairs={{0,16},{1,17},{2,18},{3,19},{4,20},{5,21},{6,22},{7,23},{8,24},{9,... | collective-permute-start | bytes 3440648 | tf_op jit(solution)/shard_map/ppermute | solution.py:48
  682.6 53.6 %collective-permute-start.67 = (bf16[2,320,482]{2,1,0:T(8,128)(2,1)}, bf16[2,320,482]{2,1,0:T(8,128)(2,1)}, u32[]{:S(2)}, u32[]{:S(2)}) collective-permute-start(bf16[2,320,482]{2,1,0:T(8,128)(2,1)} %shard_map.472), channel_id=1, source_target_pairs={{0,16},{1,17},{2,18},{3,19},{4,20},{5,21},{6,22},{7,23},{8,24},{9,... | collective-permute-start | bytes 1850888 | tf_op jit(solution)/shard_map/ppermute | solution.py:48
  684.6 51.5 %collective-permute-start.66 = (bf16[2,320,320]{2,1,0:T(8,128)(2,1)}, bf16[2,320,320]{2,1,0:T(8,128)(2,1)}, u32[]{:S(2)}, u32[]{:S(2)}) collective-permute-start(bf16[2,320,320]{2,1,0:T(8,128)(2,1)} %shard_map.464), channel_id=1, source_target_pairs={{0,16},{1,17},{2,18},{3,19},{4,20},{5,21},{6,22},{7,23},{8,24},{9,... | collective-permute-start | bytes 1228808 | tf_op jit(solution)/shard_map/ppermute | solution.py:48
  707.8 40.3 %collective-permute-start.69 = (bf16[128,2560]{1,0:T(8,128)(2,1)}, bf16[128,2560]{1,0:T(8,128)(2,1)}, u32[]{:S(2)}, u32[]{:S(2)}) collective-permute-start(bf16[128,2560]{1,0:T(8,128)(2,1)} %get-tuple-element.383), channel_id=1, source_target_pairs={{0,2},{1,3},{2,0},{3,1},{4,6},{5,7},{6,4},{7,5},{8,10},{9,11},{10,... | collective-permute-start | bytes 1966088 | tf_op jit(solution)/shard_map/ppermute | solution.py:48
  714.6 33.5 %collective-permute-start.68 = (bf16[320,896]{1,0:T(8,128)(2,1)}, bf16[320,896]{1,0:T(8,128)(2,1)}, u32[]{:S(2)}, u32[]{:S(2)}) collective-permute-start(bf16[320,896]{1,0:T(8,128)(2,1)} %fusion.17), channel_id=1, source_target_pairs={{0,8},{1,9},{2,10},{3,11},{4,12},{5,13},{6,14},{7,15},{8,0},{9,1},... | collective-permute-start | bytes 1720328 | tf_op jit(solution)/shard_map/ppermute | solution.py:48
  718.2 98.8 %collective-permute-start.65 = (bf16[128,2560]{1,0:T(8,128)(2,1)}, bf16[128,2560]{1,0:T(8,128)(2,1)}, u32[]{:S(2)}, u32[]{:S(2)}) collective-permute-start(bf16[128,2560]{1,0:T(8,128)(2,1)} %get-tuple-element.377), channel_id=1, source_target_pairs={{0,2},{1,3},{2,0},{3,1},{4,6},{5,7},{6,4},{7,5},{8,10},{9,11},{10,... | collective-permute-start | bytes 1966088 | tf_op jit(solution)/shard_map/ppermute | solution.py:48
  776.0 41.0 %collective-permute-start.70 = (bf16[128,2560]{1,0:T(8,128)(2,1)S(1)}, bf16[128,2560]{1,0:T(8,128)(2,1)S(1)}, u32[]{:S(2)}, u32[]{:S(2)}) collective-permute-start(bf16[128,2560]{1,0:T(8,128)(2,1)S(1)} %add_convert_fusion.1), channel_id=1, source_target_pairs={{0,8},{1,9},{2,10},{3,11},{4,12},{5,13},{6,14},{7,15},{8,0},{9,1},... | collective-permute-start | bytes 1966088 | tf_op jit(solution)/shard_map/ppermute | solution.py:48
  (131 other events, 1519.5 us)

commit v3 on v2

--- a/solution.py
+++ b/solution.py
@@ -124,6 +124,10 @@
         )(held)
         return given
 
+    def apart(self, *arrays):
+        self.held = hop_core(self.held)
+        return self(*arrays)
+
 
 def rest_of_ring(first):
     blocks = [first]
@@ -132,9 +136,9 @@
     return blocks
 
 
-def sum_all(value):
+def sum_rest(value):
     ring = lax.axis_size("dp") // 4
-    for step in (hop_core, hop_x, hop_low, hop_y):
+    for step in (hop_low, hop_y):
         value = value + step(value)
     travel = value
     for _ in range(1, ring):
@@ -153,7 +157,7 @@
 VMEM_LIMIT = 56 * 2**20
 
 
-def call(body, grid, in_specs, out_specs, out_shape, scratch=(), flops=0):
+def call(body, grid, in_specs, out_specs, out_shape, scratch=(), flops=10**10):
     return pl.pallas_call(
         body,
         grid=grid,
@@ -821,7 +825,7 @@
         ),
         out_shape=shape((number, rows, columns), kind),
         compiler_params=pltpu.CompilerParams(vmem_limit_bytes=VMEM_LIMIT),
-        cost_estimate=pl.CostEstimate(flops=0, bytes_accessed=0, transcendentals=0),
+        cost_estimate=pl.CostEstimate(flops=10**10, bytes_accessed=0, transcendentals=0),
     )(jnp.stack(flat), left, left, right.reshape(tokens, columns), *given)
 
 
@@ -856,7 +860,7 @@
 def share_third(turned, right, got, travel):
     ring = lax.axis_size("dp") // 4
     own = share_term(turned, right, got, ring - 1, travel)
-    return own[0], own[1].astype(low_type)
+    return own[0], own[1].astype(low_type), jnp.sum(jnp.square(own))
 
 
 def adamw(param, grad, first, second):
@@ -998,8 +1002,8 @@
     far = hop_core(near)
     u_own, u_other = halves(bit, gateup_weight, 1)
 
-    far, q_ring, g_other, u_other, o_pair, up_own = pin(
-        far, q_ring, g_other, u_other, o_pair, up_own
+    far, q_ring, g_other, u_other, o_pair, up_own, bit = pin(
+        far, q_ring, g_other, u_other, o_pair, up_own, bit
     )
     q_far = rest_of_ring(q_ring)
     q_far_y = [hop_y(block) for block in q_far]
@@ -1007,81 +1011,80 @@
     u_other = hop_low(u_other)
     ux = hop_x(up_own)
     g_pair = paired(g_own, g_other)
-
-    up_own, o_pair, *q_far_y = pin(up_own, o_pair, *q_far_y)
+    d_own, d_other = halves(bit, down_weight)
+
+    d_other, o_pair, *q_far_y = pin(d_other, o_pair, *q_far_y)
     qkv_full = legs(q_pair, q_y, q_far, q_far_y)
     turned_one, q_turned, kv_own, gains = project(near, far, qkv_full, cos, sin)
-    uz, o_y = hop_low(up_own), hop_y(o_pair)
-
-    kv_own, o_y, o_ring, u_other, ux, bit = pin(kv_own, o_y, o_ring, u_other, ux, bit)
+    d_other, o_y = hop_low(d_other), hop_y(o_pair)
+
+    kv_own, o_y, o_ring, u_other, ux = pin(kv_own, o_y, o_ring, u_other, ux)
     late = choose(l, kv_own[2:], kv_own[:2])
     kv_a, kv_b, kv_y = to_next(late, 0), to_next(late, 1), hop_y(kv_own)
     o_far = rest_of_ring(o_ring)
     o_far_y = [hop_y(block) for block in o_far]
-    d_own, d_other = halves(bit, down_weight)
     u_pair = paired(u_own, u_other)
 
-    kv_y, kv_a, kv_b, uz, g_pair, d_other, *o_far_y = pin(
-        kv_y, kv_a, kv_b, uz, g_pair, d_other, *o_far_y
+    kv_y, kv_a, kv_b, g_pair, up_own, d_other, *o_far_y = pin(
+        kv_y, kv_a, kv_b, g_pair, up_own, d_other, *o_far_y
     )
     g_ring, g_y = hop_ring(g_pair), hop_y(g_pair)
-    d_other = hop_low(d_other)
-    uf = hop_x(uz)
+    uz = hop_low(up_own)
+    d_pair = paired(d_own, d_other)
+
+    (q_turned,) = pin.apart(q_turned)
     output_full = legs(o_pair, o_y, o_far, o_far_y)
     layout = (seen, key_base, q_turned, query_lanes, start_lanes, local_column)
     kv = (kv_own, kv_y, kv_a, kv_b)
     attended, out_turned, lse, branch_near, branch_far = attend(layout, kv, output_full)
     z_got = hop_core(branch_far)
 
-    z_got, g_y, uf, u_pair = pin(z_got, g_y, uf, u_pair)
+    z_got, g_y, u_pair = pin(z_got, g_y, u_pair)
     z_own, z_x, z_low, z_corner = combine(branch_near, z_got)
-    zc, zx = hop_x(z_corner), hop_x(z_x)
+    zc = hop_x(z_corner)
     u_y = hop_y(u_pair)
     inputs = tokens.astype(wide_type)
     inverse_one = lax.rsqrt(jnp.mean(inputs * inputs, axis=-1, keepdims=True) + eps_norm)
     unit_one = inputs * inverse_one
 
-    zc, g_ring, u_pair, uf = pin(zc, g_ring, u_pair, uf)
-    zz = hop_low(onward(z_low, zc))
+    zc, z_x, g_ring, u_pair, uz = pin(zc, z_x, g_ring, u_pair, uz)
+    zz, zx = hop_low(onward(z_low, zc)), hop_x(z_x)
     g_far = rest_of_ring(g_ring)
     u_ring = hop_ring(u_pair)
-    near_up = pack(up_own, ux, uz, uf)
-
-    zx, zz, u_y, near_up, d_other = pin(zx, zz, u_y, near_up, d_other)
+
+    zx, zz, u_y, uz = pin(zx, zz, u_y, uz)
     g_far_y = [hop_y(block) for block in g_far]
     middle = inputs + arrived(z_own, zx, zz)
     inverse_two = lax.rsqrt(jnp.mean(middle * middle, axis=-1, keepdims=True) + eps_norm)
     unit_two = middle * inverse_two
     own_two = (unit_two * gains[1]).astype(low_type)
     az, ax = hop_low(own_two), hop_x(own_two)
-    far_up = hop_core(near_up)
-    d_pair = paired(d_own, d_other)
-
-    ax, az, d_pair, far_up = pin(ax, az, d_pair, far_up)
+
+    ax, az, u_ring, d_pair, uz, *g_far_y = pin(ax, az, u_ring, d_pair, uz, *g_far_y)
     af = hop_x(az)
-    d_y = hop_y(d_pair)
-
-    af, *g_far_y = pin(af, *g_far_y)
-    gate_full = legs(g_pair, g_y, g_far, g_far_y)
-    near_two = pack(own_two, ax, az, af)
-    far_two = hop_core(near_two)
-
-    far_two, u_ring, d_y, d_pair = pin(far_two, u_ring, d_y, d_pair)
     u_far = rest_of_ring(u_ring)
     u_far_y = [hop_y(block) for block in u_far]
     d_ring = hop_ring(d_pair)
-    turned_up = turn(near_up, far_up)
-
-    turned_up, *u_far_y = pin(turned_up, *u_far_y)
+    gate_full = legs(g_pair, g_y, g_far, g_far_y)
+
+    af, d_pair, uz = pin(af, d_pair, uz)
+    near_two = pack(own_two, ax, az, af)
+    far_two = hop_core(near_two)
+    d_y, uf = hop_y(d_pair), hop_x(uz)
+
+    far_two, *u_far_y = pin(far_two, *u_far_y)
     up_full = legs(u_pair, u_y, u_far, u_far_y)
     turned_two, hidden, first_factor, second_factor = ffn(
         near_two, far_two, gate_full, up_full
     )
-    down_first = share_first(turned_up, hidden)
-
-    d_ring, down_first = pin(d_ring, down_first)
+
+    d_ring, d_y, uf, hidden = pin(d_ring, d_y, uf, hidden)
     d_far = rest_of_ring(d_ring)
     d_far_y = [hop_y(block) for block in d_far]
+    near_up = pack(up_own, ux, uz, uf)
+    far_up = hop_core(near_up)
+    turned_up = turn(near_up, far_up)
+    down_first = share_first(turned_up, hidden)
 
     down_first, hidden, *d_far_y = pin(down_first, hidden, *d_far_y)
     down_sent = hop_y(down_first)
@@ -1093,10 +1096,10 @@
 
     s_got, grad_up, gate_first = pin(s_got, grad_up, gate_first)
     s_own, s_x, s_low, s_corner = branch(ffn_pairs, 0, s_got)
-    sc, sx = hop_x(s_corner), hop_x(s_x)
-
-    sc, grad_up = pin(sc, grad_up)
-    sz = hop_low(onward(s_low, sc))
+    sc = hop_x(s_corner)
+
+    sc, s_x, grad_up = pin(sc, s_x, grad_up)
+    sz, sx = hop_low(onward(s_low, sc)), hop_x(s_x)
     up_first = share_first(turned_two, grad_up)
 
     sx, sz, down_got, gate_first, up_first, hidden = pin(
@@ -1121,75 +1124,102 @@
     near_three = pack(own_three, bx, bz, bf)
     far_three = hop_core(near_three)
 
-    far_three, gate_got, down_travel, up_first, grad_gate = pin(
-        far_three, gate_sent, down_travel, up_first, grad_gate
-    )
-    up_sent = hop_y(up_first)
-    gate_travel = share_rest(
-        turned_two, grad_gate, gate_got, share_term(turned_two, grad_gate, gate_got, 0)
-    )
+    (far_three,) = pin(far_three)
     dq_turned, dkv_own, dkv_y, dkv_a, dkv_b = attend_back(
         layout, kv, output_full, near_three, far_three, out_turned, lse, cos, sin
     )
 
-    dkv_y, dkv_a, dkv_b, near_three = pin(dkv_y, dkv_a, dkv_b, near_three)
+    dkv_y, dkv_a, dkv_b, gate_got, down_travel, up_first = pin(
+        dkv_y, dkv_a, dkv_b, gate_sent, down_travel, up_first
+    )
     dkv_a, dkv_b, dkv_y = to_previous(dkv_a, 0), to_previous(dkv_b, 1), hop_y(dkv_y)
+    up_sent = hop_y(up_first)
+    gate_term = share_term(turned_two, grad_gate, gate_got, 0)
+
+    dkv_y, dkv_a, dkv_b, gate_term, near_three = pin(
+        dkv_y, dkv_a, dkv_b, gate_term, near_three
+    )
+    gate_travel = share_rest(turned_two, grad_gate, gate_got, gate_term)
+    dqkv = finish(
+        (1 - l).astype(jnp.int32).reshape(1), dq_turned, dkv_own, dkv_y, dkv_a, dkv_b, cos, sin
+    )
+    attn_pairs = [(dqkv, qkv_full)]
+    r_got = hop_core(branch(attn_pairs, 1))
     turned_three = turn(near_three, far_three)
     output_first = share_first(turned_three, attended)
 
-    dkv_y, dkv_a, dkv_b, output_first = pin(dkv_y, dkv_a, dkv_b, output_first)
-    dqkv = finish(
-        (1 - l).astype(jnp.int32).reshape(1), dq_turned, dkv_own, dkv_y, dkv_a, dkv_b, cos, sin
-    )
-    attn_pairs = [(dqkv, qkv_full)]
-    r_got = hop_core(branch(attn_pairs, 1))
+    r_got, dqkv, output_first = pin(r_got, dqkv, output_first)
     output_sent = hop_y(output_first)
-    qkv_sent = hop_y(share_first(turned_one, dqkv))
-
-    r_got, up_got, gate_travel, hidden = pin(r_got, up_sent, gate_travel, hidden)
-    r_own, r_x, r_low, r_corner = branch(attn_pairs, 0, r_got)
-    rc, rx = hop_x(r_corner), hop_x(r_x)
+    r_own, r_x, r_low, r_corner = branch([(dqkv, qkv_full)], 0, r_got)
+    rc = hop_x(r_corner)
+    qkv_first = share_first(turned_one, dqkv)
+
+    rc, r_x, up_got, qkv_first, down_travel = pin(rc, r_x, up_sent, qkv_first, down_travel)
+    rz, rx = hop_low(onward(r_low, rc)), hop_x(r_x)
     up_travel = share_rest(
         turned_two, grad_up, up_got, share_term(turned_two, grad_up, up_got, 0)
     )
 
-    rc, output_got, hidden = pin(rc, output_sent, hidden)
-    rz = hop_low(onward(r_low, rc))
+    down_travel, qkv_first = pin.apart(down_travel, qkv_first)
+    down_mine, down_theirs, down_square = share_third(turned_up, hidden, down_got, down_travel)
+
+    rx, rz, gate_travel, output_got, down_theirs, qkv_first = pin(
+        rx, rz, gate_travel, output_sent, down_theirs, qkv_first
+    )
+    qkv_sent = hop_y(qkv_first)
+    down_other = hop_low(down_theirs)
+
+    hidden, gate_travel, output_got, rx = pin.apart(hidden, gate_travel, output_got, rx)
+    f_got = hop_core(branch([(hidden, down_full)], 1))
     output_term = share_term(turned_three, attended, output_got, 0)
-    down_mine, down_theirs = share_third(turned_up, hidden, down_got, down_travel)
-
-    rx, rz, qkv_got, output_term, down_theirs, hidden = pin(
-        rx, rz, qkv_sent, output_term, down_theirs, hidden
-    )
+    grad_normed_one = arrived(r_own, rx, rz)
+    gain_one = jnp.sum(grad_normed_one * unit_one, axis=0)
+    grad_tokens = grad_middle + norm_back(grad_normed_one, unit_one, inverse_one, gains[0])
+    gate_mine, gate_theirs, gate_square = share_third(
+        turned_two, grad_gate, gate_got, gate_travel
+    )
+    gate_other = hop_low(gate_theirs)
+
+    f_got, qkv_got, output_term, down_other = pin(f_got, qkv_sent, output_term, down_other)
     output_travel = share_rest(turned_three, attended, output_got, output_term)
     qkv_travel = share_rest(
         turned_one, dqkv, qkv_got, share_term(turned_one, dqkv, qkv_got, 0)
     )
-    down_other = hop_low(down_theirs)
-    down_pairs = [(hidden, down_full)]
-    f_got = hop_core(branch(down_pairs, 1))
-    gate_mine, gate_theirs = share_third(turned_two, grad_gate, gate_got, gate_travel)
-    grad_normed_one = arrived(r_own, rx, rz)
-    gain_one = jnp.sum(grad_normed_one * unit_one, axis=0)
-    grad_tokens = grad_middle + norm_back(grad_normed_one, unit_one, inverse_one, gains[0])
-
-    f_got, up_travel, gate_theirs, down_other = pin(f_got, up_travel, gate_theirs, down_other)
-    gate_other = hop_low(gate_theirs)
-    f_own, f_x, f_low, f_corner = branch(down_pairs, 0, f_got)
-    fc, fx = hop_x(f_corner), hop_x(f_x)
-    up_mine, up_theirs = share_third(turned_two, grad_up, up_got, up_travel)
-
-    output_travel, qkv_travel, up_theirs, gate_other, fc = pin(
-        output_travel, qkv_travel, up_theirs, gate_other, fc
-    )
-    qkv_mine, qkv_theirs = share_third(turned_one, dqkv, qkv_got, qkv_travel)
+
+    up_travel, gate_other = pin.apart(up_travel, gate_other)
+    up_mine, up_theirs, up_square = share_third(turned_two, grad_up, up_got, up_travel)
+
+    up_theirs, hidden, f_got = pin(up_theirs, hidden, f_got)
+    up_other = hop_low(up_theirs)
+    f_own, f_x, f_low, f_corner = branch([(hidden, down_full)], 0, f_got)
+    fc = hop_x(f_corner)
+
+    fc, f_x, output_travel, gain_one = pin(fc, f_x, output_travel, gain_one)
+    fz, fx = hop_low(onward(f_low, fc)), hop_x(f_x)
+
+    (output_travel,) = pin.apart(output_travel)
+    output_mine, output_theirs, output_square = share_third(
+        turned_three, attended, output_got, output_travel
+    )
+    output_other = hop_low(output_theirs)
+    square_row = jnp.full(
+        (1, width), (down_square + gate_square + up_square + output_square) / width
+    )
+    sums = jnp.concatenate([gain_one[None], gain_two[None], square_row], axis=0)
+
+    qkv_travel, sums, up_other = pin(qkv_travel, sums, up_other)
+    qkv_mine, qkv_theirs, qkv_square = share_third(turned_one, dqkv, qkv_got, qkv_travel)
     qkv_other = hop_low(qkv_theirs)
-    output_mine, output_theirs = share_third(turned_three, attended, output_got, output_travel)
-    output_other = hop_low(output_theirs)
-    up_other = hop_low(up_theirs)
-    fz = hop_low(onward(f_low, fc))
+    last_row = (jnp.arange(3) == 2).astype(wide_type)[:, None]
+    totals = sums + last_row * (qkv_square / width)
+    totals = totals + hop_core(totals)
+
+    from_x = hop_x(totals)
+    from_x, qkv_other, output_other, fx, fz = pin(from_x, qkv_other, output_other, fx, fz)
     block_out = (middle + arrived(f_own, fx, fz)).astype(low_type)
-
+    totals = sum_rest(totals + from_x)
+    gain_total = totals[:2]
+    grad_norm = jnp.sqrt(totals[2, 0] * width + jnp.sum(gain_total * gain_total))
     def joined(mine, other, start, stop):
         return ordered(l, mine[:, start:stop], other[:, start:stop].astype(wide_type), 1)
 
@@ -1210,15 +1240,6 @@
         ]
     )
     grad_down = joined(down_mine, down_other, 0, hidden_part)
-    shares = (
-        down_mine, down_other, gate_mine, gate_other, up_mine, up_other,
-        output_mine, output_other, qkv_mine, qkv_other,
-    )
-    squares = [jnp.sum(jnp.square(part.astype(wide_type))) for part in shares]
-    square_row = jnp.full((1, width), functools.reduce(jnp.add, squares) / width)
-    totals = sum_all(jnp.concatenate([gain_one[None], gain_two[None], square_row], axis=0))
-    gain_total = totals[:2]
-    grad_norm = jnp.sqrt(totals[2, 0] * width + jnp.sum(gain_total * gain_total))
     rows_owned = query_weight.shape[0]
     grad_gains = lax.dynamic_slice_in_dim(
         gain_total, lax.axis_index("dp") * rows_owned, rows_owned, 1

time: 870 us -> 803 us (0.923)
  waiting for transfers between devices: 299 us -> 238 us
  other arithmetic: 108 us -> 97.4 us
  Pallas kernels: 309 us -> 319 us
    ppermute x79 -> x84, waiting for transfers between devices: 299 us -> 238 us  [hop(): return lax.ppermute(block, AXES, route)]
    pallas_call x29 -> x36, Pallas kernels: 37.1 us -> 46.2 us  [__call__(): pl.pallas_call(keep_body, out_shape=jax.ShapeDtypeStruct(held.shape, held...]
    ppermute x79 -> x84, starting transfers between devices: 99.6 us -> 98.2 us  [hop(): return lax.ppermute(block, AXES, route)]
  transfers between devices with their start and end apart: 79 -> 84, of which waited for: 39 -> 36; matrix products, arithmetic and copies ran while one was open for 11% -> 10% of each run, Pallas kernels for 32% -> 36%
where the time goes in v3:
time: 803 us; the launch traced here: 793 us
  Pallas kernels  319 us (40%)
  waiting for transfers between devices  238 us (30%)
  starting transfers between devices  98.2 us (12%)
  other arithmetic  97.4 us (12%)
  local copies, waits for them, and re-layouts  32.6 us (4%)
    ppermute x84, waiting for transfers between devices, hop(): return lax.ppermute(block, AXES, route)  238 us
    ppermute x84, starting transfers between devices, hop(): return lax.ppermute(block, AXES, route)  98.2 us
    pallas_call x15, Pallas kernels, weight_rows(): pl.pallas_call(functools.partial(weight_body, len(addends)), grid_spec=pl...  81.1 us
    pallas_call x6, Pallas kernels, branch(): call(functools.partial(branch_body, len(pairs), weight.count(), got is no...  59.8 us
    pallas_call x36, Pallas kernels, __call__(): pl.pallas_call(keep_body, out_shape=jax.ShapeDtypeStruct(held.shape, held...  46.2 us
    mul x6, other arithmetic, adamw(): -learn_rate  26.4 us
    pallas_call x1, Pallas kernels, ffn(): call(functools.partial(ffn_body, gate_weight.count()), (tiles,), [tile_of...  19.8 us
    pallas_call x1, Pallas kernels, attend_back(): call(functools.partial(attend_back_body, weight.count()), (tiles,), [smem...  19.6 us
  transfers between devices with their start and end apart: 84, of which 36 were waited for; matrix products, arithmetic and copies ran while one was open for 10% of the time, Pallas kernels for 36%

profile of v3, /device:TPU:0, one launch (start us, length us, event | category | flops | bytes accessed | tf_op | source)
XLA Modules:
  0.0 793.1 jit_solution(13335971946576917543)
XLA Ops:
  40.3 9.1 %collective-permute-done.4.refs_2_ = bf16[128,2560]{1,0:T(8,128)(2,1)} collective-permute-done((bf16[128,2560]{1,0:T(8,128)(2,1)}, bf16[128,2560]{1,0:T(8,128)(2,1)}, u32[]{:S(2)}, u32[]{:S(2)}) %collective-permute-start.4) | collective-permute-done | bytes 655392 | tf_op jit(solution)/shard_map/ppermute | solution.py:48
  51.3 12.8 %collective-permute-done.5.refs_3_ = bf16[128,2560]{1,0:T(8,128)(2,1)} collective-permute-done((bf16[128,2560]{1,0:T(8,128)(2,1)}, bf16[128,2560]{1,0:T(8,128)(2,1)}, u32[]{:S(2)}, u32[]{:S(2)}) %collective-permute-start.5) | collective-permute-done | bytes 655392 | tf_op jit(solution)/shard_map/ppermute | solution.py:48
  94.9 10.5 %shard_map.420 = (bf16[2560,1024]{1,0:T(8,128)(2,1)}, bf16[4,80,1024]{2,1,0:T(8,128)(2,1)}, bf16[4,160,256]{2,1,0:T(8,128)(2,1)}, f32[2,2560]{1,0:T(2,128)}) custom-call(bf16[4,128,2560]{2,1,0:T(8,128)(2,1)} %shard_map.415.x_ref, bf16[4,128,2560]{2,1,0:T(8,128)(2,1)} %collective-permute-done.7.xc_ref, f32[4,40,256]{2,1,0:T(8,128)} %get-tuple-element.540.cos_ref, ...), custom_call_target="tpu_custom_call" | custom-call | flops 10000000000 | tf_op jit(solution)/shard_map/pallas_call | solution.py:339
  137.1 19.0 %shard_map.424 = (bf16[4,256,320]{2,1,0:T(8,128)(2,1)}, f32[4,80,1024]{2,1,0:T(8,128)}, f32[4,1,1024]{2,1,0:T(1,128)}, bf16[4,128,2560]{2,1,0:T(8,128)(2,1)}, bf16[4,128,2560]{2,1,0:T(8,128)(2,1)}) custom-call(s32[48]{0:T(128)} %reshape.711.seen_ref, s32[12]{0:T(128)} %copy-done.66, bf16[4,80,1024]{2,1,0:T(8,128)(2,1)} %get-tuple-element.276.q_ref, ...), custom_call_target="tpu_custom_call" | custom-call | flops 10000000000 | tf_op jit(solution)/shard_map/pallas_call | solution.py:442
  171.9 8.8 %collective-permute-done.24.refs_3_.refs_5_ = bf16[2,320,896]{2,1,0:T(8,128)(2,1)} collective-permute-done((bf16[2,320,896]{2,1,0:T(8,128)(2,1)}, bf16[2,320,896]{2,1,0:T(8,128)(2,1)}, u32[]{:S(2)}, u32[]{:S(2)}) %collective-permute-start.24) | collective-permute-done | bytes 1146912 | tf_op jit(solution)/shard_map/ppermute | solution.py:48
  200.6 14.8 %collective-permute-done.27 = bf16[128,2560]{1,0:T(8,128)(2,1)} collective-permute-done((bf16[128,2560]{1,0:T(8,128)(2,1)}, bf16[128,2560]{1,0:T(8,128)(2,1)}, u32[]{:S(2)}, u32[]{:S(2)}) %collective-permute-start.27) | collective-permute-done | bytes 655392 | tf_op jit(solution)/shard_map/ppermute | solution.py:48
  223.3 19.0 %collective-permute-done.31.refs_8_.refs_10_ = bf16[2,320,896]{2,1,0:T(8,128)(2,1)} collective-permute-done((bf16[2,320,896]{2,1,0:T(8,128)(2,1)}, bf16[2,320,896]{2,1,0:T(8,128)(2,1)}, u32[]{:S(2)}, u32[]{:S(2)}) %collective-permute-start.31) | collective-permute-done | bytes 1146912 | tf_op jit(solution)/shard_map/ppermute | solution.py:48
  253.3 9.2 %collective-permute-done.33.refs_3_ = bf16[128,2560]{1,0:T(8,128)(2,1)} collective-permute-done((bf16[128,2560]{1,0:T(8,128)(2,1)}, bf16[128,2560]{1,0:T(8,128)(2,1)}, u32[]{:S(2)}, u32[]{:S(2)}) %collective-permute-start.33) | collective-permute-done | bytes 655392 | tf_op jit(solution)/shard_map/ppermute | solution.py:48
  272.2 8.8 %collective-permute-done.35.refs_9_.refs_11_ = bf16[2,320,896]{2,1,0:T(8,128)(2,1)} collective-permute-done((bf16[2,320,896]{2,1,0:T(8,128)(2,1)}, bf16[2,320,896]{2,1,0:T(8,128)(2,1)}, u32[]{:S(2)}, u32[]{:S(2)}) %collective-permute-start.35) | collective-permute-done | bytes 1146912 | tf_op jit(solution)/shard_map/ppermute | solution.py:48
  282.3 19.8 %shard_map.433 = (bf16[2560,1024]{1,0:T(8,128)(2,1)}, bf16[4,256,896]{2,1,0:T(8,128)(2,1)}, f32[4,256,896]{2,1,0:T(8,128)}, f32[4,256,896]{2,1,0:T(8,128)}) custom-call(bf16[4,128,2560]{2,1,0:T(8,128)(2,1)} %shard_map.431.near_ref, bf16[4,128,2560]{2,1,0:T(8,128)(2,1)} %collective-permute-done.34.far_ref, ...), custom_call_target="tpu_custom_call" | custom-call | flops 10000000000 | tf_op jit(solution)/shard_map/pallas_call | solution.py:652
  324.0 10.2 %collective-permute-done.40.refs_4_.refs_5_ = bf16[2,320,896]{2,1,0:T(8,128)(2,1)} collective-permute-done((bf16[2,320,896]{2,1,0:T(8,128)(2,1)}, bf16[2,320,896]{2,1,0:T(8,128)(2,1)}, u32[]{:S(2)}, u32[]{:S(2)}) %collective-permute-start.40) | collective-permute-done | bytes 1146912 | tf_op jit(solution)/shard_map/ppermute | solution.py:48
  334.2 12.4 %shard_map.439 = (bf16[4,256,896]{2,1,0:T(8,128)(2,1)}, bf16[4,256,896]{2,1,0:T(8,128)(2,1)}) custom-call(bf16[4,128,2560]{2,1,0:T(8,128)(2,1)} %shard_map.435.near_ref, bf16[4,128,2560]{2,1,0:T(8,128)(2,1)} %collective-permute-done.39.far_ref, f32[4,256,896]{2,1,0:T(8,128)} %get-tuple-element.329.one_ref, f32[4,256,896]{2,1,0:T(8,128)} %get-tuple-element.330.two_ref, ...), custom_call_target="tpu_custom_call" | custom-call | flops 10000000000 | tf_op jit(solution)/shard_map/pallas_call | solution.py:694
  346.6 13.6 %shard_map.440 = bf16[4,128,2560]{2,1,0:T(8,128)(2,1)} custom-call(bf16[4,2,128,896]{3,2,1,0:T(8,128)(2,1)} %bitcast.162, bf16[4,2,128,896]{3,2,1,0:T(8,128)(2,1)} %bitcast.157, s32[8]{0:T(128)} %stack.60.refs_0_.refs_4_.refs_5_.refs_2_.refs_7_.refs_1_, bf16[2,320,896]{2,1,0:T(8,128)(2,1)} %maximum_select_fusion.3.refs_1_.refs_3_, ...), custom_call_target="tpu_custom_call" | custom-call | flops 10000000000 | tf_op jit(solution)/shard_map/pallas_call | solution.py:771
  369.0 14.0 %shard_map.443 = (f32[128,2560]{1,0:T(8,128)}, bf16[128,2560]{1,0:T(8,128)(2,1)}, bf16[128,2560]{1,0:T(8,128)(2,1)}, bf16[128,2560]{1,0:T(8,128)(2,1)}) custom-call(bf16[4,2,128,896]{3,2,1,0:T(8,128)(2,1)} %bitcast.164, bf16[4,2,128,896]{3,2,1,0:T(8,128)(2,1)} %bitcast.158, s32[8]{0:T(128)} %stack.60.refs_0_.refs_4_.refs_5_.refs_2_.refs_7_.refs_1_, ...), custom_call_target="tpu_custom_call" | custom-call | flops 10000000000 | tf_op jit(solution)/shard_map/pallas_call | solution.py:771
  385.9 14.4 %collective-permute-done.42 = bf16[128,2560]{1,0:T(8,128)(2,1)} collective-permute-done((bf16[128,2560]{1,0:T(8,128)(2,1)}, bf16[128,2560]{1,0:T(8,128)(2,1)}, u32[]{:S(2)}, u32[]{:S(2)}) %collective-permute-start.42) | collective-permute-done | bytes 655392 | tf_op jit(solution)/shard_map/ppermute | solution.py:48
  450.0 9.2 %collective-permute-done.48.refs_3_ = bf16[128,2560]{1,0:T(8,128)(2,1)} collective-permute-done((bf16[128,2560]{1,0:T(8,128)(2,1)}, bf16[128,2560]{1,0:T(8,128)(2,1)}, u32[]{:S(2)}, u32[]{:S(2)}) %collective-permute-start.48) | collective-permute-done | bytes 655392 | tf_op jit(solution)/shard_map/ppermute | solution.py:48
  469.7 19.6 %shard_map.451 = (bf16[4,320,256]{2,1,0:T(8,128)(2,1)}, f32[4,160,256]{2,1,0:T(8,128)}, bf16[4,160,256]{2,1,0:T(8,128)(2,1)}, bf16[2,160,256]{2,1,0:T(8,128)(2,1)}, bf16[2,160,256]{2,1,0:T(8,128)(2,1)}) custom-call(s32[48]{0:T(128)} %reshape.711.seen_ref, s32[12]{0:T(128)} %copy-done.66, bf16[4,80,1024]{2,1,0:T(8,128)(2,1)} %get-tuple-element.276.q_ref, ...), custom_call_target="tpu_custom_call" | custom-call | flops 10000000000 | tf_op jit(solution)/shard_map/pallas_call | solution.py:543
  535.6 7.7 shard_map.461
  583.1 7.8 collective-permute-done.60
  599.2 8.3 %shard_map.470 = bf16[4,128,2560]{2,1,0:T(8,128)(2,1)} custom-call(bf16[4,2,128,896]{3,2,1,0:T(8,128)(2,1)} %bitcast.155, s32[8]{0:T(128)} %stack.60.refs_0_.refs_4_.refs_5_.refs_2_.refs_7_.refs_1_, bf16[2,320,896]{2,1,0:T(8,128)(2,1)} %maximum_select_fusion.5.refs_1_.refs_2_, bf16[2,320,896]{2,1,0:T(8,128)(2,1)} %collective-permute-done.37.refs_2_.refs_3_, ...), custom_call_target="tpu_custom_call" | custom-call | flops 10000000000 | tf_op jit(solution)/shard_map/pallas_call | solution.py:771
  655.9 9.5 %shard_map.476 = (f32[128,2560]{1,0:T(8,128)}, bf16[128,2560]{1,0:T(8,128)(2,1)}, bf16[128,2560]{1,0:T(8,128)(2,1)}, bf16[128,2560]{1,0:T(8,128)(2,1)}) custom-call(bf16[4,2,128,896]{3,2,1,0:T(8,128)(2,1)} %bitcast.156, s32[8]{0:T(128)} %stack.60.refs_0_.refs_4_.refs_5_.refs_2_.refs_7_.refs_1_, bf16[2,320,896]{2,1,0:T(8,128)(2,1)} %maximum_select_fusion.5.refs_1_.refs_2_, ...), custom_call_target="tpu_custom_call" | custom-call | flops 10000000000 | tf_op jit(solution)/shard_map/pallas_call | solution.py:771
  674.5 18.2 %collective-permute-done.72.refs_2_.refs_3_ = bf16[2,320,320]{2,1,0:T(8,128)(2,1)} collective-permute-done((bf16[2,320,320]{2,1,0:T(8,128)(2,1)}, bf16[2,320,320]{2,1,0:T(8,128)(2,1)}, u32[]{:S(2)}, u32[]{:S(2)}) %collective-permute-start.72) | collective-permute-done | bytes 409632 | tf_op jit(solution)/shard_map/ppermute | solution.py:48
  729.6 8.5 %collective-permute-done.78 = bf16[320,320]{1,0:T(8,128)(2,1)S(1)} collective-permute-done((bf16[320,320]{1,0:T(8,128)(2,1)S(1)}, bf16[320,320]{1,0:T(8,128)(2,1)S(1)}, u32[]{:S(2)}, u32[]{:S(2)}) %collective-permute-start.78) | collective-permute-done | bytes 204832 | tf_op jit(solution)/shard_map/ppermute | solution.py:48
  775.3 10.0 %add_multiply_fusion = (f32[2,320,1792]{2,1,0:T(8,128)}, f32[2,320,1792]{2,1,0:T(8,128)}, f32[2,320,1792]{2,1,0:T(8,128)}, f32[2,320,1792]{2,1,0:T(8,128)}) fusion(f32[2,320,1792]{2,1,0:T(8,128)S(1)} %bitcast.110, f32[]{:T(128)S(6)} %min_shard_map.3, f32[2,320,1792]{2,1,0:T(8,128)S(1)} %copy-done.9, f32[2,320,1792]{2,1,0:T(8,128)} %param.33, ...), kind=kLoop, calls=%fused_computation.3 | loop fusion | flops 18350080 | bytes 36700164 | tf_op jit(solution)/shard_map/mul | solution.py:871
  (488 shorter events, 490.2 us)
Async XLA Ops:
  26.1 47.4 %collective-permute-start.8 = (bf16[2,320,482]{2,1,0:T(8,128)(2,1)}, bf16[2,320,482]{2,1,0:T(8,128)(2,1)}, u32[]{:S(2)}, u32[]{:S(2)}) collective-permute-start(bf16[2,320,482]{2,1,0:T(8,128)(2,1)} %maximum_select_fusion.8.refs_1_.refs_2_), channel_id=1, source_target_pairs={{0,16},{1,17},{2,18},{3,19},{4,20},{5,21},{6,22},{7,23},{8,24},{9,... | collective-permute-start | bytes 1850888 | tf_op jit(solution)/shard_map/ppermute | solution.py:48
  77.5 29.3 %collective-permute-start.12 = (bf16[2,320,320]{2,1,0:T(8,128)(2,1)}, bf16[2,320,320]{2,1,0:T(8,128)(2,1)}, u32[]{:S(2)}, u32[]{:S(2)}) collective-permute-start(bf16[2,320,320]{2,1,0:T(8,128)(2,1)} %maximum_select_fusion.9.refs_5_), channel_id=1, source_target_pairs={{0,16},{1,17},{2,18},{3,19},{4,20},{5,21},{6,22},{7,23},{8,24},{9,... | collective-permute-start | bytes 1228808 | tf_op jit(solution)/shard_map/ppermute | solution.py:48
  130.2 50.6 %collective-permute-start.24 = (bf16[2,320,896]{2,1,0:T(8,128)(2,1)}, bf16[2,320,896]{2,1,0:T(8,128)(2,1)}, u32[]{:S(2)}, u32[]{:S(2)}) collective-permute-start(bf16[2,320,896]{2,1,0:T(8,128)(2,1)} %maximum_select_fusion.3.refs_1_.refs_3_), channel_id=1, source_target_pairs={{0,16},{1,17},{2,18},{3,19},{4,20},{5,21},{6,22},{7,23},{8,24},{9,... | collective-permute-start | bytes 3440648 | tf_op jit(solution)/shard_map/ppermute | solution.py:48
  134.4 37.5 %collective-permute-start.25 = (bf16[128,2560]{1,0:T(8,128)(2,1)}, bf16[128,2560]{1,0:T(8,128)(2,1)}, u32[]{:S(2)}, u32[]{:S(2)}) collective-permute-start(bf16[128,2560]{1,0:T(8,128)(2,1)} %refs_0_.1), channel_id=1, source_target_pairs={{0,8},{1,9},{2,10},{3,11},{4,12},{5,13},{6,14},{7,15},{8,0},{9,1},... | collective-permute-start | bytes 1966088 | tf_op jit(solution)/shard_map/ppermute | solution.py:48
  168.9 29.4 %collective-permute-start.28 = (bf16[2,320,896]{2,1,0:T(8,128)(2,1)}, bf16[2,320,896]{2,1,0:T(8,128)(2,1)}, u32[]{:S(2)}, u32[]{:S(2)}) collective-permute-start(bf16[2,320,896]{2,1,0:T(8,128)(2,1)} %maximum_select_fusion.4.refs_6_.refs_8_), channel_id=1, source_target_pairs={{0,4},{1,5},{2,6},{3,7},{4,0},{5,1},{6,2},{7,3},{8,12},{9,13},{10,... | collective-permute-start | bytes 3440648 | tf_op jit(solution)/shard_map/ppermute | solution.py:48
  190.0 52.3 %collective-permute-start.31 = (bf16[2,320,896]{2,1,0:T(8,128)(2,1)}, bf16[2,320,896]{2,1,0:T(8,128)(2,1)}, u32[]{:S(2)}, u32[]{:S(2)}) collective-permute-start(bf16[2,320,896]{2,1,0:T(8,128)(2,1)} %maximum_select_fusion.4.refs_6_.refs_8_), channel_id=1, source_target_pairs={{0,16},{1,17},{2,18},{3,19},{4,20},{5,21},{6,22},{7,23},{8,24},{9,... | collective-permute-start | bytes 3440648 | tf_op jit(solution)/shard_map/ppermute | solution.py:48
  193.0 49.3 %collective-permute-start.32 = (bf16[2,320,896]{2,1,0:T(8,128)(2,1)}, bf16[2,320,896]{2,1,0:T(8,128)(2,1)}, u32[]{:S(2)}, u32[]{:S(2)}) collective-permute-start(bf16[2,320,896]{2,1,0:T(8,128)(2,1)} %collective-permute-done.24.refs_3_.refs_5_), channel_id=1, source_target_pairs={{0,4},{1,5},{2,6},{3,7},{4,0},{5,1},{6,2},{7,3},{8,12},{9,13},{10,... | collective-permute-start | bytes 3440648 | tf_op jit(solution)/shard_map/ppermute | solution.py:48
  250.3 51.9 %collective-permute-start.36 = (bf16[2,320,896]{2,1,0:T(8,128)(2,1)}, bf16[2,320,896]{2,1,0:T(8,128)(2,1)}, u32[]{:S(2)}, u32[]{:S(2)}) collective-permute-start(bf16[2,320,896]{2,1,0:T(8,128)(2,1)} %maximum_select_fusion.5.refs_1_.refs_2_), channel_id=1, source_target_pairs={{0,16},{1,17},{2,18},{3,19},{4,20},{5,21},{6,22},{7,23},{8,24},{9,... | collective-permute-start | bytes 3440648 | tf_op jit(solution)/shard_map/ppermute | solution.py:48
  262.5 39.7 %collective-permute-start.37 = (bf16[2,320,896]{2,1,0:T(8,128)(2,1)}, bf16[2,320,896]{2,1,0:T(8,128)(2,1)}, u32[]{:S(2)}, u32[]{:S(2)}) collective-permute-start(bf16[2,320,896]{2,1,0:T(8,128)(2,1)} %maximum_select_fusion.5.refs_1_.refs_2_), channel_id=1, source_target_pairs={{0,4},{1,5},{2,6},{3,7},{4,0},{5,1},{6,2},{7,3},{8,12},{9,13},{10,... | collective-permute-start | bytes 3440648 | tf_op jit(solution)/shard_map/ppermute | solution.py:48
  266.4 35.8 %collective-permute-start.38 = (bf16[128,2560]{1,0:T(8,128)(2,1)}, bf16[128,2560]{1,0:T(8,128)(2,1)}, u32[]{:S(2)}, u32[]{:S(2)}) collective-permute-start(bf16[128,2560]{1,0:T(8,128)(2,1)} %collective-permute-done.25.refs_2_), channel_id=1, source_target_pairs={{0,2},{1,3},{2,0},{3,1},{4,6},{5,7},{6,4},{7,5},{8,10},{9,11},{10,... | collective-permute-start | bytes 1966088 | tf_op jit(solution)/shard_map/ppermute | solution.py:48
  361.6 52.6 %collective-permute-start.45 = (bf16[4,320,896]{2,1,0:T(8,128)(2,1)}, bf16[4,320,896]{2,1,0:T(8,128)(2,1)}, u32[]{:S(2)}, u32[]{:S(2)}) collective-permute-start(bf16[4,320,896]{2,1,0:T(8,128)(2,1)} %shard_map.437), channel_id=1, source_target_pairs={{0,4},{1,5},{2,6},{3,7},{4,0},{5,1},{6,2},{7,3},{8,12},{9,13},{10,... | collective-permute-start | bytes 6881288 | tf_op jit(solution)/shard_map/ppermute | solution.py:48
  429.4 60.0 %collective-permute-start.50 = (bf16[4,320,896]{2,1,0:T(8,128)(2,1)}, bf16[4,320,896]{2,1,0:T(8,128)(2,1)}, u32[]{:S(2)}, u32[]{:S(2)}) collective-permute-start(bf16[4,320,896]{2,1,0:T(8,128)(2,1)} %shard_map.441), channel_id=1, source_target_pairs={{0,4},{1,5},{2,6},{3,7},{4,0},{5,1},{6,2},{7,3},{8,12},{9,13},{10,... | collective-permute-start | bytes 6881288 | tf_op jit(solution)/shard_map/ppermute | solution.py:48
  436.5 52.9 %collective-permute-start.51 = (bf16[2,320,896]{2,1,0:T(8,128)(2,1)}, bf16[2,320,896]{2,1,0:T(8,128)(2,1)}, u32[]{:S(2)}, u32[]{:S(2)}) collective-permute-start(bf16[2,320,896]{2,1,0:T(8,128)(2,1)} %shard_map.452), channel_id=1, source_target_pairs={{0,16},{1,17},{2,18},{3,19},{4,20},{5,21},{6,22},{7,23},{8,24},{9,... | collective-permute-start | bytes 3440648 | tf_op jit(solution)/shard_map/ppermute | solution.py:48
  502.9 54.0 %collective-permute-start.57 = (bf16[4,320,896]{2,1,0:T(8,128)(2,1)}, bf16[4,320,896]{2,1,0:T(8,128)(2,1)}, u32[]{:S(2)}, u32[]{:S(2)}) collective-permute-start(bf16[4,320,896]{2,1,0:T(8,128)(2,1)} %shard_map.445), channel_id=1, source_target_pairs={{0,4},{1,5},{2,6},{3,7},{4,0},{5,1},{6,2},{7,3},{8,12},{9,13},{10,... | collective-permute-start | bytes 6881288 | tf_op jit(solution)/shard_map/ppermute | solution.py:48
  522.2 60.9 %collective-permute-start.61 = (bf16[2,320,896]{2,1,0:T(8,128)(2,1)}, bf16[2,320,896]{2,1,0:T(8,128)(2,1)}, u32[]{:S(2)}, u32[]{:S(2)}) collective-permute-start(bf16[2,320,896]{2,1,0:T(8,128)(2,1)} %shard_map.454), channel_id=1, source_target_pairs={{0,16},{1,17},{2,18},{3,19},{4,20},{5,21},{6,22},{7,23},{8,24},{9,... | collective-permute-start | bytes 3440648 | tf_op jit(solution)/shard_map/ppermute | solution.py:48
  546.0 37.1 %collective-permute-start.62 = (bf16[4,320,320]{2,1,0:T(8,128)(2,1)}, bf16[4,320,320]{2,1,0:T(8,128)(2,1)}, u32[]{:S(2)}, u32[]{:S(2)}) collective-permute-start(bf16[4,320,320]{2,1,0:T(8,128)(2,1)} %shard_map.459), channel_id=1, source_target_pairs={{0,4},{1,5},{2,6},{3,7},{4,0},{5,1},{6,2},{7,3},{8,12},{9,13},{10,... | collective-permute-start | bytes 2457608 | tf_op jit(solution)/shard_map/ppermute | solution.py:48
  570.7 74.5 %collective-permute-start.58 = (bf16[2,320,896]{2,1,0:T(8,128)(2,1)}, bf16[2,320,896]{2,1,0:T(8,128)(2,1)}, u32[]{:S(2)}, u32[]{:S(2)}) collective-permute-start(bf16[2,320,896]{2,1,0:T(8,128)(2,1)} %shard_map.464), channel_id=1, source_target_pairs={{0,16},{1,17},{2,18},{3,19},{4,20},{5,21},{6,22},{7,23},{8,24},{9,... | collective-permute-start | bytes 3440648 | tf_op jit(solution)/shard_map/ppermute | solution.py:48
  595.1 39.7 %collective-permute-start.67 = (bf16[4,320,482]{2,1,0:T(8,128)(2,1)}, bf16[4,320,482]{2,1,0:T(8,128)(2,1)}, u32[]{:S(2)}, u32[]{:S(2)}) collective-permute-start(bf16[4,320,482]{2,1,0:T(8,128)(2,1)} %shard_map.462), channel_id=1, source_target_pairs={{0,4},{1,5},{2,6},{3,7},{4,0},{5,1},{6,2},{7,3},{8,12},{9,13},{10,... | collective-permute-start | bytes 3701768 | tf_op jit(solution)/shard_map/ppermute | solution.py:48
  599.1 35.6 %collective-permute-start.68 = (bf16[320,896]{1,0:T(8,128)(2,1)}, bf16[320,896]{1,0:T(8,128)(2,1)}, u32[]{:S(2)}, u32[]{:S(2)}) collective-permute-start(bf16[320,896]{1,0:T(8,128)(2,1)} %fusion.14), channel_id=1, source_target_pairs={{0,8},{1,9},{2,10},{3,11},{4,12},{5,13},{6,14},{7,15},{8,0},{9,1},... | collective-permute-start | bytes 1720328 | tf_op jit(solution)/shard_map/ppermute | solution.py:48
  640.1 66.1 %collective-permute-start.70 = (bf16[2,320,482]{2,1,0:T(8,128)(2,1)}, bf16[2,320,482]{2,1,0:T(8,128)(2,1)}, u32[]{:S(2)}, u32[]{:S(2)}) collective-permute-start(bf16[2,320,482]{2,1,0:T(8,128)(2,1)} %shard_map.477), channel_id=1, source_target_pairs={{0,16},{1,17},{2,18},{3,19},{4,20},{5,21},{6,22},{7,23},{8,24},{9,... | collective-permute-start | bytes 1850888 | tf_op jit(solution)/shard_map/ppermute | solution.py:48
  640.1 52.6 %collective-permute-start.72 = (bf16[2,320,320]{2,1,0:T(8,128)(2,1)}, bf16[2,320,320]{2,1,0:T(8,128)(2,1)}, u32[]{:S(2)}, u32[]{:S(2)}) collective-permute-start(bf16[2,320,320]{2,1,0:T(8,128)(2,1)} %shard_map.471), channel_id=1, source_target_pairs={{0,16},{1,17},{2,18},{3,19},{4,20},{5,21},{6,22},{7,23},{8,24},{9,... | collective-permute-start | bytes 1228808 | tf_op jit(solution)/shard_map/ppermute | solution.py:48
  668.1 38.1 %collective-permute-start.74 = (bf16[320,896]{1,0:T(8,128)(2,1)}, bf16[320,896]{1,0:T(8,128)(2,1)}, u32[]{:S(2)}, u32[]{:S(2)}) collective-permute-start(bf16[320,896]{1,0:T(8,128)(2,1)} %fusion.16), channel_id=1, source_target_pairs={{0,8},{1,9},{2,10},{3,11},{4,12},{5,13},{6,14},{7,15},{8,0},{9,1},... | collective-permute-start | bytes 1720328 | tf_op jit(solution)/shard_map/ppermute | solution.py:48
  694.6 43.5 %collective-permute-start.79 = (bf16[128,2560]{1,0:T(8,128)(2,1)}, bf16[128,2560]{1,0:T(8,128)(2,1)}, u32[]{:S(2)}, u32[]{:S(2)}) collective-permute-start(bf16[128,2560]{1,0:T(8,128)(2,1)} %get-tuple-element.438), channel_id=1, source_target_pairs={{0,2},{1,3},{2,0},{3,1},{4,6},{5,7},{6,4},{7,5},{8,10},{9,11},{10,... | collective-permute-start | bytes 1966088 | tf_op jit(solution)/shard_map/ppermute | solution.py:48
  697.7 40.4 %collective-permute-start.80 = (bf16[128,2560]{1,0:T(8,128)(2,1)}, bf16[128,2560]{1,0:T(8,128)(2,1)}, u32[]{:S(2)}, u32[]{:S(2)}) collective-permute-start(bf16[128,2560]{1,0:T(8,128)(2,1)} %add_convert_fusion.1), channel_id=1, source_target_pairs={{0,8},{1,9},{2,10},{3,11},{4,12},{5,13},{6,14},{7,15},{8,0},{9,1},... | collective-permute-start | bytes 1966088 | tf_op jit(solution)/shard_map/ppermute | solution.py:48
  (140 other events, 1489.6 us)

commit v4 on v3

--- a/solution.py
+++ b/solution.py
@@ -993,30 +993,30 @@
     angle = freqs[None, :, None] * offset_tiles.astype(wide_type)[:, None, :]
     cos, sin = jnp.cos(angle), jnp.sin(angle)
 
-    tx, tz, g_other = pin(tx, tz, g_other)
+    tx, tz, g_other, bit = pin(tx, tz, g_other, bit)
     tf = hop_x(tz)
     g_other = hop_low(g_other)
-
-    tf, q_y, bit, up_own = pin(tf, q_y, bit, upstream)
-    near = pack(own_rows, tx, tz, tf)
-    far = hop_core(near)
     u_own, u_other = halves(bit, gateup_weight, 1)
 
-    far, q_ring, g_other, u_other, o_pair, up_own, bit = pin(
-        far, q_ring, g_other, u_other, o_pair, up_own, bit
-    )
+    q_ring, q_y, o_pair = pin.apart(q_ring, q_y, o_pair)
     q_far = rest_of_ring(q_ring)
     q_far_y = [hop_y(block) for block in q_far]
     o_ring = hop_ring(o_pair)
+
+    tf, bit, up_own = pin(tf, bit, upstream)
+    near = pack(own_rows, tx, tz, tf)
+    far = hop_core(near)
+    d_own, d_other = halves(bit, down_weight)
+
+    far, g_other, u_other, up_own, d_other, o_pair, *q_far_y = pin(
+        far, g_other, u_other, up_own, d_other, o_pair, *q_far_y
+    )
     u_other = hop_low(u_other)
-    ux = hop_x(up_own)
     g_pair = paired(g_own, g_other)
-    d_own, d_other = halves(bit, down_weight)
-
-    d_other, o_pair, *q_far_y = pin(d_other, o_pair, *q_far_y)
+
     qkv_full = legs(q_pair, q_y, q_far, q_far_y)
     turned_one, q_turned, kv_own, gains = project(near, far, qkv_full, cos, sin)
-    d_other, o_y = hop_low(d_other), hop_y(o_pair)
+    d_other, o_y, ux = hop_low(d_other), hop_y(o_pair), hop_x(up_own)
 
     kv_own, o_y, o_ring, u_other, ux = pin(kv_own, o_y, o_ring, u_other, ux)
     late = choose(l, kv_own[2:], kv_own[:2])
@@ -1140,6 +1140,8 @@
         dkv_y, dkv_a, dkv_b, gate_term, near_three
     )
     gate_travel = share_rest(turned_two, grad_gate, gate_got, gate_term)
+
+    dq_turned, near_three = pin.apart(dq_turned, near_three)
     dqkv = finish(
         (1 - l).astype(jnp.int32).reshape(1), dq_turned, dkv_own, dkv_y, dkv_a, dkv_b, cos, sin
     )
@@ -1191,10 +1193,12 @@
 
     up_theirs, hidden, f_got = pin(up_theirs, hidden, f_got)
     up_other = hop_low(up_theirs)
+
+    hidden, f_got = pin.apart(hidden, f_got)
     f_own, f_x, f_low, f_corner = branch([(hidden, down_full)], 0, f_got)
     fc = hop_x(f_corner)
 
-    fc, f_x, output_travel, gain_one = pin(fc, f_x, output_travel, gain_one)
+    fc, f_x, gain_one = pin(fc, f_x, gain_one)
     fz, fx = hop_low(onward(f_low, fc)), hop_x(f_x)
 
     (output_travel,) = pin.apart(output_travel)
@@ -1228,8 +1232,8 @@
     grad_query = joined(qkv_mine, qkv_other, 0, QROWS)
     grad_keyval = jnp.stack(
         [
-            joined(qkv_mine, qkv_other, QROWS, edge_one),
-            joined(qkv_mine, qkv_other, edge_one, EDGE),
+            joined(qkv_mine, qkv_other, QROWS, edge_one).T,
+            joined(qkv_mine, qkv_other, edge_one, EDGE).T,
         ]
     )
     grad_output = joined(output_mine, output_other, 0, QROWS)
@@ -1254,10 +1258,19 @@
     firsts = (first_query, first_keyval, first_output, first_gateup, first_down, first_gains)
     seconds = (second_query, second_keyval, second_output, second_gateup, second_down, second_gains)
     grads = (grad_query, grad_keyval, grad_output, grad_gateup, grad_down, grad_gains)
+    turned = lambda a: jnp.swapaxes(a, 1, 2)
     states = [
         adamw(params[index], grads[index] * clip, firsts[index], seconds[index])
+        if index != 1
+        else tuple(
+            turned(a)
+            for a in adamw(
+                turned(params[1]), grads[1] * clip, turned(firsts[1]), turned(seconds[1])
+            )
+        )
         for index in range(6)
     ]
+    grads = (grads[0], turned(grads[1]), *grads[2:])
     return (
         block_out,
         grad_tokens,

time: 803 us -> 791 us (0.985)
  waiting for transfers between devices: 238 us -> 220 us
    ppermute x84 -> x87, waiting for transfers between devices: 238 us -> 220 us  [hop(): return lax.ppermute(block, AXES, route)]
    pallas_call x36 -> x38, Pallas kernels: 46.2 us -> 48.7 us  [__call__(): pl.pallas_call(keep_body, out_shape=jax.ShapeDtypeStruct(held.shape, held...]
    ppermute x84 -> x87, starting transfers between devices: 98.2 us -> 99.8 us  [hop(): return lax.ppermute(block, AXES, route)]
    mul x6 -> x5, other arithmetic: 26.4 us -> 25 us  [adamw(): -learn_rate]
    select_n x19 -> x17, other arithmetic: 17.4 us -> 17 us  [choose(): return jnp.where(bit == 0, if_zero, if_one)]
  transfers between devices with their start and end apart: 84 -> 87, of which waited for: 36 -> 36; matrix products, arithmetic and copies ran while one was open for 10% -> 10% of each run, Pallas kernels for 36% -> 37%
where the time goes in v4:
time: 791 us; the launch traced here: 781 us
  Pallas kernels  321 us (41%)
  waiting for transfers between devices  220 us (28%)
  starting transfers between devices  99.8 us (13%)
  other arithmetic  95.7 us (12%)
  local copies, waits for them, and re-layouts  36.1 us (5%)
  between operations  7.97 us (1%)
    ppermute x87, waiting for transfers between devices, hop(): return lax.ppermute(block, AXES, route)  220 us
    ppermute x87, starting transfers between devices, hop(): return lax.ppermute(block, AXES, route)  99.8 us
    pallas_call x15, Pallas kernels, weight_rows(): pl.pallas_call(functools.partial(weight_body, len(addends)), grid_spec=pl...  81.2 us
    pallas_call x6, Pallas kernels, branch(): call(functools.partial(branch_body, len(pairs), weight.count(), got is no...  60.1 us
    pallas_call x38, Pallas kernels, __call__(): pl.pallas_call(keep_body, out_shape=jax.ShapeDtypeStruct(held.shape, held...  48.7 us
    mul x5, other arithmetic, adamw(): -learn_rate  25 us
    pallas_call x1, Pallas kernels, ffn(): call(functools.partial(ffn_body, gate_weight.count()), (tiles,), [tile_of...  19.8 us
    pallas_call x1, Pallas kernels, attend_back(): call(functools.partial(attend_back_body, weight.count()), (tiles,), [smem...  19.6 us
  transfers between devices with their start and end apart: 87, of which 36 were waited for; matrix products, arithmetic and copies ran while one was open for 10% of the time, Pallas kernels for 37%

profile of v4, /device:TPU:0, one launch (start us, length us, event | category | flops | bytes accessed | tf_op | source)
XLA Modules:
  0.0 780.8 jit_solution(16390343949119417091)
XLA Ops:
  40.2 10.3 %collective-permute-done.4.refs_2_ = bf16[128,2560]{1,0:T(8,128)(2,1)} collective-permute-done((bf16[128,2560]{1,0:T(8,128)(2,1)}, bf16[128,2560]{1,0:T(8,128)(2,1)}, u32[]{:S(2)}, u32[]{:S(2)}) %collective-permute-start.4) | collective-permute-done | bytes 655392 | tf_op jit(solution)/shard_map/ppermute | solution.py:48
  82.2 10.5 %shard_map.420 = (bf16[2560,1024]{1,0:T(8,128)(2,1)}, bf16[4,80,1024]{2,1,0:T(8,128)(2,1)}, bf16[4,160,256]{2,1,0:T(8,128)(2,1)}, f32[2,2560]{1,0:T(2,128)}) custom-call(bf16[4,128,2560]{2,1,0:T(8,128)(2,1)} %shard_map.416.x_ref, bf16[4,128,2560]{2,1,0:T(8,128)(2,1)} %collective-permute-done.9.xc_ref, f32[4,40,256]{2,1,0:T(8,128)} %get-tuple-element.577.cos_ref, ...), custom_call_target="tpu_custom_call" | custom-call | flops 10000000000 | tf_op jit(solution)/shard_map/pallas_call | solution.py:339
  128.2 19.0 %shard_map.424 = (bf16[4,256,320]{2,1,0:T(8,128)(2,1)}, f32[4,80,1024]{2,1,0:T(8,128)}, f32[4,1,1024]{2,1,0:T(1,128)}, bf16[4,128,2560]{2,1,0:T(8,128)(2,1)}, bf16[4,128,2560]{2,1,0:T(8,128)(2,1)}) custom-call(s32[48]{0:T(128)} %reshape.599.seen_ref, s32[12]{0:T(128)} %copy-done.67, bf16[4,80,1024]{2,1,0:T(8,128)(2,1)} %get-tuple-element.281.q_ref, ...), custom_call_target="tpu_custom_call" | custom-call | flops 10000000000 | tf_op jit(solution)/shard_map/pallas_call | solution.py:442
  191.7 17.0 %collective-permute-done.28 = bf16[128,2560]{1,0:T(8,128)(2,1)} collective-permute-done((bf16[128,2560]{1,0:T(8,128)(2,1)}, bf16[128,2560]{1,0:T(8,128)(2,1)}, u32[]{:S(2)}, u32[]{:S(2)}) %collective-permute-start.28) | collective-permute-done | bytes 655392 | tf_op jit(solution)/shard_map/ppermute | solution.py:48
  215.1 17.9 %collective-permute-done.32.refs_8_.refs_10_ = bf16[2,320,896]{2,1,0:T(8,128)(2,1)} collective-permute-done((bf16[2,320,896]{2,1,0:T(8,128)(2,1)}, bf16[2,320,896]{2,1,0:T(8,128)(2,1)}, u32[]{:S(2)}, u32[]{:S(2)}) %collective-permute-start.32) | collective-permute-done | bytes 1146912 | tf_op jit(solution)/shard_map/ppermute | solution.py:48
  245.3 8.2 %collective-permute-done.34.refs_3_ = bf16[128,2560]{1,0:T(8,128)(2,1)} collective-permute-done((bf16[128,2560]{1,0:T(8,128)(2,1)}, bf16[128,2560]{1,0:T(8,128)(2,1)}, u32[]{:S(2)}, u32[]{:S(2)}) %collective-permute-start.34) | collective-permute-done | bytes 655392 | tf_op jit(solution)/shard_map/ppermute | solution.py:48
  264.2 7.8 collective-permute-done.36.refs_9_.refs_11_
  273.2 19.8 %shard_map.433 = (bf16[2560,1024]{1,0:T(8,128)(2,1)}, bf16[4,256,896]{2,1,0:T(8,128)(2,1)}, f32[4,256,896]{2,1,0:T(8,128)}, f32[4,256,896]{2,1,0:T(8,128)}) custom-call(bf16[4,128,2560]{2,1,0:T(8,128)(2,1)} %shard_map.431.near_ref, bf16[4,128,2560]{2,1,0:T(8,128)(2,1)} %collective-permute-done.35.far_ref, ...), custom_call_target="tpu_custom_call" | custom-call | flops 10000000000 | tf_op jit(solution)/shard_map/pallas_call | solution.py:652
  314.9 10.3 %collective-permute-done.41.refs_4_.refs_5_ = bf16[2,320,896]{2,1,0:T(8,128)(2,1)} collective-permute-done((bf16[2,320,896]{2,1,0:T(8,128)(2,1)}, bf16[2,320,896]{2,1,0:T(8,128)(2,1)}, u32[]{:S(2)}, u32[]{:S(2)}) %collective-permute-start.41) | collective-permute-done | bytes 1146912 | tf_op jit(solution)/shard_map/ppermute | solution.py:48
  325.2 12.4 %shard_map.439 = (bf16[4,256,896]{2,1,0:T(8,128)(2,1)}, bf16[4,256,896]{2,1,0:T(8,128)(2,1)}) custom-call(bf16[4,128,2560]{2,1,0:T(8,128)(2,1)} %shard_map.435.near_ref, bf16[4,128,2560]{2,1,0:T(8,128)(2,1)} %collective-permute-done.40.far_ref, f32[4,256,896]{2,1,0:T(8,128)} %get-tuple-element.334.one_ref, f32[4,256,896]{2,1,0:T(8,128)} %get-tuple-element.335.two_ref, ...), custom_call_target="tpu_custom_call" | custom-call | flops 10000000000 | tf_op jit(solution)/shard_map/pallas_call | solution.py:694
  337.6 13.6 %shard_map.440 = bf16[4,128,2560]{2,1,0:T(8,128)(2,1)} custom-call(bf16[4,2,128,896]{3,2,1,0:T(8,128)(2,1)} %bitcast.186, bf16[4,2,128,896]{3,2,1,0:T(8,128)(2,1)} %bitcast.181, s32[8]{0:T(128)} %stack.64.refs_0_.refs_4_.refs_5_.refs_2_.refs_7_.refs_1_, bf16[2,320,896]{2,1,0:T(8,128)(2,1)} %maximum_select_fusion.3.refs_1_.refs_3_, ...), custom_call_target="tpu_custom_call" | custom-call | flops 10000000000 | tf_op jit(solution)/shard_map/pallas_call | solution.py:771
  361.0 14.0 %shard_map.443 = (f32[128,2560]{1,0:T(8,128)}, bf16[128,2560]{1,0:T(8,128)(2,1)}, bf16[128,2560]{1,0:T(8,128)(2,1)}, bf16[128,2560]{1,0:T(8,128)(2,1)}) custom-call(bf16[4,2,128,896]{3,2,1,0:T(8,128)(2,1)} %bitcast.188, bf16[4,2,128,896]{3,2,1,0:T(8,128)(2,1)} %bitcast.182, s32[8]{0:T(128)} %stack.64.refs_0_.refs_4_.refs_5_.refs_2_.refs_7_.refs_1_, ...), custom_call_target="tpu_custom_call" | custom-call | flops 10000000000 | tf_op jit(solution)/shard_map/pallas_call | solution.py:771
  377.0 15.2 %collective-permute-done.43 = bf16[128,2560]{1,0:T(8,128)(2,1)} collective-permute-done((bf16[128,2560]{1,0:T(8,128)(2,1)}, bf16[128,2560]{1,0:T(8,128)(2,1)}, u32[]{:S(2)}, u32[]{:S(2)}) %collective-permute-start.43) | collective-permute-done | bytes 655392 | tf_op jit(solution)/shard_map/ppermute | solution.py:48
  397.0 6.8 shard_map.445
  431.8 8.0 %collective-permute-done.48.refs_2_ = bf16[128,2560]{1,0:T(8,128)(2,1)} collective-permute-done((bf16[128,2560]{1,0:T(8,128)(2,1)}, bf16[128,2560]{1,0:T(8,128)(2,1)}, u32[]{:S(2)}, u32[]{:S(2)}) %collective-permute-start.48) | collective-permute-done | bytes 655392 | tf_op jit(solution)/shard_map/ppermute | solution.py:48
  441.7 9.9 %collective-permute-done.49.refs_3_ = bf16[128,2560]{1,0:T(8,128)(2,1)} collective-permute-done((bf16[128,2560]{1,0:T(8,128)(2,1)}, bf16[128,2560]{1,0:T(8,128)(2,1)}, u32[]{:S(2)}, u32[]{:S(2)}) %collective-permute-start.49) | collective-permute-done | bytes 655392 | tf_op jit(solution)/shard_map/ppermute | solution.py:48
  462.2 19.6 %shard_map.451 = (bf16[4,320,256]{2,1,0:T(8,128)(2,1)}, f32[4,160,256]{2,1,0:T(8,128)}, bf16[4,160,256]{2,1,0:T(8,128)(2,1)}, bf16[2,160,256]{2,1,0:T(8,128)(2,1)}, bf16[2,160,256]{2,1,0:T(8,128)(2,1)}) custom-call(s32[48]{0:T(128)} %reshape.599.seen_ref, s32[12]{0:T(128)} %copy-done.67, bf16[4,80,1024]{2,1,0:T(8,128)(2,1)} %get-tuple-element.281.q_ref, ...), custom_call_target="tpu_custom_call" | custom-call | flops 10000000000 | tf_op jit(solution)/shard_map/pallas_call | solution.py:543
  531.3 7.7 shard_map.462
  546.0 13.3 %collective-permute-done.59.refs_0_.refs_1_ = bf16[4,320,896]{2,1,0:T(8,128)(2,1)} collective-permute-done((bf16[4,320,896]{2,1,0:T(8,128)(2,1)}, bf16[4,320,896]{2,1,0:T(8,128)(2,1)}, u32[]{:S(2)}, u32[]{:S(2)}) %collective-permute-start.59) | collective-permute-done | bytes 2293792 | tf_op jit(solution)/shard_map/ppermute | solution.py:48
  589.5 8.5 %shard_map.471 = bf16[4,128,2560]{2,1,0:T(8,128)(2,1)} custom-call(bf16[4,2,128,896]{3,2,1,0:T(8,128)(2,1)} %bitcast.179, s32[8]{0:T(128)} %stack.64.refs_0_.refs_4_.refs_5_.refs_2_.refs_7_.refs_1_, bf16[2,320,896]{2,1,0:T(8,128)(2,1)} %maximum_select_fusion.5.refs_1_.refs_2_, bf16[2,320,896]{2,1,0:T(8,128)(2,1)} %collective-permute-done.38.refs_2_.refs_3_, ...), custom_call_target="tpu_custom_call" | custom-call | flops 10000000000 | tf_op jit(solution)/shard_map/pallas_call | solution.py:771
  651.8 9.5 %shard_map.478 = (f32[128,2560]{1,0:T(8,128)}, bf16[128,2560]{1,0:T(8,128)(2,1)}, bf16[128,2560]{1,0:T(8,128)(2,1)}, bf16[128,2560]{1,0:T(8,128)(2,1)}) custom-call(bf16[4,2,128,896]{3,2,1,0:T(8,128)(2,1)} %bitcast.180, s32[8]{0:T(128)} %stack.64.refs_0_.refs_4_.refs_5_.refs_2_.refs_7_.refs_1_, bf16[2,320,896]{2,1,0:T(8,128)(2,1)} %maximum_select_fusion.5.refs_1_.refs_2_, ...), custom_call_target="tpu_custom_call" | custom-call | flops 10000000000 | tf_op jit(solution)/shard_map/pallas_call | solution.py:771
  664.3 14.3 %collective-permute-done.74 = bf16[128,2560]{1,0:T(8,128)(2,1)} collective-permute-done((bf16[128,2560]{1,0:T(8,128)(2,1)}, bf16[128,2560]{1,0:T(8,128)(2,1)}, u32[]{:S(2)}, u32[]{:S(2)}) %collective-permute-start.74) | collective-permute-done | bytes 655392 | tf_op jit(solution)/shard_map/ppermute | solution.py:48
  717.6 8.4 %collective-permute-done.81 = bf16[320,320]{1,0:T(8,128)(2,1)S(1)} collective-permute-done((bf16[320,320]{1,0:T(8,128)(2,1)S(1)}, bf16[320,320]{1,0:T(8,128)(2,1)S(1)}, u32[]{:S(2)}, u32[]{:S(2)}) %collective-permute-start.81) | collective-permute-done | bytes 204832 | tf_op jit(solution)/shard_map/ppermute | solution.py:48
  762.9 10.0 %add_multiply_fusion = (f32[2,320,1792]{2,1,0:T(8,128)}, f32[2,320,1792]{2,1,0:T(8,128)}, f32[2,320,1792]{2,1,0:T(8,128)}, f32[2,320,1792]{2,1,0:T(8,128)}) fusion(f32[2,320,1792]{2,1,0:T(8,128)S(1)} %bitcast.134, f32[]{:T(128)S(6)} %min_shard_map.3, f32[2,320,1792]{2,1,0:T(8,128)S(1)} %copy-done.10, f32[2,320,1792]{2,1,0:T(8,128)} %param.33, ...), kind=kLoop, calls=%fused_computation.3 | loop fusion | flops 18350080 | bytes 36700164 | tf_op jit(solution)/shard_map/mul | solution.py:871
  (504 shorter events, 480.7 us)
Async XLA Ops:
  24.6 32.1 %collective-permute-start.6 = (bf16[2,320,482]{2,1,0:T(8,128)(2,1)}, bf16[2,320,482]{2,1,0:T(8,128)(2,1)}, u32[]{:S(2)}, u32[]{:S(2)}) collective-permute-start(bf16[2,320,482]{2,1,0:T(8,128)(2,1)} %maximum_select_fusion.8.refs_1_.refs_2_), channel_id=1, source_target_pairs={{0,16},{1,17},{2,18},{3,19},{4,20},{5,21},{6,22},{7,23},{8,24},{9,... | collective-permute-start | bytes 1850888 | tf_op jit(solution)/shard_map/ppermute | solution.py:48
  59.9 36.7 %collective-permute-start.13 = (bf16[2,320,320]{2,1,0:T(8,128)(2,1)}, bf16[2,320,320]{2,1,0:T(8,128)(2,1)}, u32[]{:S(2)}, u32[]{:S(2)}) collective-permute-start(bf16[2,320,320]{2,1,0:T(8,128)(2,1)} %maximum_select_fusion.9.refs_5_), channel_id=1, source_target_pairs={{0,16},{1,17},{2,18},{3,19},{4,20},{5,21},{6,22},{7,23},{8,24},{9,... | collective-permute-start | bytes 1228808 | tf_op jit(solution)/shard_map/ppermute | solution.py:48
  118.0 30.7 %collective-permute-start.23 = (bf16[2,320,896]{2,1,0:T(8,128)(2,1)}, bf16[2,320,896]{2,1,0:T(8,128)(2,1)}, u32[]{:S(2)}, u32[]{:S(2)}) collective-permute-start(bf16[2,320,896]{2,1,0:T(8,128)(2,1)} %maximum_select_fusion.3.refs_1_.refs_3_), channel_id=1, source_target_pairs={{0,4},{1,5},{2,6},{3,7},{4,0},{5,1},{6,2},{7,3},{8,12},{9,13},{10,... | collective-permute-start | bytes 3440648 | tf_op jit(solution)/shard_map/ppermute | solution.py:48
  119.0 51.0 %collective-permute-start.25 = (bf16[2,320,896]{2,1,0:T(8,128)(2,1)}, bf16[2,320,896]{2,1,0:T(8,128)(2,1)}, u32[]{:S(2)}, u32[]{:S(2)}) collective-permute-start(bf16[2,320,896]{2,1,0:T(8,128)(2,1)} %maximum_select_fusion.3.refs_1_.refs_3_), channel_id=1, source_target_pairs={{0,16},{1,17},{2,18},{3,19},{4,20},{5,21},{6,22},{7,23},{8,24},{9,... | collective-permute-start | bytes 3440648 | tf_op jit(solution)/shard_map/ppermute | solution.py:48
  123.3 40.7 %collective-permute-start.26 = (bf16[128,2560]{1,0:T(8,128)(2,1)}, bf16[128,2560]{1,0:T(8,128)(2,1)}, u32[]{:S(2)}, u32[]{:S(2)}) collective-permute-start(bf16[128,2560]{1,0:T(8,128)(2,1)} %refs_0_.1), channel_id=1, source_target_pairs={{0,8},{1,9},{2,10},{3,11},{4,12},{5,13},{6,14},{7,15},{8,0},{9,1},... | collective-permute-start | bytes 1966088 | tf_op jit(solution)/shard_map/ppermute | solution.py:48
  180.5 52.5 %collective-permute-start.32 = (bf16[2,320,896]{2,1,0:T(8,128)(2,1)}, bf16[2,320,896]{2,1,0:T(8,128)(2,1)}, u32[]{:S(2)}, u32[]{:S(2)}) collective-permute-start(bf16[2,320,896]{2,1,0:T(8,128)(2,1)} %maximum_select_fusion.4.refs_6_.refs_8_), channel_id=1, source_target_pairs={{0,16},{1,17},{2,18},{3,19},{4,20},{5,21},{6,22},{7,23},{8,24},{9,... | collective-permute-start | bytes 3440648 | tf_op jit(solution)/shard_map/ppermute | solution.py:48
  183.5 49.5 %collective-permute-start.33 = (bf16[2,320,896]{2,1,0:T(8,128)(2,1)}, bf16[2,320,896]{2,1,0:T(8,128)(2,1)}, u32[]{:S(2)}, u32[]{:S(2)}) collective-permute-start(bf16[2,320,896]{2,1,0:T(8,128)(2,1)} %collective-permute-done.25.refs_3_.refs_5_), channel_id=1, source_target_pairs={{0,4},{1,5},{2,6},{3,7},{4,0},{5,1},{6,2},{7,3},{8,12},{9,13},{10,... | collective-permute-start | bytes 3440648 | tf_op jit(solution)/shard_map/ppermute | solution.py:48
  242.2 50.8 %collective-permute-start.37 = (bf16[2,320,896]{2,1,0:T(8,128)(2,1)}, bf16[2,320,896]{2,1,0:T(8,128)(2,1)}, u32[]{:S(2)}, u32[]{:S(2)}) collective-permute-start(bf16[2,320,896]{2,1,0:T(8,128)(2,1)} %maximum_select_fusion.5.refs_1_.refs_2_), channel_id=1, source_target_pairs={{0,16},{1,17},{2,18},{3,19},{4,20},{5,21},{6,22},{7,23},{8,24},{9,... | collective-permute-start | bytes 3440648 | tf_op jit(solution)/shard_map/ppermute | solution.py:48
  253.5 39.6 %collective-permute-start.38 = (bf16[2,320,896]{2,1,0:T(8,128)(2,1)}, bf16[2,320,896]{2,1,0:T(8,128)(2,1)}, u32[]{:S(2)}, u32[]{:S(2)}) collective-permute-start(bf16[2,320,896]{2,1,0:T(8,128)(2,1)} %maximum_select_fusion.5.refs_1_.refs_2_), channel_id=1, source_target_pairs={{0,4},{1,5},{2,6},{3,7},{4,0},{5,1},{6,2},{7,3},{8,12},{9,13},{10,... | collective-permute-start | bytes 3440648 | tf_op jit(solution)/shard_map/ppermute | solution.py:48
  257.5 35.6 %collective-permute-start.39 = (bf16[128,2560]{1,0:T(8,128)(2,1)}, bf16[128,2560]{1,0:T(8,128)(2,1)}, u32[]{:S(2)}, u32[]{:S(2)}) collective-permute-start(bf16[128,2560]{1,0:T(8,128)(2,1)} %collective-permute-done.26.refs_2_), channel_id=1, source_target_pairs={{0,2},{1,3},{2,0},{3,1},{4,6},{5,7},{6,4},{7,5},{8,10},{9,11},{10,... | collective-permute-start | bytes 1966088 | tf_op jit(solution)/shard_map/ppermute | solution.py:48
  352.6 52.6 %collective-permute-start.46 = (bf16[4,320,896]{2,1,0:T(8,128)(2,1)}, bf16[4,320,896]{2,1,0:T(8,128)(2,1)}, u32[]{:S(2)}, u32[]{:S(2)}) collective-permute-start(bf16[4,320,896]{2,1,0:T(8,128)(2,1)} %shard_map.437), channel_id=1, source_target_pairs={{0,4},{1,5},{2,6},{3,7},{4,0},{5,1},{6,2},{7,3},{8,12},{9,13},{10,... | collective-permute-start | bytes 6881288 | tf_op jit(solution)/shard_map/ppermute | solution.py:48
  420.3 61.5 %collective-permute-start.51 = (bf16[4,320,896]{2,1,0:T(8,128)(2,1)}, bf16[4,320,896]{2,1,0:T(8,128)(2,1)}, u32[]{:S(2)}, u32[]{:S(2)}) collective-permute-start(bf16[4,320,896]{2,1,0:T(8,128)(2,1)} %shard_map.441), channel_id=1, source_target_pairs={{0,4},{1,5},{2,6},{3,7},{4,0},{5,1},{6,2},{7,3},{8,12},{9,13},{10,... | collective-permute-start | bytes 6881288 | tf_op jit(solution)/shard_map/ppermute | solution.py:48
  427.4 54.4 %collective-permute-start.52 = (bf16[2,320,896]{2,1,0:T(8,128)(2,1)}, bf16[2,320,896]{2,1,0:T(8,128)(2,1)}, u32[]{:S(2)}, u32[]{:S(2)}) collective-permute-start(bf16[2,320,896]{2,1,0:T(8,128)(2,1)} %shard_map.452), channel_id=1, source_target_pairs={{0,16},{1,17},{2,18},{3,19},{4,20},{5,21},{6,22},{7,23},{8,24},{9,... | collective-permute-start | bytes 3440648 | tf_op jit(solution)/shard_map/ppermute | solution.py:48
  503.4 55.9 %collective-permute-start.59 = (bf16[4,320,896]{2,1,0:T(8,128)(2,1)}, bf16[4,320,896]{2,1,0:T(8,128)(2,1)}, u32[]{:S(2)}, u32[]{:S(2)}) collective-permute-start(bf16[4,320,896]{2,1,0:T(8,128)(2,1)} %shard_map.445), channel_id=1, source_target_pairs={{0,4},{1,5},{2,6},{3,7},{4,0},{5,1},{6,2},{7,3},{8,12},{9,13},{10,... | collective-permute-start | bytes 6881288 | tf_op jit(solution)/shard_map/ppermute | solution.py:48
  508.3 72.6 %collective-permute-start.63 = (bf16[2,320,896]{2,1,0:T(8,128)(2,1)}, bf16[2,320,896]{2,1,0:T(8,128)(2,1)}, u32[]{:S(2)}, u32[]{:S(2)}) collective-permute-start(bf16[2,320,896]{2,1,0:T(8,128)(2,1)} %shard_map.454), channel_id=1, source_target_pairs={{0,16},{1,17},{2,18},{3,19},{4,20},{5,21},{6,22},{7,23},{8,24},{9,... | collective-permute-start | bytes 3440648 | tf_op jit(solution)/shard_map/ppermute | solution.py:48
  540.8 40.1 %collective-permute-start.64 = (bf16[4,320,320]{2,1,0:T(8,128)(2,1)}, bf16[4,320,320]{2,1,0:T(8,128)(2,1)}, u32[]{:S(2)}, u32[]{:S(2)}) collective-permute-start(bf16[4,320,320]{2,1,0:T(8,128)(2,1)} %shard_map.460), channel_id=1, source_target_pairs={{0,4},{1,5},{2,6},{3,7},{4,0},{5,1},{6,2},{7,3},{8,12},{9,13},{10,... | collective-permute-start | bytes 2457608 | tf_op jit(solution)/shard_map/ppermute | solution.py:48
  568.4 65.1 %collective-permute-start.60 = (bf16[2,320,896]{2,1,0:T(8,128)(2,1)}, bf16[2,320,896]{2,1,0:T(8,128)(2,1)}, u32[]{:S(2)}, u32[]{:S(2)}) collective-permute-start(bf16[2,320,896]{2,1,0:T(8,128)(2,1)} %shard_map.465), channel_id=1, source_target_pairs={{0,16},{1,17},{2,18},{3,19},{4,20},{5,21},{6,22},{7,23},{8,24},{9,... | collective-permute-start | bytes 3440648 | tf_op jit(solution)/shard_map/ppermute | solution.py:48
  587.2 35.9 %collective-permute-start.69 = (bf16[4,320,482]{2,1,0:T(8,128)(2,1)}, bf16[4,320,482]{2,1,0:T(8,128)(2,1)}, u32[]{:S(2)}, u32[]{:S(2)}) collective-permute-start(bf16[4,320,482]{2,1,0:T(8,128)(2,1)} %shard_map.463), channel_id=1, source_target_pairs={{0,4},{1,5},{2,6},{3,7},{4,0},{5,1},{6,2},{7,3},{8,12},{9,13},{10,... | collective-permute-start | bytes 3701768 | tf_op jit(solution)/shard_map/ppermute | solution.py:48
  587.5 35.6 %collective-permute-start.70 = (bf16[320,896]{1,0:T(8,128)(2,1)}, bf16[320,896]{1,0:T(8,128)(2,1)}, u32[]{:S(2)}, u32[]{:S(2)}) collective-permute-start(bf16[320,896]{1,0:T(8,128)(2,1)} %fusion.16), channel_id=1, source_target_pairs={{0,8},{1,9},{2,10},{3,11},{4,12},{5,13},{6,14},{7,15},{8,0},{9,1},... | collective-permute-start | bytes 1720328 | tf_op jit(solution)/shard_map/ppermute | solution.py:48
  628.4 65.9 %collective-permute-start.73 = (bf16[2,320,482]{2,1,0:T(8,128)(2,1)}, bf16[2,320,482]{2,1,0:T(8,128)(2,1)}, u32[]{:S(2)}, u32[]{:S(2)}) collective-permute-start(bf16[2,320,482]{2,1,0:T(8,128)(2,1)} %shard_map.479), channel_id=1, source_target_pairs={{0,16},{1,17},{2,18},{3,19},{4,20},{5,21},{6,22},{7,23},{8,24},{9,... | collective-permute-start | bytes 1850888 | tf_op jit(solution)/shard_map/ppermute | solution.py:48
  629.6 54.6 %collective-permute-start.75 = (bf16[2,320,320]{2,1,0:T(8,128)(2,1)}, bf16[2,320,320]{2,1,0:T(8,128)(2,1)}, u32[]{:S(2)}, u32[]{:S(2)}) collective-permute-start(bf16[2,320,320]{2,1,0:T(8,128)(2,1)} %shard_map.472), channel_id=1, source_target_pairs={{0,16},{1,17},{2,18},{3,19},{4,20},{5,21},{6,22},{7,23},{8,24},{9,... | collective-permute-start | bytes 1228808 | tf_op jit(solution)/shard_map/ppermute | solution.py:48
  651.1 43.3 %collective-permute-start.77 = (bf16[320,896]{1,0:T(8,128)(2,1)}, bf16[320,896]{1,0:T(8,128)(2,1)}, u32[]{:S(2)}, u32[]{:S(2)}) collective-permute-start(bf16[320,896]{1,0:T(8,128)(2,1)} %fusion.18), channel_id=1, source_target_pairs={{0,8},{1,9},{2,10},{3,11},{4,12},{5,13},{6,14},{7,15},{8,0},{9,1},... | collective-permute-start | bytes 1720328 | tf_op jit(solution)/shard_map/ppermute | solution.py:48
  680.5 45.5 %collective-permute-start.82 = (bf16[128,2560]{1,0:T(8,128)(2,1)}, bf16[128,2560]{1,0:T(8,128)(2,1)}, u32[]{:S(2)}, u32[]{:S(2)}) collective-permute-start(bf16[128,2560]{1,0:T(8,128)(2,1)} %get-tuple-element.448), channel_id=1, source_target_pairs={{0,2},{1,3},{2,0},{3,1},{4,6},{5,7},{6,4},{7,5},{8,10},{9,11},{10,... | collective-permute-start | bytes 1966088 | tf_op jit(solution)/shard_map/ppermute | solution.py:48
  684.2 41.9 %collective-permute-start.83 = (bf16[128,2560]{1,0:T(8,128)(2,1)}, bf16[128,2560]{1,0:T(8,128)(2,1)}, u32[]{:S(2)}, u32[]{:S(2)}) collective-permute-start(bf16[128,2560]{1,0:T(8,128)(2,1)} %add_convert_fusion.1), channel_id=1, source_target_pairs={{0,8},{1,9},{2,10},{3,11},{4,12},{5,13},{6,14},{7,15},{8,0},{9,1},... | collective-permute-start | bytes 1966088 | tf_op jit(solution)/shard_map/ppermute | solution.py:48
  (147 other events, 1510.1 us)

commit v5 on v4

--- a/solution.py
+++ b/solution.py
@@ -137,11 +137,9 @@
 
 
 def sum_rest(value):
-    ring = lax.axis_size("dp") // 4
-    for step in (hop_low, hop_y):
-        value = value + step(value)
+    value = value + hop_y(value)
     travel = value
-    for _ in range(1, ring):
+    for _ in range(1, lax.axis_size("dp") // 4):
         travel = hop_ring(travel)
         value = value + travel
     return value
@@ -279,7 +277,7 @@
 
 def pack(*parts):
     rows, width = parts[0].shape[-2:]
-    step = width // 4
+    step = width // 2
     specs, number = [], 0
     for part in parts:
         if part.ndim == 2:
@@ -290,7 +288,7 @@
             number += part.shape[0]
     return call(
         pack_body,
-        (4,),
+        (2,),
         specs,
         pl.BlockSpec((number, rows, step), lambda n: (0, 0, n)),
         shape((number, rows, width), parts[0].dtype),
@@ -718,7 +716,7 @@
 
 def combine(near, got):
     blocks, per, width = near.shape
-    step = 512
+    step = width // 2
     spec = pl.BlockSpec((blocks, per, step), lambda n: (0, 0, n))
     out_specs, out_shape = block_outputs(per, width, step)
     return call(combine_body, (width // step,), [spec, spec], out_specs, out_shape)(near, got)
@@ -1218,10 +1216,10 @@
     totals = sums + last_row * (qkv_square / width)
     totals = totals + hop_core(totals)
 
-    from_x = hop_x(totals)
-    from_x, qkv_other, output_other, fx, fz = pin(from_x, qkv_other, output_other, fx, fz)
+    totals = sum_rest(totals + hop_x(totals))
+    totals, qkv_other, output_other, fx, fz = pin(totals, qkv_other, output_other, fx, fz)
     block_out = (middle + arrived(f_own, fx, fz)).astype(low_type)
-    totals = sum_rest(totals + from_x)
+    totals = totals + hop_low(totals)
     gain_total = totals[:2]
     grad_norm = jnp.sqrt(totals[2, 0] * width + jnp.sum(gain_total * gain_total))
     def joined(mine, other, start, stop):

time: 791 us -> 780 us (0.986)
  transfers between devices with their start and end apart: 87 -> 87, of which waited for: 36 -> 36; matrix products, arithmetic and copies ran while one was open for 10% -> 11% of each run, Pallas kernels for 37% -> 37%
where the time goes in v5:
time: 780 us; the launch traced here: 771 us
  Pallas kernels  315 us (40%)
  waiting for transfers between devices  218 us (28%)
  starting transfers between devices  97.7 us (13%)
  other arithmetic  97 us (12%)
  local copies, waits for them, and re-layouts  35.2 us (5%)
  between operations  7.98 us (1%)
    ppermute x87, waiting for transfers between devices, hop(): return lax.ppermute(block, AXES, route)  218 us
    ppermute x87, starting transfers between devices, hop(): return lax.ppermute(block, AXES, route)  97.7 us
    pallas_call x15, Pallas kernels, weight_rows(): pl.pallas_call(functools.partial(weight_body, len(addends)), grid_spec=pl...  81.2 us
    pallas_call x6, Pallas kernels, branch(): call(functools.partial(branch_body, len(pairs), weight.count(), got is no...  60.1 us
    pallas_call x38, Pallas kernels, __call__(): pl.pallas_call(keep_body, out_shape=jax.ShapeDtypeStruct(held.shape, held...  48.6 us
    mul x5, other arithmetic, adamw(): -learn_rate  25 us
    pallas_call x1, Pallas kernels, ffn(): call(functools.partial(ffn_body, gate_weight.count()), (tiles,), [tile_of...  19.8 us
    pallas_call x1, Pallas kernels, attend_back(): call(functools.partial(attend_back_body, weight.count()), (tiles,), [smem...  19.6 us
  transfers between devices with their start and end apart: 87, of which 36 were waited for; matrix products, arithmetic and copies ran while one was open for 11% of the time, Pallas kernels for 37%

profile of v5, /device:TPU:0, one launch (start us, length us, event | category | flops | bytes accessed | tf_op | source)
XLA Modules:
  0.0 770.6 jit_solution(7362586678949106214)
XLA Ops:
  40.3 10.3 %collective-permute-done.4.refs_2_ = bf16[128,2560]{1,0:T(8,128)(2,1)} collective-permute-done((bf16[128,2560]{1,0:T(8,128)(2,1)}, bf16[128,2560]{1,0:T(8,128)(2,1)}, u32[]{:S(2)}, u32[]{:S(2)}) %collective-permute-start.4) | collective-permute-done | bytes 655392 | tf_op jit(solution)/shard_map/ppermute | solution.py:48
  82.2 10.5 %shard_map.420 = (bf16[2560,1024]{1,0:T(8,128)(2,1)}, bf16[4,80,1024]{2,1,0:T(8,128)(2,1)}, bf16[4,160,256]{2,1,0:T(8,128)(2,1)}, f32[2,2560]{1,0:T(2,128)}) custom-call(bf16[4,128,2560]{2,1,0:T(8,128)(2,1)} %shard_map.416.x_ref, bf16[4,128,2560]{2,1,0:T(8,128)(2,1)} %collective-permute-done.9.xc_ref, f32[4,40,256]{2,1,0:T(8,128)} %get-tuple-element.577.cos_ref, ...), custom_call_target="tpu_custom_call" | custom-call | flops 10000000000 | tf_op jit(solution)/shard_map/pallas_call | solution.py:337
  128.2 19.0 %shard_map.424 = (bf16[4,256,320]{2,1,0:T(8,128)(2,1)}, f32[4,80,1024]{2,1,0:T(8,128)}, f32[4,1,1024]{2,1,0:T(1,128)}, bf16[4,128,2560]{2,1,0:T(8,128)(2,1)}, bf16[4,128,2560]{2,1,0:T(8,128)(2,1)}) custom-call(s32[48]{0:T(128)} %reshape.599.seen_ref, s32[12]{0:T(128)} %copy-done.64, bf16[4,80,1024]{2,1,0:T(8,128)(2,1)} %get-tuple-element.281.q_ref, ...), custom_call_target="tpu_custom_call" | custom-call | flops 10000000000 | tf_op jit(solution)/shard_map/pallas_call | solution.py:440
  162.2 7.8 %collective-permute-done.25.refs_3_.refs_5_ = bf16[2,320,896]{2,1,0:T(8,128)(2,1)} collective-permute-done((bf16[2,320,896]{2,1,0:T(8,128)(2,1)}, bf16[2,320,896]{2,1,0:T(8,128)(2,1)}, u32[]{:S(2)}, u32[]{:S(2)}) %collective-permute-start.25) | collective-permute-done | bytes 1146912 | tf_op jit(solution)/shard_map/ppermute | solution.py:48
  189.9 17.0 %collective-permute-done.28 = bf16[128,2560]{1,0:T(8,128)(2,1)} collective-permute-done((bf16[128,2560]{1,0:T(8,128)(2,1)}, bf16[128,2560]{1,0:T(8,128)(2,1)}, u32[]{:S(2)}, u32[]{:S(2)}) %collective-permute-start.28) | collective-permute-done | bytes 655392 | tf_op jit(solution)/shard_map/ppermute | solution.py:48
  213.3 17.9 %collective-permute-done.32.refs_8_.refs_10_ = bf16[2,320,896]{2,1,0:T(8,128)(2,1)} collective-permute-done((bf16[2,320,896]{2,1,0:T(8,128)(2,1)}, bf16[2,320,896]{2,1,0:T(8,128)(2,1)}, u32[]{:S(2)}, u32[]{:S(2)}) %collective-permute-start.32) | collective-permute-done | bytes 1146912 | tf_op jit(solution)/shard_map/ppermute | solution.py:48
  243.5 8.2 %collective-permute-done.34.refs_3_ = bf16[128,2560]{1,0:T(8,128)(2,1)} collective-permute-done((bf16[128,2560]{1,0:T(8,128)(2,1)}, bf16[128,2560]{1,0:T(8,128)(2,1)}, u32[]{:S(2)}, u32[]{:S(2)}) %collective-permute-start.34) | collective-permute-done | bytes 655392 | tf_op jit(solution)/shard_map/ppermute | solution.py:48
  261.3 8.9 %collective-permute-done.36.refs_9_.refs_11_ = bf16[2,320,896]{2,1,0:T(8,128)(2,1)} collective-permute-done((bf16[2,320,896]{2,1,0:T(8,128)(2,1)}, bf16[2,320,896]{2,1,0:T(8,128)(2,1)}, u32[]{:S(2)}, u32[]{:S(2)}) %collective-permute-start.36) | collective-permute-done | bytes 1146912 | tf_op jit(solution)/shard_map/ppermute | solution.py:48
  271.4 19.8 %shard_map.433 = (bf16[2560,1024]{1,0:T(8,128)(2,1)}, bf16[4,256,896]{2,1,0:T(8,128)(2,1)}, f32[4,256,896]{2,1,0:T(8,128)}, f32[4,256,896]{2,1,0:T(8,128)}) custom-call(bf16[4,128,2560]{2,1,0:T(8,128)(2,1)} %shard_map.431.near_ref, bf16[4,128,2560]{2,1,0:T(8,128)(2,1)} %collective-permute-done.35.far_ref, ...), custom_call_target="tpu_custom_call" | custom-call | flops 10000000000 | tf_op jit(solution)/shard_map/pallas_call | solution.py:650
  311.9 10.3 %collective-permute-done.41.refs_4_.refs_5_ = bf16[2,320,896]{2,1,0:T(8,128)(2,1)} collective-permute-done((bf16[2,320,896]{2,1,0:T(8,128)(2,1)}, bf16[2,320,896]{2,1,0:T(8,128)(2,1)}, u32[]{:S(2)}, u32[]{:S(2)}) %collective-permute-start.41) | collective-permute-done | bytes 1146912 | tf_op jit(solution)/shard_map/ppermute | solution.py:48
  322.3 12.4 %shard_map.439 = (bf16[4,256,896]{2,1,0:T(8,128)(2,1)}, bf16[4,256,896]{2,1,0:T(8,128)(2,1)}) custom-call(bf16[4,128,2560]{2,1,0:T(8,128)(2,1)} %shard_map.435.near_ref, bf16[4,128,2560]{2,1,0:T(8,128)(2,1)} %collective-permute-done.40.far_ref, f32[4,256,896]{2,1,0:T(8,128)} %get-tuple-element.334.one_ref, f32[4,256,896]{2,1,0:T(8,128)} %get-tuple-element.335.two_ref, ...), custom_call_target="tpu_custom_call" | custom-call | flops 10000000000 | tf_op jit(solution)/shard_map/pallas_call | solution.py:692
  334.7 13.6 %shard_map.440 = bf16[4,128,2560]{2,1,0:T(8,128)(2,1)} custom-call(bf16[4,2,128,896]{3,2,1,0:T(8,128)(2,1)} %bitcast.186, bf16[4,2,128,896]{3,2,1,0:T(8,128)(2,1)} %bitcast.181, s32[8]{0:T(128)} %stack.64.refs_0_.refs_4_.refs_5_.refs_2_.refs_7_.refs_1_, bf16[2,320,896]{2,1,0:T(8,128)(2,1)} %maximum_select_fusion.3.refs_1_.refs_3_, ...), custom_call_target="tpu_custom_call" | custom-call | flops 10000000000 | tf_op jit(solution)/shard_map/pallas_call | solution.py:769
  358.1 14.0 %shard_map.443 = (f32[128,2560]{1,0:T(8,128)}, bf16[128,2560]{1,0:T(8,128)(2,1)}, bf16[128,2560]{1,0:T(8,128)(2,1)}, bf16[128,2560]{1,0:T(8,128)(2,1)}) custom-call(bf16[4,2,128,896]{3,2,1,0:T(8,128)(2,1)} %bitcast.188, bf16[4,2,128,896]{3,2,1,0:T(8,128)(2,1)} %bitcast.182, s32[8]{0:T(128)} %stack.64.refs_0_.refs_4_.refs_5_.refs_2_.refs_7_.refs_1_, ...), custom_call_target="tpu_custom_call" | custom-call | flops 10000000000 | tf_op jit(solution)/shard_map/pallas_call | solution.py:769
  374.0 15.3 %collective-permute-done.43 = bf16[128,2560]{1,0:T(8,128)(2,1)} collective-permute-done((bf16[128,2560]{1,0:T(8,128)(2,1)}, bf16[128,2560]{1,0:T(8,128)(2,1)}, u32[]{:S(2)}, u32[]{:S(2)}) %collective-permute-start.43) | collective-permute-done | bytes 655392 | tf_op jit(solution)/shard_map/ppermute | solution.py:48
  394.1 6.8 shard_map.445
  428.8 8.1 %collective-permute-done.48.refs_2_ = bf16[128,2560]{1,0:T(8,128)(2,1)} collective-permute-done((bf16[128,2560]{1,0:T(8,128)(2,1)}, bf16[128,2560]{1,0:T(8,128)(2,1)}, u32[]{:S(2)}, u32[]{:S(2)}) %collective-permute-start.48) | collective-permute-done | bytes 655392 | tf_op jit(solution)/shard_map/ppermute | solution.py:48
  438.7 10.1 %collective-permute-done.49.refs_3_ = bf16[128,2560]{1,0:T(8,128)(2,1)} collective-permute-done((bf16[128,2560]{1,0:T(8,128)(2,1)}, bf16[128,2560]{1,0:T(8,128)(2,1)}, u32[]{:S(2)}, u32[]{:S(2)}) %collective-permute-start.49) | collective-permute-done | bytes 655392 | tf_op jit(solution)/shard_map/ppermute | solution.py:48
  458.2 19.6 %shard_map.451 = (bf16[4,320,256]{2,1,0:T(8,128)(2,1)}, f32[4,160,256]{2,1,0:T(8,128)}, bf16[4,160,256]{2,1,0:T(8,128)(2,1)}, bf16[2,160,256]{2,1,0:T(8,128)(2,1)}, bf16[2,160,256]{2,1,0:T(8,128)(2,1)}) custom-call(s32[48]{0:T(128)} %reshape.599.seen_ref, s32[12]{0:T(128)} %copy-done.64, bf16[4,80,1024]{2,1,0:T(8,128)(2,1)} %get-tuple-element.281.q_ref, ...), custom_call_target="tpu_custom_call" | custom-call | flops 10000000000 | tf_op jit(solution)/shard_map/pallas_call | solution.py:541
  527.3 7.7 %shard_map.462 = (f32[128,2560]{1,0:T(8,128)}, bf16[128,2560]{1,0:T(8,128)(2,1)}, bf16[128,2560]{1,0:T(8,128)(2,1)}, bf16[128,2560]{1,0:T(8,128)(2,1)}) custom-call(bf16[4,2,128,482]{3,2,1,0:T(8,128)(2,1)} %bitcast.192, s32[8]{0:T(128)} %stack.64.refs_0_.refs_4_.refs_5_.refs_2_.refs_7_.refs_1_, bf16[2,320,482]{2,1,0:T(8,128)(2,1)} %maximum_select_fusion.8.refs_1_.refs_2_, ...), custom_call_target="tpu_custom_call" | custom-call | flops 10000000000 | tf_op jit(solution)/shard_map/pallas_call | solution.py:769
  542.0 13.3 %collective-permute-done.59.refs_0_.refs_1_ = bf16[4,320,896]{2,1,0:T(8,128)(2,1)} collective-permute-done((bf16[4,320,896]{2,1,0:T(8,128)(2,1)}, bf16[4,320,896]{2,1,0:T(8,128)(2,1)}, u32[]{:S(2)}, u32[]{:S(2)}) %collective-permute-start.59) | collective-permute-done | bytes 2293792 | tf_op jit(solution)/shard_map/ppermute | solution.py:48
  585.5 8.5 %shard_map.471 = bf16[4,128,2560]{2,1,0:T(8,128)(2,1)} custom-call(bf16[4,2,128,896]{3,2,1,0:T(8,128)(2,1)} %bitcast.179, s32[8]{0:T(128)} %stack.64.refs_0_.refs_4_.refs_5_.refs_2_.refs_7_.refs_1_, bf16[2,320,896]{2,1,0:T(8,128)(2,1)} %maximum_select_fusion.5.refs_1_.refs_2_, bf16[2,320,896]{2,1,0:T(8,128)(2,1)} %collective-permute-done.38.refs_2_.refs_3_, ...), custom_call_target="tpu_custom_call" | custom-call | flops 10000000000 | tf_op jit(solution)/shard_map/pallas_call | solution.py:769
  647.7 9.5 %shard_map.478 = (f32[128,2560]{1,0:T(8,128)}, bf16[128,2560]{1,0:T(8,128)(2,1)}, bf16[128,2560]{1,0:T(8,128)(2,1)}, bf16[128,2560]{1,0:T(8,128)(2,1)}) custom-call(bf16[4,2,128,896]{3,2,1,0:T(8,128)(2,1)} %bitcast.180, s32[8]{0:T(128)} %stack.64.refs_0_.refs_4_.refs_5_.refs_2_.refs_7_.refs_1_, bf16[2,320,896]{2,1,0:T(8,128)(2,1)} %maximum_select_fusion.5.refs_1_.refs_2_, ...), custom_call_target="tpu_custom_call" | custom-call | flops 10000000000 | tf_op jit(solution)/shard_map/pallas_call | solution.py:769
  660.2 14.3 %collective-permute-done.74 = bf16[128,2560]{1,0:T(8,128)(2,1)} collective-permute-done((bf16[128,2560]{1,0:T(8,128)(2,1)}, bf16[128,2560]{1,0:T(8,128)(2,1)}, u32[]{:S(2)}, u32[]{:S(2)}) %collective-permute-start.74) | collective-permute-done | bytes 655392 | tf_op jit(solution)/shard_map/ppermute | solution.py:48
  752.7 10.0 %add_multiply_fusion = (f32[2,320,1792]{2,1,0:T(8,128)}, f32[2,320,1792]{2,1,0:T(8,128)}, f32[2,320,1792]{2,1,0:T(8,128)}, f32[2,320,1792]{2,1,0:T(8,128)}) fusion(f32[2,320,1792]{2,1,0:T(8,128)S(1)} %bitcast.134, f32[]{:T(128)S(6)} %min_shard_map.3, f32[2,320,1792]{2,1,0:T(8,128)S(1)} %copy-done.9, f32[2,320,1792]{2,1,0:T(8,128)} %param.33, ...), kind=kLoop, calls=%fused_computation.3 | loop fusion | flops 18350080 | bytes 36700164 | tf_op jit(solution)/shard_map/mul | solution.py:869
  (498 shorter events, 469.6 us)
Async XLA Ops:
  24.6 32.1 %collective-permute-start.6 = (bf16[2,320,482]{2,1,0:T(8,128)(2,1)}, bf16[2,320,482]{2,1,0:T(8,128)(2,1)}, u32[]{:S(2)}, u32[]{:S(2)}) collective-permute-start(bf16[2,320,482]{2,1,0:T(8,128)(2,1)} %maximum_select_fusion.8.refs_1_.refs_2_), channel_id=1, source_target_pairs={{0,16},{1,17},{2,18},{3,19},{4,20},{5,21},{6,22},{7,23},{8,24},{9,... | collective-permute-start | bytes 1850888 | tf_op jit(solution)/shard_map/ppermute | solution.py:48
  59.9 36.7 %collective-permute-start.13 = (bf16[2,320,320]{2,1,0:T(8,128)(2,1)}, bf16[2,320,320]{2,1,0:T(8,128)(2,1)}, u32[]{:S(2)}, u32[]{:S(2)}) collective-permute-start(bf16[2,320,320]{2,1,0:T(8,128)(2,1)} %maximum_select_fusion.9.refs_5_), channel_id=1, source_target_pairs={{0,16},{1,17},{2,18},{3,19},{4,20},{5,21},{6,22},{7,23},{8,24},{9,... | collective-permute-start | bytes 1228808 | tf_op jit(solution)/shard_map/ppermute | solution.py:48
  118.0 30.7 %collective-permute-start.23 = (bf16[2,320,896]{2,1,0:T(8,128)(2,1)}, bf16[2,320,896]{2,1,0:T(8,128)(2,1)}, u32[]{:S(2)}, u32[]{:S(2)}) collective-permute-start(bf16[2,320,896]{2,1,0:T(8,128)(2,1)} %maximum_select_fusion.3.refs_1_.refs_3_), channel_id=1, source_target_pairs={{0,4},{1,5},{2,6},{3,7},{4,0},{5,1},{6,2},{7,3},{8,12},{9,13},{10,... | collective-permute-start | bytes 3440648 | tf_op jit(solution)/shard_map/ppermute | solution.py:48
  119.0 50.9 %collective-permute-start.25 = (bf16[2,320,896]{2,1,0:T(8,128)(2,1)}, bf16[2,320,896]{2,1,0:T(8,128)(2,1)}, u32[]{:S(2)}, u32[]{:S(2)}) collective-permute-start(bf16[2,320,896]{2,1,0:T(8,128)(2,1)} %maximum_select_fusion.3.refs_1_.refs_3_), channel_id=1, source_target_pairs={{0,16},{1,17},{2,18},{3,19},{4,20},{5,21},{6,22},{7,23},{8,24},{9,... | collective-permute-start | bytes 3440648 | tf_op jit(solution)/shard_map/ppermute | solution.py:48
  123.3 38.9 %collective-permute-start.26 = (bf16[128,2560]{1,0:T(8,128)(2,1)}, bf16[128,2560]{1,0:T(8,128)(2,1)}, u32[]{:S(2)}, u32[]{:S(2)}) collective-permute-start(bf16[128,2560]{1,0:T(8,128)(2,1)} %refs_0_.1), channel_id=1, source_target_pairs={{0,8},{1,9},{2,10},{3,11},{4,12},{5,13},{6,14},{7,15},{8,0},{9,1},... | collective-permute-start | bytes 1966088 | tf_op jit(solution)/shard_map/ppermute | solution.py:48
  178.7 52.5 %collective-permute-start.32 = (bf16[2,320,896]{2,1,0:T(8,128)(2,1)}, bf16[2,320,896]{2,1,0:T(8,128)(2,1)}, u32[]{:S(2)}, u32[]{:S(2)}) collective-permute-start(bf16[2,320,896]{2,1,0:T(8,128)(2,1)} %maximum_select_fusion.4.refs_6_.refs_8_), channel_id=1, source_target_pairs={{0,16},{1,17},{2,18},{3,19},{4,20},{5,21},{6,22},{7,23},{8,24},{9,... | collective-permute-start | bytes 3440648 | tf_op jit(solution)/shard_map/ppermute | solution.py:48
  181.7 49.5 %collective-permute-start.33 = (bf16[2,320,896]{2,1,0:T(8,128)(2,1)}, bf16[2,320,896]{2,1,0:T(8,128)(2,1)}, u32[]{:S(2)}, u32[]{:S(2)}) collective-permute-start(bf16[2,320,896]{2,1,0:T(8,128)(2,1)} %collective-permute-done.25.refs_3_.refs_5_), channel_id=1, source_target_pairs={{0,4},{1,5},{2,6},{3,7},{4,0},{5,1},{6,2},{7,3},{8,12},{9,13},{10,... | collective-permute-start | bytes 3440648 | tf_op jit(solution)/shard_map/ppermute | solution.py:48
  240.5 50.8 %collective-permute-start.37 = (bf16[2,320,896]{2,1,0:T(8,128)(2,1)}, bf16[2,320,896]{2,1,0:T(8,128)(2,1)}, u32[]{:S(2)}, u32[]{:S(2)}) collective-permute-start(bf16[2,320,896]{2,1,0:T(8,128)(2,1)} %maximum_select_fusion.5.refs_1_.refs_2_), channel_id=1, source_target_pairs={{0,16},{1,17},{2,18},{3,19},{4,20},{5,21},{6,22},{7,23},{8,24},{9,... | collective-permute-start | bytes 3440648 | tf_op jit(solution)/shard_map/ppermute | solution.py:48
  251.7 39.5 %collective-permute-start.38 = (bf16[2,320,896]{2,1,0:T(8,128)(2,1)}, bf16[2,320,896]{2,1,0:T(8,128)(2,1)}, u32[]{:S(2)}, u32[]{:S(2)}) collective-permute-start(bf16[2,320,896]{2,1,0:T(8,128)(2,1)} %maximum_select_fusion.5.refs_1_.refs_2_), channel_id=1, source_target_pairs={{0,4},{1,5},{2,6},{3,7},{4,0},{5,1},{6,2},{7,3},{8,12},{9,13},{10,... | collective-permute-start | bytes 3440648 | tf_op jit(solution)/shard_map/ppermute | solution.py:48
  255.6 35.6 %collective-permute-start.39 = (bf16[128,2560]{1,0:T(8,128)(2,1)}, bf16[128,2560]{1,0:T(8,128)(2,1)}, u32[]{:S(2)}, u32[]{:S(2)}) collective-permute-start(bf16[128,2560]{1,0:T(8,128)(2,1)} %collective-permute-done.26.refs_2_), channel_id=1, source_target_pairs={{0,2},{1,3},{2,0},{3,1},{4,6},{5,7},{6,4},{7,5},{8,10},{9,11},{10,... | collective-permute-start | bytes 1966088 | tf_op jit(solution)/shard_map/ppermute | solution.py:48
  349.6 52.6 %collective-permute-start.46 = (bf16[4,320,896]{2,1,0:T(8,128)(2,1)}, bf16[4,320,896]{2,1,0:T(8,128)(2,1)}, u32[]{:S(2)}, u32[]{:S(2)}) collective-permute-start(bf16[4,320,896]{2,1,0:T(8,128)(2,1)} %shard_map.437), channel_id=1, source_target_pairs={{0,4},{1,5},{2,6},{3,7},{4,0},{5,1},{6,2},{7,3},{8,12},{9,13},{10,... | collective-permute-start | bytes 6881288 | tf_op jit(solution)/shard_map/ppermute | solution.py:48
  417.6 60.2 %collective-permute-start.51 = (bf16[4,320,896]{2,1,0:T(8,128)(2,1)}, bf16[4,320,896]{2,1,0:T(8,128)(2,1)}, u32[]{:S(2)}, u32[]{:S(2)}) collective-permute-start(bf16[4,320,896]{2,1,0:T(8,128)(2,1)} %shard_map.441), channel_id=1, source_target_pairs={{0,4},{1,5},{2,6},{3,7},{4,0},{5,1},{6,2},{7,3},{8,12},{9,13},{10,... | collective-permute-start | bytes 6881288 | tf_op jit(solution)/shard_map/ppermute | solution.py:48
  424.4 53.3 %collective-permute-start.52 = (bf16[2,320,896]{2,1,0:T(8,128)(2,1)}, bf16[2,320,896]{2,1,0:T(8,128)(2,1)}, u32[]{:S(2)}, u32[]{:S(2)}) collective-permute-start(bf16[2,320,896]{2,1,0:T(8,128)(2,1)} %shard_map.452), channel_id=1, source_target_pairs={{0,16},{1,17},{2,18},{3,19},{4,20},{5,21},{6,22},{7,23},{8,24},{9,... | collective-permute-start | bytes 3440648 | tf_op jit(solution)/shard_map/ppermute | solution.py:48
  499.4 55.9 %collective-permute-start.59 = (bf16[4,320,896]{2,1,0:T(8,128)(2,1)}, bf16[4,320,896]{2,1,0:T(8,128)(2,1)}, u32[]{:S(2)}, u32[]{:S(2)}) collective-permute-start(bf16[4,320,896]{2,1,0:T(8,128)(2,1)} %shard_map.445), channel_id=1, source_target_pairs={{0,4},{1,5},{2,6},{3,7},{4,0},{5,1},{6,2},{7,3},{8,12},{9,13},{10,... | collective-permute-start | bytes 6881288 | tf_op jit(solution)/shard_map/ppermute | solution.py:48
  504.3 72.6 %collective-permute-start.63 = (bf16[2,320,896]{2,1,0:T(8,128)(2,1)}, bf16[2,320,896]{2,1,0:T(8,128)(2,1)}, u32[]{:S(2)}, u32[]{:S(2)}) collective-permute-start(bf16[2,320,896]{2,1,0:T(8,128)(2,1)} %shard_map.454), channel_id=1, source_target_pairs={{0,16},{1,17},{2,18},{3,19},{4,20},{5,21},{6,22},{7,23},{8,24},{9,... | collective-permute-start | bytes 3440648 | tf_op jit(solution)/shard_map/ppermute | solution.py:48
  536.8 40.1 %collective-permute-start.64 = (bf16[4,320,320]{2,1,0:T(8,128)(2,1)}, bf16[4,320,320]{2,1,0:T(8,128)(2,1)}, u32[]{:S(2)}, u32[]{:S(2)}) collective-permute-start(bf16[4,320,320]{2,1,0:T(8,128)(2,1)} %shard_map.460), channel_id=1, source_target_pairs={{0,4},{1,5},{2,6},{3,7},{4,0},{5,1},{6,2},{7,3},{8,12},{9,13},{10,... | collective-permute-start | bytes 2457608 | tf_op jit(solution)/shard_map/ppermute | solution.py:48
  564.4 65.1 %collective-permute-start.60 = (bf16[2,320,896]{2,1,0:T(8,128)(2,1)}, bf16[2,320,896]{2,1,0:T(8,128)(2,1)}, u32[]{:S(2)}, u32[]{:S(2)}) collective-permute-start(bf16[2,320,896]{2,1,0:T(8,128)(2,1)} %shard_map.465), channel_id=1, source_target_pairs={{0,16},{1,17},{2,18},{3,19},{4,20},{5,21},{6,22},{7,23},{8,24},{9,... | collective-permute-start | bytes 3440648 | tf_op jit(solution)/shard_map/ppermute | solution.py:48
  583.2 35.8 %collective-permute-start.69 = (bf16[4,320,482]{2,1,0:T(8,128)(2,1)}, bf16[4,320,482]{2,1,0:T(8,128)(2,1)}, u32[]{:S(2)}, u32[]{:S(2)}) collective-permute-start(bf16[4,320,482]{2,1,0:T(8,128)(2,1)} %shard_map.463), channel_id=1, source_target_pairs={{0,4},{1,5},{2,6},{3,7},{4,0},{5,1},{6,2},{7,3},{8,12},{9,13},{10,... | collective-permute-start | bytes 3701768 | tf_op jit(solution)/shard_map/ppermute | solution.py:48
  583.5 35.6 %collective-permute-start.70 = (bf16[320,896]{1,0:T(8,128)(2,1)}, bf16[320,896]{1,0:T(8,128)(2,1)}, u32[]{:S(2)}, u32[]{:S(2)}) collective-permute-start(bf16[320,896]{1,0:T(8,128)(2,1)} %fusion.16), channel_id=1, source_target_pairs={{0,8},{1,9},{2,10},{3,11},{4,12},{5,13},{6,14},{7,15},{8,0},{9,1},... | collective-permute-start | bytes 1720328 | tf_op jit(solution)/shard_map/ppermute | solution.py:48
  624.4 65.9 %collective-permute-start.73 = (bf16[2,320,482]{2,1,0:T(8,128)(2,1)}, bf16[2,320,482]{2,1,0:T(8,128)(2,1)}, u32[]{:S(2)}, u32[]{:S(2)}) collective-permute-start(bf16[2,320,482]{2,1,0:T(8,128)(2,1)} %shard_map.479), channel_id=1, source_target_pairs={{0,16},{1,17},{2,18},{3,19},{4,20},{5,21},{6,22},{7,23},{8,24},{9,... | collective-permute-start | bytes 1850888 | tf_op jit(solution)/shard_map/ppermute | solution.py:48
  625.6 54.5 %collective-permute-start.75 = (bf16[2,320,320]{2,1,0:T(8,128)(2,1)}, bf16[2,320,320]{2,1,0:T(8,128)(2,1)}, u32[]{:S(2)}, u32[]{:S(2)}) collective-permute-start(bf16[2,320,320]{2,1,0:T(8,128)(2,1)} %shard_map.472), channel_id=1, source_target_pairs={{0,16},{1,17},{2,18},{3,19},{4,20},{5,21},{6,22},{7,23},{8,24},{9,... | collective-permute-start | bytes 1228808 | tf_op jit(solution)/shard_map/ppermute | solution.py:48
  647.1 43.3 %collective-permute-start.77 = (bf16[320,896]{1,0:T(8,128)(2,1)}, bf16[320,896]{1,0:T(8,128)(2,1)}, u32[]{:S(2)}, u32[]{:S(2)}) collective-permute-start(bf16[320,896]{1,0:T(8,128)(2,1)} %fusion.18), channel_id=1, source_target_pairs={{0,8},{1,9},{2,10},{3,11},{4,12},{5,13},{6,14},{7,15},{8,0},{9,1},... | collective-permute-start | bytes 1720328 | tf_op jit(solution)/shard_map/ppermute | solution.py:48
  676.5 46.7 %collective-permute-start.84 = (bf16[128,2560]{1,0:T(8,128)(2,1)}, bf16[128,2560]{1,0:T(8,128)(2,1)}, u32[]{:S(2)}, u32[]{:S(2)}) collective-permute-start(bf16[128,2560]{1,0:T(8,128)(2,1)} %get-tuple-element.448), channel_id=1, source_target_pairs={{0,2},{1,3},{2,0},{3,1},{4,6},{5,7},{6,4},{7,5},{8,10},{9,11},{10,... | collective-permute-start | bytes 1966088 | tf_op jit(solution)/shard_map/ppermute | solution.py:48
  680.2 43.1 %collective-permute-start.85 = (bf16[128,2560]{1,0:T(8,128)(2,1)}, bf16[128,2560]{1,0:T(8,128)(2,1)}, u32[]{:S(2)}, u32[]{:S(2)}) collective-permute-start(bf16[128,2560]{1,0:T(8,128)(2,1)} %add_convert_fusion.1), channel_id=1, source_target_pairs={{0,8},{1,9},{2,10},{3,11},{4,12},{5,13},{6,14},{7,15},{8,0},{9,1},... | collective-permute-start | bytes 1966088 | tf_op jit(solution)/shard_map/ppermute | solution.py:48
  (144 other events, 1462.9 us)

commit v6 on v5

--- a/solution.py
+++ b/solution.py
@@ -750,7 +750,7 @@
 
 
 def branch(pairs, core, got=None):
-    step = 512
+    step = 640
     specs, lefts, weight_specs, weights, scratch = [], [], [], [], []
     for left, weight in pairs:
         tiles, wide, inner = left.shape

time: 780 us -> 781 us (level)
  transfers between devices with their start and end apart: 87 -> 87, of which waited for: 36 -> 35; matrix products, arithmetic and copies ran while one was open for 11% -> 11% of each run, Pallas kernels for 37% -> 37%
where the time goes in v6:
time: 781 us; the launch traced here: 771 us
  Pallas kernels  315 us (40%)
  waiting for transfers between devices  218 us (28%)
  starting transfers between devices  97.4 us (12%)
  other arithmetic  97 us (12%)
  local copies, waits for them, and re-layouts  35.3 us (5%)
    ppermute x87, waiting for transfers between devices, hop(): return lax.ppermute(block, AXES, route)  218 us
    ppermute x87, starting transfers between devices, hop(): return lax.ppermute(block, AXES, route)  97.4 us
    pallas_call x15, Pallas kernels, weight_rows(): pl.pallas_call(functools.partial(weight_body, len(addends)), grid_spec=pl...  81.4 us
    pallas_call x6, Pallas kernels, branch(): call(functools.partial(branch_body, len(pairs), weight.count(), got is no...  60.3 us
    pallas_call x38, Pallas kernels, __call__(): pl.pallas_call(keep_body, out_shape=jax.ShapeDtypeStruct(held.shape, held...  48.6 us
    mul x5, other arithmetic, adamw(): -learn_rate  25 us
    pallas_call x1, Pallas kernels, ffn(): call(functools.partial(ffn_body, gate_weight.count()), (tiles,), [tile_of...  19.8 us
    pallas_call x1, Pallas kernels, attend_back(): call(functools.partial(attend_back_body, weight.count()), (tiles,), [smem...  19.6 us
  transfers between devices with their start and end apart: 87, of which 35 were waited for; matrix products, arithmetic and copies ran while one was open for 11% of the time, Pallas kernels for 37%

profile of v6, /device:TPU:0, one launch (start us, length us, event | category | flops | bytes accessed | tf_op | source)
XLA Modules:
  0.0 771.0 jit_solution(6683782713134970468)
XLA Ops:
  40.3 10.3 %collective-permute-done.4.refs_2_ = bf16[128,2560]{1,0:T(8,128)(2,1)} collective-permute-done((bf16[128,2560]{1,0:T(8,128)(2,1)}, bf16[128,2560]{1,0:T(8,128)(2,1)}, u32[]{:S(2)}, u32[]{:S(2)}) %collective-permute-start.4) | collective-permute-done | bytes 655392 | tf_op jit(solution)/shard_map/ppermute | solution.py:48
  82.2 10.5 %shard_map.420 = (bf16[2560,1024]{1,0:T(8,128)(2,1)}, bf16[4,80,1024]{2,1,0:T(8,128)(2,1)}, bf16[4,160,256]{2,1,0:T(8,128)(2,1)}, f32[2,2560]{1,0:T(2,128)}) custom-call(bf16[4,128,2560]{2,1,0:T(8,128)(2,1)} %shard_map.416.x_ref, bf16[4,128,2560]{2,1,0:T(8,128)(2,1)} %collective-permute-done.9.xc_ref, f32[4,40,256]{2,1,0:T(8,128)} %get-tuple-element.577.cos_ref, ...), custom_call_target="tpu_custom_call" | custom-call | flops 10000000000 | tf_op jit(solution)/shard_map/pallas_call | solution.py:337
  128.2 18.7 %shard_map.424 = (bf16[4,256,320]{2,1,0:T(8,128)(2,1)}, f32[4,80,1024]{2,1,0:T(8,128)}, f32[4,1,1024]{2,1,0:T(1,128)}, bf16[4,128,2560]{2,1,0:T(8,128)(2,1)}, bf16[4,128,2560]{2,1,0:T(8,128)(2,1)}) custom-call(s32[48]{0:T(128)} %reshape.599.seen_ref, s32[12]{0:T(128)} %copy-done.64, bf16[4,80,1024]{2,1,0:T(8,128)(2,1)} %get-tuple-element.281.q_ref, ...), custom_call_target="tpu_custom_call" | custom-call | flops 10000000000 | tf_op jit(solution)/shard_map/pallas_call | solution.py:440
  161.9 8.1 %collective-permute-done.25.refs_3_.refs_5_ = bf16[2,320,896]{2,1,0:T(8,128)(2,1)} collective-permute-done((bf16[2,320,896]{2,1,0:T(8,128)(2,1)}, bf16[2,320,896]{2,1,0:T(8,128)(2,1)}, u32[]{:S(2)}, u32[]{:S(2)}) %collective-permute-start.25) | collective-permute-done | bytes 1146912 | tf_op jit(solution)/shard_map/ppermute | solution.py:48
  189.6 17.0 %collective-permute-done.28 = bf16[128,2560]{1,0:T(8,128)(2,1)} collective-permute-done((bf16[128,2560]{1,0:T(8,128)(2,1)}, bf16[128,2560]{1,0:T(8,128)(2,1)}, u32[]{:S(2)}, u32[]{:S(2)}) %collective-permute-start.28) | collective-permute-done | bytes 655392 | tf_op jit(solution)/shard_map/ppermute | solution.py:48
  213.0 17.9 %collective-permute-done.32.refs_8_.refs_10_ = bf16[2,320,896]{2,1,0:T(8,128)(2,1)} collective-permute-done((bf16[2,320,896]{2,1,0:T(8,128)(2,1)}, bf16[2,320,896]{2,1,0:T(8,128)(2,1)}, u32[]{:S(2)}, u32[]{:S(2)}) %collective-permute-start.32) | collective-permute-done | bytes 1146912 | tf_op jit(solution)/shard_map/ppermute | solution.py:48
  243.3 8.1 %collective-permute-done.34.refs_3_ = bf16[128,2560]{1,0:T(8,128)(2,1)} collective-permute-done((bf16[128,2560]{1,0:T(8,128)(2,1)}, bf16[128,2560]{1,0:T(8,128)(2,1)}, u32[]{:S(2)}, u32[]{:S(2)}) %collective-permute-start.34) | collective-permute-done | bytes 655392 | tf_op jit(solution)/shard_map/ppermute | solution.py:48
  260.9 8.9 %collective-permute-done.36.refs_9_.refs_11_ = bf16[2,320,896]{2,1,0:T(8,128)(2,1)} collective-permute-done((bf16[2,320,896]{2,1,0:T(8,128)(2,1)}, bf16[2,320,896]{2,1,0:T(8,128)(2,1)}, u32[]{:S(2)}, u32[]{:S(2)}) %collective-permute-start.36) | collective-permute-done | bytes 1146912 | tf_op jit(solution)/shard_map/ppermute | solution.py:48
  271.1 19.8 %shard_map.433 = (bf16[2560,1024]{1,0:T(8,128)(2,1)}, bf16[4,256,896]{2,1,0:T(8,128)(2,1)}, f32[4,256,896]{2,1,0:T(8,128)}, f32[4,256,896]{2,1,0:T(8,128)}) custom-call(bf16[4,128,2560]{2,1,0:T(8,128)(2,1)} %shard_map.431.near_ref, bf16[4,128,2560]{2,1,0:T(8,128)(2,1)} %collective-permute-done.35.far_ref, ...), custom_call_target="tpu_custom_call" | custom-call | flops 10000000000 | tf_op jit(solution)/shard_map/pallas_call | solution.py:650
  311.6 10.4 %collective-permute-done.41.refs_4_.refs_5_ = bf16[2,320,896]{2,1,0:T(8,128)(2,1)} collective-permute-done((bf16[2,320,896]{2,1,0:T(8,128)(2,1)}, bf16[2,320,896]{2,1,0:T(8,128)(2,1)}, u32[]{:S(2)}, u32[]{:S(2)}) %collective-permute-start.41) | collective-permute-done | bytes 1146912 | tf_op jit(solution)/shard_map/ppermute | solution.py:48
  322.0 12.4 %shard_map.439 = (bf16[4,256,896]{2,1,0:T(8,128)(2,1)}, bf16[4,256,896]{2,1,0:T(8,128)(2,1)}) custom-call(bf16[4,128,2560]{2,1,0:T(8,128)(2,1)} %shard_map.435.near_ref, bf16[4,128,2560]{2,1,0:T(8,128)(2,1)} %collective-permute-done.40.far_ref, f32[4,256,896]{2,1,0:T(8,128)} %get-tuple-element.334.one_ref, f32[4,256,896]{2,1,0:T(8,128)} %get-tuple-element.335.two_ref, ...), custom_call_target="tpu_custom_call" | custom-call | flops 10000000000 | tf_op jit(solution)/shard_map/pallas_call | solution.py:692
  334.4 14.2 %shard_map.440 = bf16[4,128,2560]{2,1,0:T(8,128)(2,1)} custom-call(bf16[4,2,128,896]{3,2,1,0:T(8,128)(2,1)} %bitcast.186, bf16[4,2,128,896]{3,2,1,0:T(8,128)(2,1)} %bitcast.181, s32[8]{0:T(128)} %stack.64.refs_0_.refs_4_.refs_5_.refs_2_.refs_7_.refs_1_, bf16[2,320,896]{2,1,0:T(8,128)(2,1)} %maximum_select_fusion.3.refs_1_.refs_3_, ...), custom_call_target="tpu_custom_call" | custom-call | flops 10000000000 | tf_op jit(solution)/shard_map/pallas_call | solution.py:769
  358.7 14.5 %shard_map.443 = (f32[128,2560]{1,0:T(8,128)}, bf16[128,2560]{1,0:T(8,128)(2,1)}, bf16[128,2560]{1,0:T(8,128)(2,1)}, bf16[128,2560]{1,0:T(8,128)(2,1)}) custom-call(bf16[4,2,128,896]{3,2,1,0:T(8,128)(2,1)} %bitcast.188, bf16[4,2,128,896]{3,2,1,0:T(8,128)(2,1)} %bitcast.182, s32[8]{0:T(128)} %stack.64.refs_0_.refs_4_.refs_5_.refs_2_.refs_7_.refs_1_, ...), custom_call_target="tpu_custom_call" | custom-call | flops 10000000000 | tf_op jit(solution)/shard_map/pallas_call | solution.py:769
  375.1 15.3 %collective-permute-done.43 = bf16[128,2560]{1,0:T(8,128)(2,1)} collective-permute-done((bf16[128,2560]{1,0:T(8,128)(2,1)}, bf16[128,2560]{1,0:T(8,128)(2,1)}, u32[]{:S(2)}, u32[]{:S(2)}) %collective-permute-start.43) | collective-permute-done | bytes 655392 | tf_op jit(solution)/shard_map/ppermute | solution.py:48
  430.9 7.8 %collective-permute-done.48.refs_2_ = bf16[128,2560]{1,0:T(8,128)(2,1)} collective-permute-done((bf16[128,2560]{1,0:T(8,128)(2,1)}, bf16[128,2560]{1,0:T(8,128)(2,1)}, u32[]{:S(2)}, u32[]{:S(2)}) %collective-permute-start.48) | collective-permute-done | bytes 655392 | tf_op jit(solution)/shard_map/ppermute | solution.py:48
  440.6 11.5 %collective-permute-done.49.refs_3_ = bf16[128,2560]{1,0:T(8,128)(2,1)} collective-permute-done((bf16[128,2560]{1,0:T(8,128)(2,1)}, bf16[128,2560]{1,0:T(8,128)(2,1)}, u32[]{:S(2)}, u32[]{:S(2)}) %collective-permute-start.49) | collective-permute-done | bytes 655392 | tf_op jit(solution)/shard_map/ppermute | solution.py:48
  461.5 19.6 %shard_map.451 = (bf16[4,320,256]{2,1,0:T(8,128)(2,1)}, f32[4,160,256]{2,1,0:T(8,128)}, bf16[4,160,256]{2,1,0:T(8,128)(2,1)}, bf16[2,160,256]{2,1,0:T(8,128)(2,1)}, bf16[2,160,256]{2,1,0:T(8,128)(2,1)}) custom-call(s32[48]{0:T(128)} %reshape.599.seen_ref, s32[12]{0:T(128)} %copy-done.64, bf16[4,80,1024]{2,1,0:T(8,128)(2,1)} %get-tuple-element.281.q_ref, ...), custom_call_target="tpu_custom_call" | custom-call | flops 10000000000 | tf_op jit(solution)/shard_map/pallas_call | solution.py:541
  490.5 7.9 %collective-permute-done.54.a_ref = bf16[2,160,256]{2,1,0:T(8,128)(2,1)} collective-permute-done((bf16[2,160,256]{2,1,0:T(8,128)(2,1)}, bf16[2,160,256]{2,1,0:T(8,128)(2,1)}, u32[]{:S(2)}, u32[]{:S(2)}) %collective-permute-start.54) | collective-permute-done | bytes 163872 | tf_op jit(solution)/shard_map/ppermute | solution.py:48
  528.0 7.2 shard_map.462
  542.3 13.7 %collective-permute-done.59.refs_0_.refs_1_ = bf16[4,320,896]{2,1,0:T(8,128)(2,1)} collective-permute-done((bf16[4,320,896]{2,1,0:T(8,128)(2,1)}, bf16[4,320,896]{2,1,0:T(8,128)(2,1)}, u32[]{:S(2)}, u32[]{:S(2)}) %collective-permute-start.59) | collective-permute-done | bytes 2293792 | tf_op jit(solution)/shard_map/ppermute | solution.py:48
  586.4 8.7 %shard_map.471 = bf16[4,128,2560]{2,1,0:T(8,128)(2,1)} custom-call(bf16[4,2,128,896]{3,2,1,0:T(8,128)(2,1)} %bitcast.179, s32[8]{0:T(128)} %stack.64.refs_0_.refs_4_.refs_5_.refs_2_.refs_7_.refs_1_, bf16[2,320,896]{2,1,0:T(8,128)(2,1)} %maximum_select_fusion.5.refs_1_.refs_2_, bf16[2,320,896]{2,1,0:T(8,128)(2,1)} %collective-permute-done.38.refs_2_.refs_3_, ...), custom_call_target="tpu_custom_call" | custom-call | flops 10000000000 | tf_op jit(solution)/shard_map/pallas_call | solution.py:769
  648.6 9.3 %shard_map.478 = (f32[128,2560]{1,0:T(8,128)}, bf16[128,2560]{1,0:T(8,128)(2,1)}, bf16[128,2560]{1,0:T(8,128)(2,1)}, bf16[128,2560]{1,0:T(8,128)(2,1)}) custom-call(bf16[4,2,128,896]{3,2,1,0:T(8,128)(2,1)} %bitcast.180, s32[8]{0:T(128)} %stack.64.refs_0_.refs_4_.refs_5_.refs_2_.refs_7_.refs_1_, bf16[2,320,896]{2,1,0:T(8,128)(2,1)} %maximum_select_fusion.5.refs_1_.refs_2_, ...), custom_call_target="tpu_custom_call" | custom-call | flops 10000000000 | tf_op jit(solution)/shard_map/pallas_call | solution.py:769
  660.6 14.5 %collective-permute-done.74 = bf16[128,2560]{1,0:T(8,128)(2,1)} collective-permute-done((bf16[128,2560]{1,0:T(8,128)(2,1)}, bf16[128,2560]{1,0:T(8,128)(2,1)}, u32[]{:S(2)}, u32[]{:S(2)}) %collective-permute-start.74) | collective-permute-done | bytes 655392 | tf_op jit(solution)/shard_map/ppermute | solution.py:48
  753.3 10.0 %add_multiply_fusion = (f32[2,320,1792]{2,1,0:T(8,128)}, f32[2,320,1792]{2,1,0:T(8,128)}, f32[2,320,1792]{2,1,0:T(8,128)}, f32[2,320,1792]{2,1,0:T(8,128)}) fusion(f32[2,320,1792]{2,1,0:T(8,128)S(1)} %bitcast.134, f32[]{:T(128)S(6)} %min_shard_map.3, f32[2,320,1792]{2,1,0:T(8,128)S(1)} %copy-done.9, f32[2,320,1792]{2,1,0:T(8,128)} %param.33, ...), kind=kLoop, calls=%fused_computation.3 | loop fusion | flops 18350080 | bytes 36700164 | tf_op jit(solution)/shard_map/mul | solution.py:869
  (498 shorter events, 466.9 us)
Async XLA Ops:
  24.6 32.1 %collective-permute-start.6 = (bf16[2,320,482]{2,1,0:T(8,128)(2,1)}, bf16[2,320,482]{2,1,0:T(8,128)(2,1)}, u32[]{:S(2)}, u32[]{:S(2)}) collective-permute-start(bf16[2,320,482]{2,1,0:T(8,128)(2,1)} %maximum_select_fusion.8.refs_1_.refs_2_), channel_id=1, source_target_pairs={{0,16},{1,17},{2,18},{3,19},{4,20},{5,21},{6,22},{7,23},{8,24},{9,... | collective-permute-start | bytes 1850888 | tf_op jit(solution)/shard_map/ppermute | solution.py:48
  59.9 36.7 %collective-permute-start.13 = (bf16[2,320,320]{2,1,0:T(8,128)(2,1)}, bf16[2,320,320]{2,1,0:T(8,128)(2,1)}, u32[]{:S(2)}, u32[]{:S(2)}) collective-permute-start(bf16[2,320,320]{2,1,0:T(8,128)(2,1)} %maximum_select_fusion.9.refs_5_), channel_id=1, source_target_pairs={{0,16},{1,17},{2,18},{3,19},{4,20},{5,21},{6,22},{7,23},{8,24},{9,... | collective-permute-start | bytes 1228808 | tf_op jit(solution)/shard_map/ppermute | solution.py:48
  118.0 30.4 %collective-permute-start.23 = (bf16[2,320,896]{2,1,0:T(8,128)(2,1)}, bf16[2,320,896]{2,1,0:T(8,128)(2,1)}, u32[]{:S(2)}, u32[]{:S(2)}) collective-permute-start(bf16[2,320,896]{2,1,0:T(8,128)(2,1)} %maximum_select_fusion.3.refs_1_.refs_3_), channel_id=1, source_target_pairs={{0,4},{1,5},{2,6},{3,7},{4,0},{5,1},{6,2},{7,3},{8,12},{9,13},{10,... | collective-permute-start | bytes 3440648 | tf_op jit(solution)/shard_map/ppermute | solution.py:48
  119.0 50.9 %collective-permute-start.25 = (bf16[2,320,896]{2,1,0:T(8,128)(2,1)}, bf16[2,320,896]{2,1,0:T(8,128)(2,1)}, u32[]{:S(2)}, u32[]{:S(2)}) collective-permute-start(bf16[2,320,896]{2,1,0:T(8,128)(2,1)} %maximum_select_fusion.3.refs_1_.refs_3_), channel_id=1, source_target_pairs={{0,16},{1,17},{2,18},{3,19},{4,20},{5,21},{6,22},{7,23},{8,24},{9,... | collective-permute-start | bytes 3440648 | tf_op jit(solution)/shard_map/ppermute | solution.py:48
  123.3 38.6 %collective-permute-start.26 = (bf16[128,2560]{1,0:T(8,128)(2,1)}, bf16[128,2560]{1,0:T(8,128)(2,1)}, u32[]{:S(2)}, u32[]{:S(2)}) collective-permute-start(bf16[128,2560]{1,0:T(8,128)(2,1)} %refs_0_.1), channel_id=1, source_target_pairs={{0,8},{1,9},{2,10},{3,11},{4,12},{5,13},{6,14},{7,15},{8,0},{9,1},... | collective-permute-start | bytes 1966088 | tf_op jit(solution)/shard_map/ppermute | solution.py:48
  178.4 52.5 %collective-permute-start.32 = (bf16[2,320,896]{2,1,0:T(8,128)(2,1)}, bf16[2,320,896]{2,1,0:T(8,128)(2,1)}, u32[]{:S(2)}, u32[]{:S(2)}) collective-permute-start(bf16[2,320,896]{2,1,0:T(8,128)(2,1)} %maximum_select_fusion.4.refs_6_.refs_8_), channel_id=1, source_target_pairs={{0,16},{1,17},{2,18},{3,19},{4,20},{5,21},{6,22},{7,23},{8,24},{9,... | collective-permute-start | bytes 3440648 | tf_op jit(solution)/shard_map/ppermute | solution.py:48
  181.4 49.5 %collective-permute-start.33 = (bf16[2,320,896]{2,1,0:T(8,128)(2,1)}, bf16[2,320,896]{2,1,0:T(8,128)(2,1)}, u32[]{:S(2)}, u32[]{:S(2)}) collective-permute-start(bf16[2,320,896]{2,1,0:T(8,128)(2,1)} %collective-permute-done.25.refs_3_.refs_5_), channel_id=1, source_target_pairs={{0,4},{1,5},{2,6},{3,7},{4,0},{5,1},{6,2},{7,3},{8,12},{9,13},{10,... | collective-permute-start | bytes 3440648 | tf_op jit(solution)/shard_map/ppermute | solution.py:48
  240.2 50.7 %collective-permute-start.37 = (bf16[2,320,896]{2,1,0:T(8,128)(2,1)}, bf16[2,320,896]{2,1,0:T(8,128)(2,1)}, u32[]{:S(2)}, u32[]{:S(2)}) collective-permute-start(bf16[2,320,896]{2,1,0:T(8,128)(2,1)} %maximum_select_fusion.5.refs_1_.refs_2_), channel_id=1, source_target_pairs={{0,16},{1,17},{2,18},{3,19},{4,20},{5,21},{6,22},{7,23},{8,24},{9,... | collective-permute-start | bytes 3440648 | tf_op jit(solution)/shard_map/ppermute | solution.py:48
  251.4 39.6 %collective-permute-start.38 = (bf16[2,320,896]{2,1,0:T(8,128)(2,1)}, bf16[2,320,896]{2,1,0:T(8,128)(2,1)}, u32[]{:S(2)}, u32[]{:S(2)}) collective-permute-start(bf16[2,320,896]{2,1,0:T(8,128)(2,1)} %maximum_select_fusion.5.refs_1_.refs_2_), channel_id=1, source_target_pairs={{0,4},{1,5},{2,6},{3,7},{4,0},{5,1},{6,2},{7,3},{8,12},{9,13},{10,... | collective-permute-start | bytes 3440648 | tf_op jit(solution)/shard_map/ppermute | solution.py:48
  255.4 35.6 %collective-permute-start.39 = (bf16[128,2560]{1,0:T(8,128)(2,1)}, bf16[128,2560]{1,0:T(8,128)(2,1)}, u32[]{:S(2)}, u32[]{:S(2)}) collective-permute-start(bf16[128,2560]{1,0:T(8,128)(2,1)} %collective-permute-done.26.refs_2_), channel_id=1, source_target_pairs={{0,2},{1,3},{2,0},{3,1},{4,6},{5,7},{6,4},{7,5},{8,10},{9,11},{10,... | collective-permute-start | bytes 1966088 | tf_op jit(solution)/shard_map/ppermute | solution.py:48
  350.0 53.6 %collective-permute-start.46 = (bf16[4,320,896]{2,1,0:T(8,128)(2,1)}, bf16[4,320,896]{2,1,0:T(8,128)(2,1)}, u32[]{:S(2)}, u32[]{:S(2)}) collective-permute-start(bf16[4,320,896]{2,1,0:T(8,128)(2,1)} %shard_map.437), channel_id=1, source_target_pairs={{0,4},{1,5},{2,6},{3,7},{4,0},{5,1},{6,2},{7,3},{8,12},{9,13},{10,... | collective-permute-start | bytes 6881288 | tf_op jit(solution)/shard_map/ppermute | solution.py:48
  420.0 61.1 %collective-permute-start.51 = (bf16[4,320,896]{2,1,0:T(8,128)(2,1)}, bf16[4,320,896]{2,1,0:T(8,128)(2,1)}, u32[]{:S(2)}, u32[]{:S(2)}) collective-permute-start(bf16[4,320,896]{2,1,0:T(8,128)(2,1)} %shard_map.441), channel_id=1, source_target_pairs={{0,4},{1,5},{2,6},{3,7},{4,0},{5,1},{6,2},{7,3},{8,12},{9,13},{10,... | collective-permute-start | bytes 6881288 | tf_op jit(solution)/shard_map/ppermute | solution.py:48
  425.7 55.4 %collective-permute-start.52 = (bf16[2,320,896]{2,1,0:T(8,128)(2,1)}, bf16[2,320,896]{2,1,0:T(8,128)(2,1)}, u32[]{:S(2)}, u32[]{:S(2)}) collective-permute-start(bf16[2,320,896]{2,1,0:T(8,128)(2,1)} %shard_map.452), channel_id=1, source_target_pairs={{0,16},{1,17},{2,18},{3,19},{4,20},{5,21},{6,22},{7,23},{8,24},{9,... | collective-permute-start | bytes 3440648 | tf_op jit(solution)/shard_map/ppermute | solution.py:48
  500.8 55.2 %collective-permute-start.59 = (bf16[4,320,896]{2,1,0:T(8,128)(2,1)}, bf16[4,320,896]{2,1,0:T(8,128)(2,1)}, u32[]{:S(2)}, u32[]{:S(2)}) collective-permute-start(bf16[4,320,896]{2,1,0:T(8,128)(2,1)} %shard_map.445), channel_id=1, source_target_pairs={{0,4},{1,5},{2,6},{3,7},{4,0},{5,1},{6,2},{7,3},{8,12},{9,13},{10,... | collective-permute-start | bytes 6881288 | tf_op jit(solution)/shard_map/ppermute | solution.py:48
  505.0 72.8 %collective-permute-start.63 = (bf16[2,320,896]{2,1,0:T(8,128)(2,1)}, bf16[2,320,896]{2,1,0:T(8,128)(2,1)}, u32[]{:S(2)}, u32[]{:S(2)}) collective-permute-start(bf16[2,320,896]{2,1,0:T(8,128)(2,1)} %shard_map.454), channel_id=1, source_target_pairs={{0,16},{1,17},{2,18},{3,19},{4,20},{5,21},{6,22},{7,23},{8,24},{9,... | collective-permute-start | bytes 3440648 | tf_op jit(solution)/shard_map/ppermute | solution.py:48
  537.2 40.6 %collective-permute-start.64 = (bf16[4,320,320]{2,1,0:T(8,128)(2,1)}, bf16[4,320,320]{2,1,0:T(8,128)(2,1)}, u32[]{:S(2)}, u32[]{:S(2)}) collective-permute-start(bf16[4,320,320]{2,1,0:T(8,128)(2,1)} %shard_map.460), channel_id=1, source_target_pairs={{0,4},{1,5},{2,6},{3,7},{4,0},{5,1},{6,2},{7,3},{8,12},{9,13},{10,... | collective-permute-start | bytes 2457608 | tf_op jit(solution)/shard_map/ppermute | solution.py:48
  565.4 65.3 %collective-permute-start.60 = (bf16[2,320,896]{2,1,0:T(8,128)(2,1)}, bf16[2,320,896]{2,1,0:T(8,128)(2,1)}, u32[]{:S(2)}, u32[]{:S(2)}) collective-permute-start(bf16[2,320,896]{2,1,0:T(8,128)(2,1)} %shard_map.465), channel_id=1, source_target_pairs={{0,16},{1,17},{2,18},{3,19},{4,20},{5,21},{6,22},{7,23},{8,24},{9,... | collective-permute-start | bytes 3440648 | tf_op jit(solution)/shard_map/ppermute | solution.py:48
  583.8 36.3 %collective-permute-start.69 = (bf16[4,320,482]{2,1,0:T(8,128)(2,1)}, bf16[4,320,482]{2,1,0:T(8,128)(2,1)}, u32[]{:S(2)}, u32[]{:S(2)}) collective-permute-start(bf16[4,320,482]{2,1,0:T(8,128)(2,1)} %shard_map.463), channel_id=1, source_target_pairs={{0,4},{1,5},{2,6},{3,7},{4,0},{5,1},{6,2},{7,3},{8,12},{9,13},{10,... | collective-permute-start | bytes 3701768 | tf_op jit(solution)/shard_map/ppermute | solution.py:48
  584.4 35.8 %collective-permute-start.70 = (bf16[320,896]{1,0:T(8,128)(2,1)}, bf16[320,896]{1,0:T(8,128)(2,1)}, u32[]{:S(2)}, u32[]{:S(2)}) collective-permute-start(bf16[320,896]{1,0:T(8,128)(2,1)} %fusion.16), channel_id=1, source_target_pairs={{0,8},{1,9},{2,10},{3,11},{4,12},{5,13},{6,14},{7,15},{8,0},{9,1},... | collective-permute-start | bytes 1720328 | tf_op jit(solution)/shard_map/ppermute | solution.py:48
  625.6 65.1 %collective-permute-start.73 = (bf16[2,320,482]{2,1,0:T(8,128)(2,1)}, bf16[2,320,482]{2,1,0:T(8,128)(2,1)}, u32[]{:S(2)}, u32[]{:S(2)}) collective-permute-start(bf16[2,320,482]{2,1,0:T(8,128)(2,1)} %shard_map.479), channel_id=1, source_target_pairs={{0,16},{1,17},{2,18},{3,19},{4,20},{5,21},{6,22},{7,23},{8,24},{9,... | collective-permute-start | bytes 1850888 | tf_op jit(solution)/shard_map/ppermute | solution.py:48
  626.7 53.8 %collective-permute-start.75 = (bf16[2,320,320]{2,1,0:T(8,128)(2,1)}, bf16[2,320,320]{2,1,0:T(8,128)(2,1)}, u32[]{:S(2)}, u32[]{:S(2)}) collective-permute-start(bf16[2,320,320]{2,1,0:T(8,128)(2,1)} %shard_map.472), channel_id=1, source_target_pairs={{0,16},{1,17},{2,18},{3,19},{4,20},{5,21},{6,22},{7,23},{8,24},{9,... | collective-permute-start | bytes 1228808 | tf_op jit(solution)/shard_map/ppermute | solution.py:48
  647.9 42.8 %collective-permute-start.77 = (bf16[320,896]{1,0:T(8,128)(2,1)}, bf16[320,896]{1,0:T(8,128)(2,1)}, u32[]{:S(2)}, u32[]{:S(2)}) collective-permute-start(bf16[320,896]{1,0:T(8,128)(2,1)} %fusion.18), channel_id=1, source_target_pairs={{0,8},{1,9},{2,10},{3,11},{4,12},{5,13},{6,14},{7,15},{8,0},{9,1},... | collective-permute-start | bytes 1720328 | tf_op jit(solution)/shard_map/ppermute | solution.py:48
  677.1 46.7 %collective-permute-start.84 = (bf16[128,2560]{1,0:T(8,128)(2,1)}, bf16[128,2560]{1,0:T(8,128)(2,1)}, u32[]{:S(2)}, u32[]{:S(2)}) collective-permute-start(bf16[128,2560]{1,0:T(8,128)(2,1)} %get-tuple-element.448), channel_id=1, source_target_pairs={{0,2},{1,3},{2,0},{3,1},{4,6},{5,7},{6,4},{7,5},{8,10},{9,11},{10,... | collective-permute-start | bytes 1966088 | tf_op jit(solution)/shard_map/ppermute | solution.py:48
  680.5 43.3 %collective-permute-start.85 = (bf16[128,2560]{1,0:T(8,128)(2,1)}, bf16[128,2560]{1,0:T(8,128)(2,1)}, u32[]{:S(2)}, u32[]{:S(2)}) collective-permute-start(bf16[128,2560]{1,0:T(8,128)(2,1)} %add_convert_fusion.1), channel_id=1, source_target_pairs={{0,8},{1,9},{2,10},{3,11},{4,12},{5,13},{6,14},{7,15},{8,0},{9,1},... | collective-permute-start | bytes 1966088 | tf_op jit(solution)/shard_map/ppermute | solution.py:48
  (144 other events, 1463.9 us)
